TPU v7x, 512 devices: a whole 4x4x16 slice. The times are simulated.
512 devices in a mesh: group: 16 (over z), slab: 32 (over y, x, core).
Axes of the slice: x: 4, y: 4, z: 16, core: 2. Of those that a mesh axis runs over, the one named last changes fastest.
Arguments:
- operator: float32 [8192, 64, 448], P(('group', 'slab'))
- adjacency: int32 [8192, 6], P(('group', 'slab')), may hold values from -1 to 8191, as said below
- counts: int32 [8192], P(('group', 'slab')), may hold values from 1 to 6, as said below
- rhs: float32 [524288], P(('group', 'slab')), may hold values from -6 to 6
- start: float32 [524288], P(('group', 'slab')), may hold values from -6 to 6
- shifts: float32 [8], replicated, may hold values from 0.8 to 2.2
Outputs:
- solution: float32 [524288], P(('group', 'slab'))
- residual: float32 [524288], P(('group', 'slab'))
- upper: float32 [9, 9], replicated
Inputs may be any that keep to these rules, and one draw needn't show every extreme that they name: Each element has 1 to 6 face neighbours; counts reach both ends in every draw. `adjacency`: entries f < counts[e] name an element other than e whose global number differs from e's by at most 2, so it lies on the same device or on the device just before or after it in the order group then slab; some element reaches a difference of 2 in every draw; entries f >= counts[e] are -1.
All inputs are finite; a program needn't handle non-finite values.
Results may differ from a plain program's by a relative error of at most 0.0008.
Values sent between devices are 32-bit elements; how exact they have to be, the bound alone decides.
No kernel may reach another device: no remote copies, remote signals or barrier semaphores. Data moves between devices by JAX's collectives and lax.ppermute only.
A program may use at most 64 MiB of HBM per device.

v0:
```python
import jax
import jax.numpy as jnp
from jax import lax
from jax.sharding import PartitionSpec as P


def from_behind(array, axis, by):
    size = lax.axis_size(axis)
    pairs = [(i, i + by) for i in range(size) if 0 <= i + by < size]
    return lax.ppermute(array, axis, pairs)


def upper_factor(columns):
    size, length = columns.shape
    position = jnp.arange(length)
    work = columns
    for index in range(size):
        column = jnp.where(position >= index, work[index], 0.0)
        magnitude = jnp.sqrt(jnp.sum(column * column))
        alpha = jnp.where(column[index] >= 0, -magnitude, magnitude)
        mirror = column - alpha * jnp.where(position == index, 1.0, 0.0)
        denom = jnp.sum(mirror * mirror)
        inner = jnp.dot(work, mirror, precision=lax.Precision.HIGHEST)
        work = work - 2.0 / denom * inner[:, None] * mirror[None, :]
    factor = jnp.triu(work[:, :size].T)
    signs = jnp.where(jnp.diagonal(factor) >= 0, 1.0, -1.0)
    return factor * signs[:, None]


def back_solve(triangle, target):
    length = target.shape[0]
    result = jnp.zeros_like(target)
    for index in range(length - 1, -1, -1):
        partial_sum = jnp.sum(triangle[index] * result)
        result = result.at[index].set((target[index] - partial_sum) / triangle[index, index])
    return result


def body(operator, adjacency, counts, rhs, start, shifts):
    elems = operator.shape[0]
    width = operator.shape[1]
    faces = adjacency.shape[1]
    ghost = elems // 8
    steps = shifts.shape[0]
    devices = lax.axis_size(("group", "slab"))
    base = lax.axis_index(("group", "slab")) * elems
    valid = jnp.arange(faces)[None, :] < counts[:, None]
    offset = adjacency - base
    slot = jnp.where(valid, offset + ghost, 0)

    def apply_operator(vec):
        rim_low = vec[:ghost]
        rim_high = vec[elems - ghost :]
        below = from_behind(rim_high, ("group", "slab"), 1)
        above = from_behind(rim_low, ("group", "slab"), -1)
        extended = jnp.concatenate([below, vec, above], axis=0)
        near = jnp.where(valid[:, :, None], extended[slot], 0.0)
        stacked = jnp.concatenate([vec[:, None, :], near], axis=1).reshape(
            elems, (faces + 1) * width
        )
        return jnp.einsum("eij,ej->ei", operator, stacked, precision=lax.Precision.HIGHEST)

    x_start = start.reshape(elems, width)
    first = rhs.reshape(elems, width) - apply_operator(x_start)
    vectors = [first]
    for step in range(steps):
        vectors.append(apply_operator(vectors[-1]) - shifts[step] * vectors[-1])
    basis = jnp.stack(vectors).reshape(steps + 1, elems * width)
    local_factor = upper_factor(basis)
    stacked_slab = lax.all_gather(local_factor, "slab", axis=0, tiled=True)
    middle = upper_factor(stacked_slab.T)
    stacked_group = lax.all_gather(middle, "group", axis=0, tiled=True)
    factor = upper_factor(stacked_group.T)
    bidiag = jnp.eye(steps + 1, steps, dtype=jnp.float32) * shifts[None, :] + jnp.eye(
        steps + 1, steps, k=-1, dtype=jnp.float32
    )
    hess = jnp.dot(factor, bidiag, precision=lax.Precision.HIGHEST)
    augmented = jnp.concatenate([hess, factor[:, 0:1]], axis=1)
    second = upper_factor(augmented.T)
    coeffs = back_solve(second[:steps, :steps], second[:steps, steps])
    solution = start + jnp.dot(coeffs, basis[:steps], precision=lax.Precision.HIGHEST)
    moved = basis[1:] + shifts[:, None] * basis[:steps]
    residual = first.reshape(-1) - jnp.dot(coeffs, moved, precision=lax.Precision.HIGHEST)
    upper = factor / jnp.sqrt(jnp.float32(devices * elems * width))
    return (solution, residual, upper)


def solution(mesh):
    return jax.shard_map(
        body,
        mesh=mesh,
        in_specs=(
            P(("group", "slab"), None, None),
            P(("group", "slab"), None),
            P(("group", "slab")),
            P(("group", "slab")),
            P(("group", "slab")),
            P(),
        ),
        out_specs=(P(("group", "slab")), P(("group", "slab")), P()),
        check_vma=False,
    )
```

profile of v0, /device:TPU:1, one launch (start us, length us, event | category | flops | bytes accessed | tf_op | source)
XLA Modules:
  0.0 375.6 jit_solution(12887353253536105076)
XLA Ops:
  1.6 8.8 %collective-permute-start.1 = (f32[2,64]{1,0:T(2,128)S(1)}, f32[2,64]{1,0:T(2,128)S(1)}, u32[]{:S(2)}, u32[]{:S(2)}) collective-permute-start(f32[2,64]{1,0:T(2,128)S(1)} %slice.528), channel_id=1, source_target_pairs={{1,0},{2,1},{3,2},{4,3},{5,4},{6,5},{7,6},{8,7},{9,8},{10,9},{11,1... | collective-permute-start | bytes 1544 | tf_op jit(solution)/shard_map/ppermute | solution.py:10
  23.2 2.4 collective-permute-start.3
  31.9 2.6 collective-permute-start.4
  36.5 2.9 collective-permute-done.5
  42.8 2.0 collective-permute-start.6
  44.8 2.4 collective-permute-start.7
  47.1 2.5 collective-permute-done.7
  53.0 2.0 collective-permute-start.8
  54.9 2.4 collective-permute-start.9
  57.3 2.5 collective-permute-done.9
  63.2 2.0 collective-permute-start.10
  65.1 2.4 collective-permute-start.11
  67.5 3.7 collective-permute-done.11
  74.6 2.0 collective-permute-start.12
  76.6 2.5 collective-permute-start.13
  79.1 4.4 %collective-permute-done.13 = f32[2,64]{1,0:T(2,128)S(1)} collective-permute-done((f32[2,64]{1,0:T(2,128)S(1)}, f32[2,64]{1,0:T(2,128)S(1)}, u32[]{:S(2)}, u32[]{:S(2)}) %collective-permute-start.13) | collective-permute-done | bytes 544 | tf_op jit(solution)/shard_map/ppermute | solution.py:10
  86.8 2.0 collective-permute-start.14
  88.8 2.4 collective-permute-start.15
  91.3 4.5 %collective-permute-done.15 = f32[2,64]{1,0:T(2,128)S(1)} collective-permute-done((f32[2,64]{1,0:T(2,128)S(1)}, f32[2,64]{1,0:T(2,128)S(1)}, u32[]{:S(2)}, u32[]{:S(2)}) %collective-permute-start.15) | collective-permute-done | bytes 544 | tf_op jit(solution)/shard_map/ppermute | solution.py:10
  99.2 2.0 collective-permute-start.16
  101.2 2.4 collective-permute-start.17
  104.8 3.4 collective-permute-done.17
  146.1 52.3 %all-gather = f32[32,9,9]{2,1,0:T(8,128)S(1)} all-gather(f32[1,9,9]{2,1,0:T(8,128)S(1)} %bitcast.691), channel_id=1, replica_groups=mesh['group'=16,'slab'=32] {'slab'}, dimensions={0}, use_global_device_ids=true | all-gather | bytes 10692 | tf_op jit(solution)/shard_map/all_gather | solution.py:70
  236.6 40.5 %all-gather.1 = f32[16,9,9]{2,1,0:T(8,128)S(1)} all-gather(f32[1,9,9]{2,1,0:T(8,128)S(1)} %bitcast.692), channel_id=1, replica_groups=mesh['group'=16,'slab'=32] {'group'}, dimensions={0}, use_global_device_ids=true | all-gather | bytes 5508 | tf_op jit(solution)/shard_map/all_gather | solution.py:72
  (423 shorter events, 128.5 us)
Async XLA Ops:
  0.6 18.2 %copy-start = (f32[16,64,448]{2,1,0:T(8,128)S(1)}, f32[16,64,448]{2,1,0:T(8,128)}, u32[]{:S(2)}) copy-start(f32[16,64,448]{2,1,0:T(8,128)} %param.22) | copy-start | bytes 5505028
  1.6 16.3 %collective-permute-start.1 = (f32[2,64]{1,0:T(2,128)S(1)}, f32[2,64]{1,0:T(2,128)S(1)}, u32[]{:S(2)}, u32[]{:S(2)}) collective-permute-start(f32[2,64]{1,0:T(2,128)S(1)} %slice.528), channel_id=1, source_target_pairs={{1,0},{2,1},{3,2},{4,3},{5,4},{6,5},{7,6},{8,7},{9,8},{10,9},{11,1... | collective-permute-start | bytes 1544 | tf_op jit(solution)/shard_map/ppermute | solution.py:10
  10.4 7.5 %collective-permute-start = (f32[2,64]{1,0:T(2,128)S(1)}, f32[2,64]{1,0:T(2,128)S(1)}, u32[]{:S(2)}, u32[]{:S(2)}) collective-permute-start(f32[2,64]{1,0:T(2,128)S(1)} %slice.526), channel_id=1, source_target_pairs={{0,1},{1,2},{2,3},{3,4},{4,5},{5,6},{6,7},{7,8},{8,9},{9,10},{10,1... | collective-permute-start | bytes 1544 | tf_op jit(solution)/shard_map/ppermute | solution.py:10
  21.2 6.3 %collective-permute-start.2 = (f32[2,64]{1,0:T(2,128)S(1)}, f32[2,64]{1,0:T(2,128)S(1)}, u32[]{:S(2)}, u32[]{:S(2)}) collective-permute-start(f32[2,64]{1,0:T(2,128)S(1)} %get-tuple-element.220), channel_id=1, source_target_pairs={{0,1},{1,2},{2,3},{3,4},{4,5},{5,6},{6,7},{7,8},{8,9},{9,10},{10,1... | collective-permute-start | bytes 1544 | tf_op jit(solution)/shard_map/ppermute | solution.py:10
  23.2 4.9 %collective-permute-start.3 = (f32[2,64]{1,0:T(2,128)S(1)}, f32[2,64]{1,0:T(2,128)S(1)}, u32[]{:S(2)}, u32[]{:S(2)}) collective-permute-start(f32[2,64]{1,0:T(2,128)S(1)} %get-tuple-element.221), channel_id=1, source_target_pairs={{1,0},{2,1},{3,2},{4,3},{5,4},{6,5},{7,6},{8,7},{9,8},{10,9},{11,1... | collective-permute-start | bytes 1544 | tf_op jit(solution)/shard_map/ppermute | solution.py:10
  31.9 4.6 %collective-permute-start.4 = (f32[2,64]{1,0:T(2,128)S(1)}, f32[2,64]{1,0:T(2,128)S(1)}, u32[]{:S(2)}, u32[]{:S(2)}) collective-permute-start(f32[2,64]{1,0:T(2,128)S(1)} %get-tuple-element.218), channel_id=1, source_target_pairs={{0,1},{1,2},{2,3},{3,4},{4,5},{5,6},{6,7},{7,8},{8,9},{9,10},{10,1... | collective-permute-start | bytes 1544 | tf_op jit(solution)/shard_map/ppermute | solution.py:10
  34.6 4.9 %collective-permute-start.5 = (f32[2,64]{1,0:T(2,128)S(1)}, f32[2,64]{1,0:T(2,128)S(1)}, u32[]{:S(2)}, u32[]{:S(2)}) collective-permute-start(f32[2,64]{1,0:T(2,128)S(1)} %get-tuple-element.219), channel_id=1, source_target_pairs={{1,0},{2,1},{3,2},{4,3},{5,4},{6,5},{7,6},{8,7},{9,8},{10,9},{11,1... | collective-permute-start | bytes 1544 | tf_op jit(solution)/shard_map/ppermute | solution.py:10
  42.8 4.3 %collective-permute-start.6 = (f32[2,64]{1,0:T(2,128)S(1)}, f32[2,64]{1,0:T(2,128)S(1)}, u32[]{:S(2)}, u32[]{:S(2)}) collective-permute-start(f32[2,64]{1,0:T(2,128)S(1)} %get-tuple-element.216), channel_id=1, source_target_pairs={{0,1},{1,2},{2,3},{3,4},{4,5},{5,6},{6,7},{7,8},{8,9},{9,10},{10,1... | collective-permute-start | bytes 1544 | tf_op jit(solution)/shard_map/ppermute | solution.py:10
  44.8 4.9 %collective-permute-start.7 = (f32[2,64]{1,0:T(2,128)S(1)}, f32[2,64]{1,0:T(2,128)S(1)}, u32[]{:S(2)}, u32[]{:S(2)}) collective-permute-start(f32[2,64]{1,0:T(2,128)S(1)} %get-tuple-element.217), channel_id=1, source_target_pairs={{1,0},{2,1},{3,2},{4,3},{5,4},{6,5},{7,6},{8,7},{9,8},{10,9},{11,1... | collective-permute-start | bytes 1544 | tf_op jit(solution)/shard_map/ppermute | solution.py:10
  53.0 4.3 %collective-permute-start.8 = (f32[2,64]{1,0:T(2,128)S(1)}, f32[2,64]{1,0:T(2,128)S(1)}, u32[]{:S(2)}, u32[]{:S(2)}) collective-permute-start(f32[2,64]{1,0:T(2,128)S(1)} %get-tuple-element.214), channel_id=1, source_target_pairs={{0,1},{1,2},{2,3},{3,4},{4,5},{5,6},{6,7},{7,8},{8,9},{9,10},{10,1... | collective-permute-start | bytes 1544 | tf_op jit(solution)/shard_map/ppermute | solution.py:10
  54.9 4.9 %collective-permute-start.9 = (f32[2,64]{1,0:T(2,128)S(1)}, f32[2,64]{1,0:T(2,128)S(1)}, u32[]{:S(2)}, u32[]{:S(2)}) collective-permute-start(f32[2,64]{1,0:T(2,128)S(1)} %get-tuple-element.215), channel_id=1, source_target_pairs={{1,0},{2,1},{3,2},{4,3},{5,4},{6,5},{7,6},{8,7},{9,8},{10,9},{11,1... | collective-permute-start | bytes 1544 | tf_op jit(solution)/shard_map/ppermute | solution.py:10
  63.2 4.4 %collective-permute-start.10 = (f32[2,64]{1,0:T(2,128)S(1)}, f32[2,64]{1,0:T(2,128)S(1)}, u32[]{:S(2)}, u32[]{:S(2)}) collective-permute-start(f32[2,64]{1,0:T(2,128)S(1)} %get-tuple-element.212), channel_id=1, source_target_pairs={{0,1},{1,2},{2,3},{3,4},{4,5},{5,6},{6,7},{7,8},{8,9},{9,10},{10,1... | collective-permute-start | bytes 1544 | tf_op jit(solution)/shard_map/ppermute | solution.py:10
  65.1 6.1 %collective-permute-start.11 = (f32[2,64]{1,0:T(2,128)S(1)}, f32[2,64]{1,0:T(2,128)S(1)}, u32[]{:S(2)}, u32[]{:S(2)}) collective-permute-start(f32[2,64]{1,0:T(2,128)S(1)} %get-tuple-element.213), channel_id=1, source_target_pairs={{1,0},{2,1},{3,2},{4,3},{5,4},{6,5},{7,6},{8,7},{9,8},{10,9},{11,1... | collective-permute-start | bytes 1544 | tf_op jit(solution)/shard_map/ppermute | solution.py:10
  74.6 4.5 %collective-permute-start.12 = (f32[2,64]{1,0:T(2,128)S(1)}, f32[2,64]{1,0:T(2,128)S(1)}, u32[]{:S(2)}, u32[]{:S(2)}) collective-permute-start(f32[2,64]{1,0:T(2,128)S(1)} %get-tuple-element.210), channel_id=1, source_target_pairs={{0,1},{1,2},{2,3},{3,4},{4,5},{5,6},{6,7},{7,8},{8,9},{9,10},{10,1... | collective-permute-start | bytes 1544 | tf_op jit(solution)/shard_map/ppermute | solution.py:10
  76.6 7.0 %collective-permute-start.13 = (f32[2,64]{1,0:T(2,128)S(1)}, f32[2,64]{1,0:T(2,128)S(1)}, u32[]{:S(2)}, u32[]{:S(2)}) collective-permute-start(f32[2,64]{1,0:T(2,128)S(1)} %get-tuple-element.211), channel_id=1, source_target_pairs={{1,0},{2,1},{3,2},{4,3},{5,4},{6,5},{7,6},{8,7},{9,8},{10,9},{11,1... | collective-permute-start | bytes 1544 | tf_op jit(solution)/shard_map/ppermute | solution.py:10
  86.8 4.5 %collective-permute-start.14 = (f32[2,64]{1,0:T(2,128)S(1)}, f32[2,64]{1,0:T(2,128)S(1)}, u32[]{:S(2)}, u32[]{:S(2)}) collective-permute-start(f32[2,64]{1,0:T(2,128)S(1)} %get-tuple-element.208), channel_id=1, source_target_pairs={{0,1},{1,2},{2,3},{3,4},{4,5},{5,6},{6,7},{7,8},{8,9},{9,10},{10,1... | collective-permute-start | bytes 1544 | tf_op jit(solution)/shard_map/ppermute | solution.py:10
  88.8 7.0 %collective-permute-start.15 = (f32[2,64]{1,0:T(2,128)S(1)}, f32[2,64]{1,0:T(2,128)S(1)}, u32[]{:S(2)}, u32[]{:S(2)}) collective-permute-start(f32[2,64]{1,0:T(2,128)S(1)} %get-tuple-element.209), channel_id=1, source_target_pairs={{1,0},{2,1},{3,2},{4,3},{5,4},{6,5},{7,6},{8,7},{9,8},{10,9},{11,1... | collective-permute-start | bytes 1544 | tf_op jit(solution)/shard_map/ppermute | solution.py:10
  99.2 5.6 %collective-permute-start.16 = (f32[2,64]{1,0:T(2,128)S(1)}, f32[2,64]{1,0:T(2,128)S(1)}, u32[]{:S(2)}, u32[]{:S(2)}) collective-permute-start(f32[2,64]{1,0:T(2,128)S(1)} %get-tuple-element.206), channel_id=1, source_target_pairs={{0,1},{1,2},{2,3},{3,4},{4,5},{5,6},{6,7},{7,8},{8,9},{9,10},{10,1... | collective-permute-start | bytes 1544 | tf_op jit(solution)/shard_map/ppermute | solution.py:10
  101.2 7.0 %collective-permute-start.17 = (f32[2,64]{1,0:T(2,128)S(1)}, f32[2,64]{1,0:T(2,128)S(1)}, u32[]{:S(2)}, u32[]{:S(2)}) collective-permute-start(f32[2,64]{1,0:T(2,128)S(1)} %get-tuple-element.207), channel_id=1, source_target_pairs={{1,0},{2,1},{3,2},{4,3},{5,4},{6,5},{7,6},{8,7},{9,8},{10,9},{11,1... | collective-permute-start | bytes 1544 | tf_op jit(solution)/shard_map/ppermute | solution.py:10
  198.4 116.1 %copy-start.2 = (f32[8]{0:T(128)S(1)}, f32[8]{0:T(128)}, u32[]{:S(2)}) copy-start(f32[8]{0:T(128)} %param.27) | copy-start | bytes 100
  227.4 147.1 %copy-start.1 = (f32[1024]{0:T(1024)S(1)}, f32[1024]{0:T(1024)}, u32[]{:S(2)}) copy-start(f32[1024]{0:T(1024)} %param.26) | copy-start | bytes 12292
where the time goes:
time: 381 us; the launch traced here: 376 us
  blocking collectives  92.8 us (24%)
  between operations  90.5 us (24%)
  other arithmetic  61.5 us (16%)
  starting transfers between devices  45.7 us (12%)
  local copies, waits for them, and re-layouts  38.6 us (10%)
  waiting for transfers between devices  24.5 us (6%)
  matrix products  22.1 us (6%)
    all_gather x1, blocking collectives, body(): stacked_slab = lax.all_gather(local_factor, 'slab', axis=0, tiled=True)  52.3 us
    ppermute x18, starting transfers between devices, from_behind(): return lax.ppermute(array, axis, pairs)  45.7 us
    all_gather x1, blocking collectives, body(): stacked_group = lax.all_gather(middle, 'group', axis=0, tiled=True)  40.5 us
    ppermute x18, waiting for transfers between devices, from_behind(): return lax.ppermute(array, axis, pairs)  24.5 us
    reduce_sum x36, other arithmetic, upper_factor(): denom = jnp.sum(mirror * mirror)  22.3 us
    reduce_sum x36, other arithmetic, upper_factor(): magnitude = jnp.sqrt(jnp.sum(column * column))  21.8 us
    slice x36, local copies, waits for them, and re-layouts, upper_factor(): alpha = jnp.where(column[index] >= 0, -magnitude, magnitude)  20.7 us
    dot_general x9, matrix products, apply_operator(): jnp.einsum('eij,ej->ei', operator, stacked, precision=lax.Precision.HIGHEST)  16.4 us
  transfers between devices with their start and end apart: 18, of which 8 were waited for; matrix products, arithmetic and copies ran while one was open for 2% of the time, Pallas kernels for 0%

commit v1 on v0

v1 whole, which is shorter than its diff:
```python
import functools

import jax
import jax.numpy as jnp
from jax import lax
from jax.experimental import pallas as pl
from jax.experimental.pallas import tpu as pltpu
from jax.sharding import PartitionSpec as P

AXES = ("group", "slab")
WIDTH = 64
LANES = 128
REACH = 2
BANDS = 2 * REACH + 1
HALF = WIDTH // 2
ROWS = BANDS * HALF
PAD = 8


def shifted(array, by):
    size = lax.axis_size(AXES)
    pairs = [(i, i + by) for i in range(size) if 0 <= i + by < size]
    return lax.ppermute(array, AXES, pairs)


def lane_ids(rows):
    return lax.broadcasted_iota(jnp.int32, (rows, LANES), 1)


def band_kernel(op_ref, adj_ref, counts_ref, start_ref, rhs_ref, out_ref):
    elems, _, columns = op_ref.shape
    faces = columns // WIDTH - 1
    base = lax.axis_index(AXES) * elems
    left = lane_ids(HALF) < WIDTH

    def one(e, carry):
        blocks = []
        for tile in range(columns // LANES):
            lanes = pl.ds(tile * LANES, LANES)
            top = op_ref[e, pl.ds(0, HALF), lanes]
            low = op_ref[e, pl.ds(HALF, HALF), lanes]
            blocks.append(jnp.where(left, top, pltpu.roll(low, WIDTH, 1)))
            blocks.append(jnp.where(left, pltpu.roll(top, WIDTH, 1), low))
        if columns % LANES:
            lanes = pl.ds(columns - WIDTH, WIDTH)
            top = op_ref[e, pl.ds(0, HALF), lanes]
            low = op_ref[e, pl.ds(HALF, HALF), lanes]
            blocks.append(jnp.concatenate([top, low], axis=1))
        count = counts_ref[e]
        place = []
        for face in range(faces):
            offset = adj_ref[face, e] - (base + e) + REACH
            place.append(jnp.where(face < count, offset, -1))
        for band in range(BANDS):
            rows = pl.ds(pl.multiple_of(e * ROWS + band * HALF, HALF), HALF)
            total = blocks[0] if band == REACH else None
            if band != REACH:
                for face in range(faces):
                    weight = jnp.where(place[face] == band, jnp.float32(1), jnp.float32(0))
                    term = blocks[face + 1] * weight
                    total = term if total is None else total + term
            out_ref[rows, :] = total
        return carry

    lax.fori_loop(0, elems, one, 0)
    tail = elems * ROWS
    out_ref[pl.ds(tail, 8), :] = start_ref[...]
    out_ref[pl.ds(tail + 8, 8), :] = rhs_ref[...]


def basis_kernel(
    elems, steps, copies,
    below_ref, own_ref, above_ref, far_low_ref, far_high_ref, shifts_ref,
    basis_ref, gram_ref,
    held, vecs, given, sems,
):
    block = elems * ROWS + 16
    sources = (below_ref, own_ref, above_ref)
    moves = [
        pltpu.make_async_copy(source, held.at[pl.ds(part * block, block), :], sems.at[part])
        for part, source in enumerate(sources)
    ]
    for move in moves:
        move.start()
    level = vecs.shape[0] // (steps + 2)
    lane = lane_ids(8)
    left8 = lane < WIDTH
    lane_h = lane_ids(HALF)
    row_h = lax.broadcasted_iota(jnp.int32, (HALF, LANES), 0)
    left = lane_h < WIDTH
    spot = lane_h % WIDTH
    pick_top = spot == row_h
    pick_low = spot == row_h + HALF
    for move in moves:
        move.wait()

    def spread(ref, row, packed):
        turned = pltpu.roll(packed, WIDTH, 1)
        ref[pl.ds(row, 8, stride=2), :] = jnp.where(left8, packed, turned)
        ref[pl.ds(row + 1, 8, stride=2), :] = jnp.where(left8, turned, packed)

    for part in range(3):
        tail = part * block + elems * ROWS
        spread(vecs, PAD + part * elems, held[pl.ds(tail, 8), :])
        spread(given, part * elems, held[pl.ds(tail + 8, 8), :])
    for ref, row in ((far_low_ref, PAD - 2), (far_high_ref, PAD + 3 * elems)):
        packed = jnp.broadcast_to(ref[...], (8, LANES))
        turned = pltpu.roll(packed, WIDTH, 1)
        vecs[pl.ds(row, 1), :] = jnp.where(left8, packed, turned)[:1]
        vecs[pl.ds(row + 1, 1), :] = jnp.where(left8, turned, packed)[:1]

    def times(e, at):
        first = e * ROWS + (e // elems) * 16
        total = None
        for band in range(BANDS):
            rows = pl.ds(pl.multiple_of(first + band * HALF, 16), HALF)
            near = vecs[pl.ds(at + e + (band - REACH), 1), :]
            term = held[rows, :] * near
            total = term if total is None else total + term
        top = jnp.sum(jnp.where(left, total, 0.0), axis=1, keepdims=True)
        low = jnp.sum(jnp.where(left, 0.0, total), axis=1, keepdims=True)
        placed = jnp.where(pick_top, top, jnp.where(pick_low, low, 0.0))
        return jnp.sum(placed, axis=0, keepdims=True)

    unroll = 4

    def residual_group(group, carry):
        for k in range(unroll):
            e = group * unroll + k
            vecs[pl.ds(level + PAD + e, 1), :] = given[pl.ds(e, 1), :] - times(e, PAD)
        return carry

    lax.fori_loop(0, 3 * elems // unroll, residual_group, 0)

    def step(index, carry):
        at = (index + 1) * level + PAD
        shift = shifts_ref[index]
        first = REACH * (index + 1)

        def group(number, inner):
            for k in range(unroll):
                e = first + number * unroll + k
                vecs[pl.ds(at + level + e, 1), :] = times(e, at) - shift * vecs[pl.ds(at + e, 1), :]
            return inner

        lax.fori_loop(0, (3 * elems - 2 * first) // unroll, group, 0)
        return carry

    lax.fori_loop(0, steps, step, 0)

    rows = []
    for k in range(steps + 1):
        at = (k + 1) * level + PAD + elems
        packed = jnp.where(left8, vecs[pl.ds(at, 8, stride=2), :], vecs[pl.ds(at + 1, 8, stride=2), :])
        basis_ref[pl.ds(8 * k, 8), :] = packed
        rows.append(packed)
    total = jnp.zeros((8, LANES), jnp.float32)
    number = 0
    for i in range(steps + 1):
        for j in range(i, steps + 1):
            entry = jnp.sum(rows[i] * rows[j], axis=1, keepdims=True)
            total = jnp.where(lane == number, entry, total)
            number += 1
    gram = jnp.sum(total, axis=0, keepdims=True)
    gram_ref[...] = jnp.broadcast_to(gram, (copies, LANES))


def partial_kernel(copies, parts_ref, out_ref):
    total = jnp.sum(parts_ref[...], axis=0, keepdims=True)
    out_ref[...] = jnp.broadcast_to(total, (copies, LANES))


def inverse_root(value):
    guess = lax.rsqrt(value)
    return guess * (1.5 - 0.5 * value * guess * guess)


def finish_kernel(count, steps, parts_ref, basis_ref, start_ref, shifts_ref, sol_ref, res_ref, upper_ref):
    size = steps + 1
    lane = lane_ids(8)
    summed = jnp.broadcast_to(jnp.sum(parts_ref[...], axis=0, keepdims=True), (8, LANES))
    gram = {}
    number = 0
    for i in range(size):
        for j in range(i, size):
            entry = jnp.sum(jnp.where(lane == number, summed, 0.0), axis=1, keepdims=True)
            gram[i, j] = jnp.broadcast_to(entry, (8, LANES))
            number += 1
    factor = {}
    for k in range(size):
        turn = inverse_root(gram[k, k])
        for j in range(k, size):
            factor[k, j] = gram[k, j] * turn
        for i in range(k + 1, size):
            for j in range(i, size):
                gram[i, j] = gram[i, j] - factor[k, i] * factor[k, j]
    hess = {}
    for k in range(steps):
        for i in range(k + 1):
            hess[i, k] = factor[i, k] * shifts_ref[k] + factor[i, k + 1]
        hess[k + 1, k] = factor[k + 1, k + 1]
    target = [factor[0, 0]] + [jnp.zeros((8, LANES), jnp.float32)] * steps
    inverse = []
    for k in range(steps):
        a, b = hess[k, k], hess[k + 1, k]
        scale = inverse_root(a * a + b * b)
        cos, sin = a * scale, b * scale
        inverse.append(scale)
        for j in range(k + 1, steps):
            up, down = hess[k, j], hess[k + 1, j]
            hess[k, j] = cos * up + sin * down
            hess[k + 1, j] = cos * down - sin * up
        target[k], target[k + 1] = cos * target[k], -(sin * target[k])
    coeffs = [None] * steps
    for k in range(steps - 1, -1, -1):
        value = target[k]
        for j in range(k + 1, steps):
            value = value - hess[k, j] * coeffs[j]
        coeffs[k] = value * inverse[k]
    rows = [basis_ref[pl.ds(8 * k, 8), :] for k in range(size)]
    sol, res = 0.0, 0.0
    for k in range(steps):
        sol = sol + coeffs[k] * rows[k]
        res = res + coeffs[k] * (rows[k + 1] + shifts_ref[k] * rows[k])
    sol_ref[...] = start_ref[...] + sol
    res_ref[...] = rows[0] - res
    wide = lane_ids(16)
    tall = lax.broadcasted_iota(jnp.int32, (16, LANES), 0)
    scale = 1.0 / (count ** 0.5)
    upper = jnp.zeros((16, LANES), jnp.float32)
    for i in range(size):
        for j in range(i, size):
            entry = jnp.concatenate([factor[i, j]] * 2, axis=0) * scale
            upper = jnp.where((wide == j) & (tall == i), entry, upper)
    upper_ref[...] = upper[:size, :size]


def body(operator, adjacency, counts, rhs, start, shifts):
    elems, width, columns = operator.shape
    steps = shifts.shape[0]
    devices = lax.axis_size(AXES)
    slabs = lax.axis_size("slab")
    groups = lax.axis_size("group")
    packed = elems * width // LANES
    block = elems * ROWS + 2 * packed
    vmem = pl.BlockSpec(memory_space=pltpu.VMEM)
    smem = pl.BlockSpec(memory_space=pltpu.SMEM)
    hbm = pl.BlockSpec(memory_space=pl.ANY)
    params = pltpu.CompilerParams(vmem_limit_bytes=32 * 1024 * 1024)
    f32 = jnp.float32

    x = start.reshape(packed, LANES)
    b = rhs.reshape(packed, LANES)
    far_low = shifted(x[packed - 1 :], 2)
    far_high = shifted(x[:1], -2)
    own = pl.pallas_call(
        band_kernel,
        out_shape=jax.ShapeDtypeStruct((block, LANES), f32),
        in_specs=[vmem, smem, smem, vmem, vmem],
        out_specs=vmem,
        compiler_params=params,
        name="bands",
    )(operator, adjacency.T, counts, x, b)
    below = shifted(own, 1)
    above = shifted(own, -1)
    basis, gram = pl.pallas_call(
        functools.partial(basis_kernel, elems, steps, slabs),
        out_shape=(
            jax.ShapeDtypeStruct((8 * (steps + 1), LANES), f32),
            jax.ShapeDtypeStruct((slabs, LANES), f32),
        ),
        in_specs=[hbm, hbm, hbm, vmem, vmem, smem],
        out_specs=(vmem, vmem),
        scratch_shapes=[
            pltpu.VMEM((3 * block, LANES), f32),
            pltpu.VMEM(((steps + 2) * (3 * elems + 2 * PAD), LANES), f32),
            pltpu.VMEM((3 * elems, LANES), f32),
            pltpu.SemaphoreType.DMA((3,)),
        ],
        compiler_params=params,
        name="basis",
    )(below, own, above, far_low, far_high, shifts)
    by_slab = lax.all_to_all(gram, "slab", 0, 0, tiled=True)
    partial = pl.pallas_call(
        functools.partial(partial_kernel, groups),
        out_shape=jax.ShapeDtypeStruct((groups, LANES), f32),
        in_specs=[vmem],
        out_specs=vmem,
        name="partial",
    )(by_slab)
    by_group = lax.all_to_all(partial, "group", 0, 0, tiled=True)
    sol, res, upper = pl.pallas_call(
        functools.partial(finish_kernel, devices * elems * width, steps),
        out_shape=(
            jax.ShapeDtypeStruct((packed, LANES), f32),
            jax.ShapeDtypeStruct((packed, LANES), f32),
            jax.ShapeDtypeStruct((steps + 1, steps + 1), f32),
        ),
        in_specs=[vmem, vmem, vmem, smem],
        out_specs=(vmem, vmem, vmem),
        name="finish",
    )(by_group, basis, x, shifts)
    return (sol.reshape(-1), res.reshape(-1), upper)


def solution(mesh):
    split = P(AXES)
    return jax.shard_map(
        body,
        mesh=mesh,
        in_specs=(P(AXES, None, None), P(AXES, None), split, split, split, P()),
        out_specs=(split, split, P()),
        check_vma=False,
    )
```

time: 381 us -> 90.6 us (0.24); the launches traced: 376 us -> 90.1 us
  between operations: 90.5 us -> 0.72 us
  other arithmetic: 61.5 us -> 0 us
  blocking collectives: 92.8 us -> 43.1 us
  local copies, waits for them, and re-layouts: 38.6 us -> 4.91 us
  starting transfers between devices: 45.7 us -> 16 us
  matrix products: 22.1 us -> 0 us
  Pallas kernels: 0 us -> 16 us
  waiting for transfers between devices: 24.5 us -> 9.35 us
    all_gather x2 -> x0, blocking collectives: 92.8 us -> none  [the longest x1 52.3 us: body(): stacked_slab = lax.all_gather(local_factor, 'slab', axis=0, tiled=True)]
    reduce_sum x79 -> x0, other arithmetic: 48.5 us -> none  [the longest x36 22.3 us: upper_factor(): denom = jnp.sum(mirror * mirror)]
    all_to_all x0 -> x2, blocking collectives: none -> 43.1 us  [the longest x1 29.7 us: body(): by_group = lax.all_to_all(partial, 'group', 0, 0, tiled=True)]
    ppermute x18 -> x4, starting transfers between devices: 45.7 us -> 16 us  [shifted(): return lax.ppermute(array, AXES, pairs)]
    slice x79 -> x1, local copies, waits for them, and re-layouts: 24.4 us -> 0.01 us  [body(): far_high = shifted(x[:1], -2)]
    dot_general x48 -> x0, matrix products: 22.1 us -> none  [the longest x9 16.4 us: apply_operator(): jnp.einsum('eij,ej->ei', operator, stacked, precision=lax.Precision.HIGHEST)]
    pallas_call x0 -> x4, Pallas kernels: none -> 16 us  [the longest x1 10.7 us: body(): pl.pallas_call(functools.partial(basis_kernel, elems, steps, slabs), out_...]
    ppermute x18 -> x4, waiting for transfers between devices: 24.5 us -> 9.35 us  [shifted(): return lax.ppermute(array, AXES, pairs)]
  transfers between devices with their start and end apart: 18 -> 4, of which waited for: 8 -> 1; matrix products, arithmetic and copies ran while one was open for 2% -> 0% of each run, Pallas kernels for 0% -> 0%
where the time goes in v1:
time: 90.6 us; the launch traced here: 90.1 us
  blocking collectives  43.1 us (48%)
  Pallas kernels  16 us (18%)
  starting transfers between devices  16 us (18%)
  waiting for transfers between devices  9.35 us (10%)
  local copies, waits for them, and re-layouts  4.91 us (5%)
    all_to_all x1, blocking collectives, body(): by_group = lax.all_to_all(partial, 'group', 0, 0, tiled=True)  29.7 us
    ppermute x4, starting transfers between devices, shifted(): return lax.ppermute(array, AXES, pairs)  16 us
    all_to_all x1, blocking collectives, body(): by_slab = lax.all_to_all(gram, 'slab', 0, 0, tiled=True)  13.4 us
    pallas_call x1, Pallas kernels, body(): pl.pallas_call(functools.partial(basis_kernel, elems, steps, slabs), out_...  10.7 us
    ppermute x4, waiting for transfers between devices, shifted(): return lax.ppermute(array, AXES, pairs)  9.35 us
    unnamed x14, local copies, waits for them, and re-layouts  4.91 us
    pallas_call x1, Pallas kernels, body(): pl.pallas_call(band_kernel, out_shape=jax.ShapeDtypeStruct((block, LANES)...  2.22 us
  transfers between devices with their start and end apart: 4, of which 1 were waited for; matrix products, arithmetic and copies ran while one was open for 0% of the time, Pallas kernels for 0%

profile of v1, /device:TPU:1, one launch (start us, length us, event | category | flops | bytes accessed | tf_op | source)
XLA Modules:
  0.0 90.1 jit_solution(18035446012255221876)
XLA Ops:
  0.6 0.0 copy-start
  0.6 1.6 %copy-done = f32[16,64,448]{2,1,0:T(8,128)S(1)} copy-done((f32[16,64,448]{2,1,0:T(8,128)S(1)}, f32[16,64,448]{2,1,0:T(8,128)}, u32[]{:S(2)}) %copy-start) | copy-done | bytes 1835032
  2.2 0.0 copy-start.2
  2.2 0.7 copy-done.2
  2.9 0.7 copy-done.3
  3.6 0.7 copy-done.4
  4.3 0.7 copy-done.6
  4.9 2.2 %bands.1.own_ref = f32[2576,128]{1,0:T(8,128)S(1)} custom-call(f32[16,64,448]{2,1,0:T(8,128)S(1)} %copy-done, s32[6,16]{1,0:T(8,128)S(1)} %bitcast.20, s32[16]{0:T(128)S(1)} %copy-done.6, f32[8,128]{1,0:T(8,128)S(1)} %bitcast.18, f32[8,128]{1,0:T(8,128)S(1)} %bitcast.21), custom_call_target="tpu_custom_call" | custom-call | tf_op jit(solution)/shard_map/bands/pallas_call | solution.py:256
  7.2 8.8 %collective-permute-start.1 = (f32[2576,128]{1,0:T(8,128)S(1)}, f32[2576,128]{1,0:T(8,128)S(1)}, u32[]{:S(2)}, u32[]{:S(2)}) collective-permute-start(f32[2576,128]{1,0:T(8,128)S(1)} %bands.1.own_ref), channel_id=1, source_target_pairs={{1,0},{2,1},{3,2},{4,3},{5,4},{6,5},{7,6},{8,7},{9,8},{10,9},{11,1... | collective-permute-start | bytes 3956744 | tf_op jit(solution)/shard_map/ppermute | solution.py:23
  16.0 1.9 %collective-permute-start = (f32[2576,128]{1,0:T(8,128)S(1)}, f32[2576,128]{1,0:T(8,128)S(1)}, u32[]{:S(2)}, u32[]{:S(2)}) collective-permute-start(f32[2576,128]{1,0:T(8,128)S(1)} %bands.1.own_ref), channel_id=1, source_target_pairs={{0,1},{1,2},{2,3},{3,4},{4,5},{5,6},{6,7},{7,8},{8,9},{9,10},{10,1... | collective-permute-start | bytes 3956744 | tf_op jit(solution)/shard_map/ppermute | solution.py:23
  17.9 1.3 %collective-permute-start.3 = (f32[1,128]{1,0:T(1,128)S(1)}, f32[1,128]{1,0:T(1,128)S(1)}, u32[]{:S(2)}, u32[]{:S(2)}) collective-permute-start(f32[1,128]{1,0:T(1,128)S(1)} %get-tuple-element.13), channel_id=1, source_target_pairs={{2,0},{3,1},{4,2},{5,3},{6,4},{7,5},{8,6},{9,7},{10,8},{11,9},{12,... | collective-permute-start | bytes 1544 | tf_op jit(solution)/shard_map/ppermute | solution.py:23
  19.2 4.0 %collective-permute-start.2 = (f32[1,128]{1,0:T(1,128)S(1)}, f32[1,128]{1,0:T(1,128)S(1)}, u32[]{:S(2)}, u32[]{:S(2)}) collective-permute-start(f32[1,128]{1,0:T(1,128)S(1)} %get-tuple-element.14), channel_id=1, source_target_pairs={{0,2},{1,3},{2,4},{3,5},{4,6},{5,7},{6,8},{7,9},{8,10},{9,11},{10,... | collective-permute-start | bytes 1544 | tf_op jit(solution)/shard_map/ppermute | solution.py:23
  23.2 0.0 collective-permute-done.3.far_high_ref
  23.2 9.3 %collective-permute-done.2.far_low_ref = f32[1,128]{1,0:T(1,128)S(1)} collective-permute-done((f32[1,128]{1,0:T(1,128)S(1)}, f32[1,128]{1,0:T(1,128)S(1)}, u32[]{:S(2)}, u32[]{:S(2)}) %collective-permute-start.2) | collective-permute-done | bytes 544 | tf_op jit(solution)/shard_map/ppermute | solution.py:23
  32.6 0.0 collective-permute-done.1.above_ref
  32.6 0.0 collective-permute-done.below_ref
  32.6 0.0 copy-done.5
  32.6 10.7 %basis.1 = (f32[72,128]{1,0:T(8,128)S(1)}, f32[32,128]{1,0:T(8,128)S(1)}) custom-call(f32[2576,128]{1,0:T(8,128)S(1)} %collective-permute-done.below_ref, f32[2576,128]{1,0:T(8,128)S(1)} %bands.1.own_ref, f32[2576,128]{1,0:T(8,128)S(1)} %collective-permute-done.1.above_ref, f32[1,128]{1,0:T(1,128)S(1)} %collective-permute-done.2.far_low_ref, ...), custom_call_target="tpu_custom_call" | custom-call | tf_op jit(solution)/shard_map/basis/pallas_call | solution.py:266
  43.3 0.0 copy-start.1
  43.3 0.6 copy-done.1
  43.9 13.4 %all_to_all.22 = f32[32,1,128]{2,1,0:T(1,128)} all-to-all(f32[32,1,128]{2,1,0:T(1,128)S(1)} %bitcast.19), channel_id=1, replica_groups=mesh['group'=16,'slab'=32] {'slab'}, dimensions={0} | all-to-all | bytes 32768 | tf_op jit(solution)/shard_map/all_to_all | solution.py:283
  57.3 1.3 %partial.1 = f32[16,128]{1,0:T(8,128)} custom-call(f32[32,128]{1,0:T(8,128)} %bitcast.22), custom_call_target="tpu_custom_call" | custom-call | tf_op jit(solution)/shard_map/partial/pallas_call | solution.py:284
  58.6 29.7 %all_to_all.23 = f32[16,1,128]{2,1,0:T(1,128)} all-to-all(f32[16,1,128]{2,1,0:T(1,128)} %bitcast.24), channel_id=1, replica_groups=mesh['group'=16,'slab'=32] {'group'}, dimensions={0} | all-to-all | bytes 16384 | tf_op jit(solution)/shard_map/all_to_all | solution.py:291
  88.3 1.7 %finish.1 = (f32[8,128]{1,0:T(8,128)}, f32[8,128]{1,0:T(8,128)}, f32[9,9]{1,0:T(8,128)}) custom-call(f32[16,128]{1,0:T(8,128)} %bitcast.23, f32[72,128]{1,0:T(8,128)} %copy-done.1, f32[8,128]{1,0:T(8,128)} %bitcast.17, f32[8]{0:T(128)} %shifts_ref.3), custom_call_target="tpu_custom_call" | custom-call | tf_op jit(solution)/shard_map/finish/pallas_call | solution.py:292
  (5 shorter events, 0.0 us)
Async XLA Ops:
  0.6 1.6 %copy-start = (f32[16,64,448]{2,1,0:T(8,128)S(1)}, f32[16,64,448]{2,1,0:T(8,128)}, u32[]{:S(2)}) copy-start(f32[16,64,448]{2,1,0:T(8,128)} %op_ref.1) | copy-start | bytes 5505028
  2.2 0.7 copy-start.2
  2.9 0.7 copy-start.3
  3.6 0.7 copy-start.4
  4.3 0.7 copy-start.6
  4.9 27.6 %copy-start.5 = (f32[8]{0:T(128)S(1)}, f32[8]{0:T(128)}, u32[]{:S(2)}) copy-start(f32[8]{0:T(128)} %shifts_ref.3) | copy-start | bytes 100
  7.2 25.4 %collective-permute-start.1 = (f32[2576,128]{1,0:T(8,128)S(1)}, f32[2576,128]{1,0:T(8,128)S(1)}, u32[]{:S(2)}, u32[]{:S(2)}) collective-permute-start(f32[2576,128]{1,0:T(8,128)S(1)} %bands.1.own_ref), channel_id=1, source_target_pairs={{1,0},{2,1},{3,2},{4,3},{5,4},{6,5},{7,6},{8,7},{9,8},{10,9},{11,1... | collective-permute-start | bytes 3956744 | tf_op jit(solution)/shard_map/ppermute | solution.py:23
  16.0 16.6 %collective-permute-start = (f32[2576,128]{1,0:T(8,128)S(1)}, f32[2576,128]{1,0:T(8,128)S(1)}, u32[]{:S(2)}, u32[]{:S(2)}) collective-permute-start(f32[2576,128]{1,0:T(8,128)S(1)} %bands.1.own_ref), channel_id=1, source_target_pairs={{0,1},{1,2},{2,3},{3,4},{4,5},{5,6},{6,7},{7,8},{8,9},{9,10},{10,1... | collective-permute-start | bytes 3956744 | tf_op jit(solution)/shard_map/ppermute | solution.py:23
  17.9 5.3 %collective-permute-start.3 = (f32[1,128]{1,0:T(1,128)S(1)}, f32[1,128]{1,0:T(1,128)S(1)}, u32[]{:S(2)}, u32[]{:S(2)}) collective-permute-start(f32[1,128]{1,0:T(1,128)S(1)} %get-tuple-element.13), channel_id=1, source_target_pairs={{2,0},{3,1},{4,2},{5,3},{6,4},{7,5},{8,6},{9,7},{10,8},{11,9},{12,... | collective-permute-start | bytes 1544 | tf_op jit(solution)/shard_map/ppermute | solution.py:23
  19.2 13.4 %collective-permute-start.2 = (f32[1,128]{1,0:T(1,128)S(1)}, f32[1,128]{1,0:T(1,128)S(1)}, u32[]{:S(2)}, u32[]{:S(2)}) collective-permute-start(f32[1,128]{1,0:T(1,128)S(1)} %get-tuple-element.14), channel_id=1, source_target_pairs={{0,2},{1,3},{2,4},{3,5},{4,6},{5,7},{6,8},{7,9},{8,10},{9,11},{10,... | collective-permute-start | bytes 1544 | tf_op jit(solution)/shard_map/ppermute | solution.py:23
  43.3 0.6 copy-start.1

commit v2 on v1

v2 whole, which is shorter than its diff:
```python
import functools

import jax
import jax.numpy as jnp
from jax import lax
from jax.experimental import pallas as pl
from jax.experimental.pallas import tpu as pltpu
from jax.sharding import PartitionSpec as P

AXES = ("group", "slab")
WIDTH = 64
LANES = 128
REACH = 2
BANDS = 2 * REACH + 1
HALF = WIDTH // 2
ROWS = BANDS * HALF
CHUNK = 4
PAD = 8


def shifted(array, by):
    size = lax.axis_size(AXES)
    pairs = [(i, i + by) for i in range(size) if 0 <= i + by < size]
    return lax.ppermute(array, AXES, pairs)


def lane_ids(rows):
    return lax.broadcasted_iota(jnp.int32, (rows, LANES), 1)


def band_kernel(op_ref, adj_ref, counts_ref, start_ref, rhs_ref, out_ref, held, made, in_sems, out_sems):
    elems, _, columns = op_ref.shape
    faces = columns // WIDTH - 1
    chunks = elems // CHUNK
    base = lax.axis_index(AXES) * elems
    left = lane_ids(HALF) < WIDTH
    tail = elems * ROWS

    def arriving(chunk):
        part = pl.ds(chunk * CHUNK, CHUNK)
        return pltpu.make_async_copy(op_ref.at[part], held.at[part], in_sems.at[chunk])

    def leaving(chunk):
        size = CHUNK * ROWS
        part = pl.ds(pl.multiple_of(chunk * size, size), size)
        return pltpu.make_async_copy(made.at[part, :], out_ref.at[part, :], out_sems.at[chunk])

    for chunk in range(chunks):
        arriving(chunk).start()
    extras = [
        pltpu.make_async_copy(start_ref, out_ref.at[pl.ds(tail, 8), :], out_sems.at[chunks]),
        pltpu.make_async_copy(rhs_ref, out_ref.at[pl.ds(tail + 8, 8), :], out_sems.at[chunks + 1]),
    ]
    for extra in extras:
        extra.start()

    def one(e):
        blocks = []
        for tile in range(columns // LANES):
            lanes = pl.ds(tile * LANES, LANES)
            top = held[e, pl.ds(0, HALF), lanes]
            low = held[e, pl.ds(HALF, HALF), lanes]
            blocks.append(jnp.where(left, top, pltpu.roll(low, WIDTH, 1)))
            blocks.append(jnp.where(left, pltpu.roll(top, WIDTH, 1), low))
        if columns % LANES:
            lanes = pl.ds(columns - WIDTH, WIDTH)
            top = held[e, pl.ds(0, HALF), lanes]
            low = held[e, pl.ds(HALF, HALF), lanes]
            blocks.append(jnp.concatenate([top, low], axis=1))
        count = counts_ref[e]
        place = []
        for face in range(faces):
            offset = adj_ref[face, e] - (base + e) + REACH
            place.append(jnp.where(face < count, offset, -1))
        for band in range(BANDS):
            rows = pl.ds(pl.multiple_of(e * ROWS + band * HALF, HALF), HALF)
            total = blocks[0] if band == REACH else None
            if band != REACH:
                for face in range(faces):
                    weight = jnp.where(place[face] == band, jnp.float32(1), jnp.float32(0))
                    term = blocks[face + 1] * weight
                    total = term if total is None else total + term
            made[rows, :] = total

    def some(chunk, carry):
        arriving(chunk).wait()
        for k in range(CHUNK):
            one(chunk * CHUNK + k)
        leaving(chunk).start()
        return carry

    lax.fori_loop(0, chunks, some, 0)
    for chunk in range(chunks):
        leaving(chunk).wait()
    for extra in extras:
        extra.wait()


def stacked_sums(terms, row):
    for span in (4, 2, 1):
        low = (row & span) == 0
        half = len(terms) // 2
        merged = []
        for a, b in zip(terms[:half], terms[half:]):
            kept = jnp.where(low, a, b)
            if span == 4:
                moved = pltpu.roll(jnp.where(low, b, a), 4, 0)
            else:
                moved = jnp.where(low, pltpu.roll(a, 8 - span, 0), pltpu.roll(b, span, 0))
            merged.append(kept + moved)
        terms = merged
    return terms[0]


def basis_kernel(
    elems, steps,
    below_ref, own_ref, above_ref, far_low_ref, far_high_ref, shifts_ref,
    basis_ref, gram_ref,
    vecs,
):
    refs = (below_ref, own_ref, above_ref)
    level = 3 * elems + 2 * PAD
    given = (steps + 2) * level
    lane = lane_ids(8)
    row = lax.broadcasted_iota(jnp.int32, (8, LANES), 0)
    left = lane < WIDTH
    half = lane_ids(HALF)
    left_half = half < WIDTH
    pick_top = half % WIDTH == lax.broadcasted_iota(jnp.int32, (HALF, LANES), 0)
    pick_low = half % WIDTH == lax.broadcasted_iota(jnp.int32, (HALF, LANES), 0) + HALF

    empty = jnp.zeros((8, LANES), jnp.float32)
    for at in range(0, vecs.shape[0], 8):
        vecs[pl.ds(at, 8), :] = empty

    def spread(at, packed):
        turned = pltpu.roll(packed, WIDTH, 1)
        vecs[pl.ds(at, 8, stride=2), :] = jnp.where(left, packed, turned)
        vecs[pl.ds(at + 1, 8, stride=2), :] = jnp.where(left, turned, packed)

    for part, ref in enumerate(refs):
        tail = elems * ROWS
        spread(PAD + part * elems, ref[pl.ds(tail, 8), :])
        spread(given + PAD + part * elems, ref[pl.ds(tail + 8, 8), :])
    for ref, at in ((far_low_ref, PAD - 2), (far_high_ref, PAD + 3 * elems)):
        packed = jnp.broadcast_to(ref[...], (8, LANES))
        turned = pltpu.roll(packed, WIDTH, 1)
        vecs[pl.ds(at, 1), :] = jnp.where(left, packed, turned)[:1]
        vecs[pl.ds(at + 1, 1), :] = jnp.where(left, turned, packed)[:1]

    def times(part, first, at):
        near = [vecs[pl.ds(at + (k - REACH), 1), :] for k in range(8 + 2 * REACH)]
        terms = []
        for k in range(8):
            total = None
            for band in range(BANDS):
                rows = pl.ds((first + k) * ROWS + band * HALF, HALF)
                term = refs[part][rows, :] * near[k + band]
                total = term if total is None else total + term
            top = jnp.sum(jnp.where(left_half, total, 0.0), axis=1, keepdims=True)
            low = jnp.sum(jnp.where(left_half, 0.0, total), axis=1, keepdims=True)
            placed = jnp.where(pick_top, top, jnp.where(pick_low, low, 0.0))
            terms.append(jnp.sum(placed.reshape(HALF // 8, 8, LANES), axis=0))
        return stacked_sums(terms, row)

    def apply(index, groups):
        at = pl.multiple_of(index * level + PAD, 8)
        if isinstance(index, int):
            opening = index == 0
            source = given + PAD if opening else at
            sign, scale = (-1.0, 1.0) if opening else (1.0, -shifts_ref[index - 1])
        else:
            opening = index == 0
            source = pl.multiple_of(jnp.where(opening, given + PAD, at), 8)
            sign = jnp.where(opening, jnp.float32(-1), jnp.float32(1))
            scale = jnp.where(opening, jnp.float32(1), -shifts_ref[jnp.maximum(index - 1, 0)])
        made = []
        for part, first in groups:
            place = part * elems + first
            fresh = times(part, first, at + place)
            made.append((place, sign * fresh + scale * vecs[pl.ds(source + place, 8), :]))
        for place, value in made:
            vecs[pl.ds(at + level + place, 8), :] = value

    own = [(1, first) for first in range(0, elems, 8)]
    groups = [(part, first) for part in (0, 2) for first in range(0, elems, 8)]
    done = 0
    while done <= steps:
        reach = REACH * (steps - done)
        wanted = [
            (part, first)
            for part, first in groups
            if (elems - first - 8 < reach if part == 0 else first < reach)
        ]
        until = done
        while until <= steps:
            later = REACH * (steps - until)
            if wanted != [
                (part, first)
                for part, first in groups
                if (elems - first - 8 < later if part == 0 else first < later)
            ]:
                break
            until += 1

        def turn(index, carry, wanted=wanted):
            apply(index, wanted + own)
            return carry

        if until - done == 1:
            apply(done, wanted + own)
        else:
            lax.fori_loop(done, until, turn, 0)
        done = until

    rows = []
    for k in range(steps + 1):
        at = (k + 1) * level + PAD + elems
        packed = jnp.where(left, vecs[pl.ds(at, 8, stride=2), :], vecs[pl.ds(at + 1, 8, stride=2), :])
        basis_ref[pl.ds(8 * k, 8), :] = packed
        rows.append(packed)
    total = jnp.zeros((8, LANES), jnp.float32)
    number = 0
    for i in range(steps + 1):
        for j in range(i, steps + 1):
            entry = jnp.sum(rows[i] * rows[j], axis=1, keepdims=True)
            total = jnp.where(lane == number, entry, total)
            number += 1
    gram_ref[...] = jnp.sum(total, axis=0, keepdims=True)


def inverse_root(value):
    guess = lax.rsqrt(value)
    return guess * (1.5 - 0.5 * value * guess * guess)


def finish_kernel(count, steps, parts_ref, basis_ref, start_ref, shifts_ref, sol_ref, res_ref, upper_ref):
    size = steps + 1
    lane = lane_ids(8)
    summed = jnp.broadcast_to(jnp.sum(parts_ref[...], axis=0, keepdims=True), (8, LANES))
    gram = {}
    number = 0
    for i in range(size):
        for j in range(i, size):
            entry = jnp.sum(jnp.where(lane == number, summed, 0.0), axis=1, keepdims=True)
            gram[i, j] = jnp.broadcast_to(entry, (8, LANES))
            number += 1
    factor = {}
    for k in range(size):
        turn = inverse_root(gram[k, k])
        for j in range(k, size):
            factor[k, j] = gram[k, j] * turn
        for i in range(k + 1, size):
            for j in range(i, size):
                gram[i, j] = gram[i, j] - factor[k, i] * factor[k, j]
    hess = {}
    for k in range(steps):
        for i in range(k + 1):
            hess[i, k] = factor[i, k] * shifts_ref[k] + factor[i, k + 1]
        hess[k + 1, k] = factor[k + 1, k + 1]
    target = [factor[0, 0]] + [jnp.zeros((8, LANES), jnp.float32)] * steps
    inverse = []
    for k in range(steps):
        a, b = hess[k, k], hess[k + 1, k]
        scale = inverse_root(a * a + b * b)
        cos, sin = a * scale, b * scale
        inverse.append(scale)
        for j in range(k + 1, steps):
            up, down = hess[k, j], hess[k + 1, j]
            hess[k, j] = cos * up + sin * down
            hess[k + 1, j] = cos * down - sin * up
        target[k], target[k + 1] = cos * target[k], -(sin * target[k])
    coeffs = [None] * steps
    for k in range(steps - 1, -1, -1):
        value = target[k]
        for j in range(k + 1, steps):
            value = value - hess[k, j] * coeffs[j]
        coeffs[k] = value * inverse[k]
    rows = [basis_ref[pl.ds(8 * k, 8), :] for k in range(size)]
    sol, res = 0.0, 0.0
    for k in range(steps):
        sol = sol + coeffs[k] * rows[k]
        res = res + coeffs[k] * (rows[k + 1] + shifts_ref[k] * rows[k])
    sol_ref[...] = start_ref[...] + sol
    res_ref[...] = rows[0] - res
    wide = lane_ids(16)
    tall = lax.broadcasted_iota(jnp.int32, (16, LANES), 0)
    scale = 1.0 / (count ** 0.5)
    upper = jnp.zeros((16, LANES), jnp.float32)
    for i in range(size):
        for j in range(i, size):
            entry = jnp.concatenate([factor[i, j]] * 2, axis=0) * scale
            upper = jnp.where((wide == j) & (tall == i), entry, upper)
    upper_ref[...] = upper[:size, :size]


def body(operator, adjacency, counts, rhs, start, shifts):
    elems, width, columns = operator.shape
    steps = shifts.shape[0]
    devices = lax.axis_size(AXES)
    packed = elems * width // LANES
    block = elems * ROWS + 2 * packed
    vmem = pl.BlockSpec(memory_space=pltpu.VMEM)
    smem = pl.BlockSpec(memory_space=pltpu.SMEM)
    hbm = pl.BlockSpec(memory_space=pl.ANY)
    mebi = 1024 * 1024
    f32 = jnp.float32

    x = start.reshape(packed, LANES)
    b = rhs.reshape(packed, LANES)
    own = pl.pallas_call(
        band_kernel,
        out_shape=jax.ShapeDtypeStruct((block, LANES), f32),
        in_specs=[hbm, smem, smem, hbm, hbm],
        out_specs=hbm,
        scratch_shapes=[
            pltpu.VMEM(operator.shape, f32),
            pltpu.VMEM((elems * ROWS, LANES), f32),
            pltpu.SemaphoreType.DMA((elems // CHUNK,)),
            pltpu.SemaphoreType.DMA((elems // CHUNK + 2,)),
        ],
        compiler_params=pltpu.CompilerParams(vmem_limit_bytes=60 * mebi),
        name="bands",
    )(operator, adjacency.T, counts, x, b)
    below = shifted(own, 1)
    above = shifted(own, -1)
    far_low = shifted(x[packed - 1 :], 2)
    far_high = shifted(x[:1], -2)
    basis, gram = pl.pallas_call(
        functools.partial(basis_kernel, elems, steps),
        out_shape=(
            jax.ShapeDtypeStruct((8 * (steps + 1), LANES), f32),
            jax.ShapeDtypeStruct((1, LANES), f32),
        ),
        in_specs=[vmem, vmem, vmem, vmem, vmem, smem],
        out_specs=(vmem, vmem),
        scratch_shapes=[pltpu.VMEM(((steps + 3) * (3 * elems + 2 * PAD), LANES), f32)],
        compiler_params=pltpu.CompilerParams(vmem_limit_bytes=16 * mebi),
        name="basis",
    )(below, own, above, far_low, far_high, shifts)
    gram = lax.psum(gram, AXES)
    sol, res, upper = pl.pallas_call(
        functools.partial(finish_kernel, devices * elems * width, steps),
        out_shape=(
            jax.ShapeDtypeStruct((packed, LANES), f32),
            jax.ShapeDtypeStruct((packed, LANES), f32),
            jax.ShapeDtypeStruct((steps + 1, steps + 1), f32),
        ),
        in_specs=[vmem, vmem, vmem, smem],
        out_specs=(vmem, vmem, vmem),
        compiler_params=pltpu.CompilerParams(vmem_limit_bytes=4 * mebi),
        name="finish",
    )(gram, basis, x, shifts)
    return (sol.reshape(-1), res.reshape(-1), upper)


def solution(mesh):
    split = P(AXES)
    return jax.shard_map(
        body,
        mesh=mesh,
        in_specs=(P(AXES, None, None), P(AXES, None), split, split, split, P()),
        out_specs=(split, split, P()),
        check_vma=False,
    )
```

time: 90.6 us -> 150 us (1.66)
  blocking collectives: 43.1 us -> 113 us
  Pallas kernels: 16 us -> 9.45 us
  local copies, waits for them, and re-layouts: 4.91 us -> 1.33 us
    psum x0 -> x1, blocking collectives: none -> 113 us  [body(): gram = lax.psum(gram, AXES)]
    all_to_all x2 -> x0, blocking collectives: 43.1 us -> none  [the longest x1 29.7 us: body(): by_group = lax.all_to_all(partial, 'group', 0, 0, tiled=True)]
    pallas_call x2 -> x1, Pallas kernels: 12.1 us -> 4.48 us  [body(): pl.pallas_call(functools.partial(basis_kernel, elems, steps), out_shape=(...]
    unnamed x14 -> x6, local copies, waits for them, and re-layouts: 4.91 us -> 1.32 us
where the time goes in v2:
time: 150 us
  blocking collectives  113 us (75%)
  starting transfers between devices  16 us (11%)
  waiting for transfers between devices  9.62 us (6%)
  Pallas kernels  9.45 us (6%)
    psum x1, blocking collectives, body(): gram = lax.psum(gram, AXES)  113 us
    ppermute x4, starting transfers between devices, shifted(): return lax.ppermute(array, AXES, pairs)  16 us
    ppermute x4, waiting for transfers between devices, shifted(): return lax.ppermute(array, AXES, pairs)  9.62 us
    pallas_call x1, Pallas kernels, body(): pl.pallas_call(functools.partial(basis_kernel, elems, steps), out_shape=(...  4.48 us
    pallas_call x1, Pallas kernels, body(): pl.pallas_call(band_kernel, out_shape=jax.ShapeDtypeStruct((block, LANES)...  3.5 us
  transfers between devices with their start and end apart: 4, of which 1 were waited for; matrix products, arithmetic and copies ran while one was open for 0% of the time, Pallas kernels for 0%

profile of v2, /device:TPU:1, one launch (start us, length us, event | category | flops | bytes accessed | tf_op | source)
XLA Modules:
  0.0 150.1 jit_solution(7835794524832706418)
XLA Ops:
  0.6 0.0 copy-start.1
  0.6 0.0 copy-start.2
  0.7 3.5 %bands.1.own_ref = f32[2576,128]{1,0:T(8,128)} custom-call(f32[16,64,448]{2,1,0:T(8,128)} %op_ref.1, s32[6,16]{1,0:T(8,128)} %bitcast.11, s32[16]{0:T(128)} %counts_ref.1, f32[8,128]{1,0:T(8,128)} %bitcast.9, f32[8,128]{1,0:T(8,128)} %bitcast.12), custom_call_target="tpu_custom_call" | custom-call | tf_op jit(solution)/shard_map/bands/pallas_call | solution.py:311
  4.2 8.8 %collective-permute-start.1 = (f32[2576,128]{1,0:T(8,128)}, f32[2576,128]{1,0:T(8,128)S(1)}, u32[]{:S(2)}, u32[]{:S(2)}) collective-permute-start(f32[2576,128]{1,0:T(8,128)} %bands.1.own_ref), channel_id=1, source_target_pairs={{1,0},{2,1},{3,2},{4,3},{5,4},{6,5},{7,6},{8,7},{9,8},{10,9},{11,1... | collective-permute-start | bytes 3956744 | tf_op jit(solution)/shard_map/ppermute | solution.py:24
  13.0 1.9 %collective-permute-start = (f32[2576,128]{1,0:T(8,128)}, f32[2576,128]{1,0:T(8,128)S(1)}, u32[]{:S(2)}, u32[]{:S(2)}) collective-permute-start(f32[2576,128]{1,0:T(8,128)} %bands.1.own_ref), channel_id=1, source_target_pairs={{0,1},{1,2},{2,3},{3,4},{4,5},{5,6},{6,7},{7,8},{8,9},{9,10},{10,1... | collective-permute-start | bytes 3956744 | tf_op jit(solution)/shard_map/ppermute | solution.py:24
  14.9 0.0 copy-done.1
  14.9 1.3 collective-permute-start.3
  16.2 4.0 %collective-permute-start.2 = (f32[1,128]{1,0:T(1,128)S(1)}, f32[1,128]{1,0:T(1,128)S(1)}, u32[]{:S(2)}, u32[]{:S(2)}) collective-permute-start(f32[1,128]{1,0:T(1,128)S(1)} %get-tuple-element.14), channel_id=1, source_target_pairs={{0,2},{1,3},{2,4},{3,5},{4,6},{5,7},{6,8},{7,9},{8,10},{9,11},{10,... | collective-permute-start | bytes 1544 | tf_op jit(solution)/shard_map/ppermute | solution.py:24
  20.2 0.0 collective-permute-done.3.far_high_ref
  20.2 9.6 %collective-permute-done.2.far_low_ref = f32[1,128]{1,0:T(1,128)S(1)} collective-permute-done((f32[1,128]{1,0:T(1,128)S(1)}, f32[1,128]{1,0:T(1,128)S(1)}, u32[]{:S(2)}, u32[]{:S(2)}) %collective-permute-start.2) | collective-permute-done | bytes 544 | tf_op jit(solution)/shard_map/ppermute | solution.py:24
  29.8 0.0 collective-permute-done.1.above_ref
  29.8 0.0 collective-permute-done.below_ref
  29.8 0.0 copy-done.2
  29.8 0.0 copy-start
  29.8 1.3 copy-done
  31.2 4.5 %basis.1 = (f32[72,128]{1,0:T(8,128)S(1)}, f32[1,128]{1,0:T(1,128)S(1)}) custom-call(f32[2576,128]{1,0:T(8,128)S(1)} %collective-permute-done.below_ref, f32[2576,128]{1,0:T(8,128)S(1)} %copy-done, f32[2576,128]{1,0:T(8,128)S(1)} %collective-permute-done.1.above_ref, f32[1,128]{1,0:T(1,128)S(1)} %collective-permute-done.2.far_low_ref, ...), custom_call_target="tpu_custom_call" | custom-call | tf_op jit(solution)/shard_map/basis/pallas_call | solution.py:329
  35.6 113.0 %psum.7.parts_ref = f32[1,128]{1,0:T(1,128)S(1)} all-reduce(f32[1,128]{1,0:T(1,128)S(1)} %get-tuple-element.8), channel_id=1, replica_groups=mesh['group'=16,'slab'=32] {'group','slab'}, use_global_device_ids=true, to_apply=%region_0.0 | all-reduce | flops 128 | bytes 1024 | tf_op jit(solution)/shard_map/psum | solution.py:341
  148.6 1.5 finish.1
  (1 shorter events, 0.0 us)
Async XLA Ops:
  0.6 14.3 %copy-start.1 = (f32[1024]{0:T(1024)S(1)}, f32[1024]{0:T(1024)}, u32[]{:S(2)}) copy-start(f32[1024]{0:T(1024)} %param.10) | copy-start | bytes 12292
  0.6 29.2 %copy-start.2 = (f32[8]{0:T(128)S(1)}, f32[8]{0:T(128)}, u32[]{:S(2)}) copy-start(f32[8]{0:T(128)} %shifts_ref.3) | copy-start | bytes 100
  4.2 25.7 %collective-permute-start.1 = (f32[2576,128]{1,0:T(8,128)}, f32[2576,128]{1,0:T(8,128)S(1)}, u32[]{:S(2)}, u32[]{:S(2)}) collective-permute-start(f32[2576,128]{1,0:T(8,128)} %bands.1.own_ref), channel_id=1, source_target_pairs={{1,0},{2,1},{3,2},{4,3},{5,4},{6,5},{7,6},{8,7},{9,8},{10,9},{11,1... | collective-permute-start | bytes 3956744 | tf_op jit(solution)/shard_map/ppermute | solution.py:24
  13.0 16.9 %collective-permute-start = (f32[2576,128]{1,0:T(8,128)}, f32[2576,128]{1,0:T(8,128)S(1)}, u32[]{:S(2)}, u32[]{:S(2)}) collective-permute-start(f32[2576,128]{1,0:T(8,128)} %bands.1.own_ref), channel_id=1, source_target_pairs={{0,1},{1,2},{2,3},{3,4},{4,5},{5,6},{6,7},{7,8},{8,9},{9,10},{10,1... | collective-permute-start | bytes 3956744 | tf_op jit(solution)/shard_map/ppermute | solution.py:24
  14.9 5.3 %collective-permute-start.3 = (f32[1,128]{1,0:T(1,128)S(1)}, f32[1,128]{1,0:T(1,128)S(1)}, u32[]{:S(2)}, u32[]{:S(2)}) collective-permute-start(f32[1,128]{1,0:T(1,128)S(1)} %get-tuple-element.13), channel_id=1, source_target_pairs={{2,0},{3,1},{4,2},{5,3},{6,4},{7,5},{8,6},{9,7},{10,8},{11,9},{12,... | collective-permute-start | bytes 1544 | tf_op jit(solution)/shard_map/ppermute | solution.py:24
  16.2 13.6 %collective-permute-start.2 = (f32[1,128]{1,0:T(1,128)S(1)}, f32[1,128]{1,0:T(1,128)S(1)}, u32[]{:S(2)}, u32[]{:S(2)}) collective-permute-start(f32[1,128]{1,0:T(1,128)S(1)} %get-tuple-element.14), channel_id=1, source_target_pairs={{0,2},{1,3},{2,4},{3,5},{4,6},{5,7},{6,8},{7,9},{8,10},{9,11},{10,... | collective-permute-start | bytes 1544 | tf_op jit(solution)/shard_map/ppermute | solution.py:24
  29.8 1.3 copy-start

commit v3 on v2

--- a/solution.py
+++ b/solution.py
@@ -24,11 +24,25 @@
     return lax.ppermute(array, AXES, pairs)
 
 
+def between_chips(array):
+    size = lax.axis_size(AXES)
+    pairs = [(i, i + 1 if i % 2 else i - 1) for i in range(1, size - 1)]
+    return lax.ppermute(array, AXES, pairs)
+
+
+def within_chip(array):
+    size = lax.axis_size(AXES)
+    return lax.ppermute(array, AXES, [(i, i + 1 - 2 * (i % 2)) for i in range(size)])
+
+
 def lane_ids(rows):
     return lax.broadcasted_iota(jnp.int32, (rows, LANES), 1)
 
 
-def band_kernel(op_ref, adj_ref, counts_ref, start_ref, rhs_ref, out_ref, held, made, in_sems, out_sems):
+def band_kernel(
+    op_ref, adjacency_ref, valid_ref, start_ref, rhs_ref, out_ref,
+    held, adj_ref, counts_ref, in_sems, out_sems,
+):
     elems, _, columns = op_ref.shape
     faces = columns // WIDTH - 1
     chunks = elems // CHUNK
@@ -40,19 +54,20 @@
         part = pl.ds(chunk * CHUNK, CHUNK)
         return pltpu.make_async_copy(op_ref.at[part], held.at[part], in_sems.at[chunk])
 
-    def leaving(chunk):
-        size = CHUNK * ROWS
-        part = pl.ds(pl.multiple_of(chunk * size, size), size)
-        return pltpu.make_async_copy(made.at[part, :], out_ref.at[part, :], out_sems.at[chunk])
-
     for chunk in range(chunks):
         arriving(chunk).start()
+    scalars = [
+        pltpu.make_async_copy(adjacency_ref, adj_ref, out_sems.at[0]),
+        pltpu.make_async_copy(valid_ref, counts_ref, out_sems.at[1]),
+    ]
     extras = [
-        pltpu.make_async_copy(start_ref, out_ref.at[pl.ds(tail, 8), :], out_sems.at[chunks]),
-        pltpu.make_async_copy(rhs_ref, out_ref.at[pl.ds(tail + 8, 8), :], out_sems.at[chunks + 1]),
+        pltpu.make_async_copy(start_ref, out_ref.at[pl.ds(tail, 8), :], out_sems.at[2]),
+        pltpu.make_async_copy(rhs_ref, out_ref.at[pl.ds(tail + 8, 8), :], out_sems.at[3]),
     ]
-    for extra in extras:
-        extra.start()
+    for copy in scalars + extras:
+        copy.start()
+    for copy in scalars:
+        copy.wait()
 
     def one(e):
         blocks = []
@@ -80,18 +95,15 @@
                     weight = jnp.where(place[face] == band, jnp.float32(1), jnp.float32(0))
                     term = blocks[face + 1] * weight
                     total = term if total is None else total + term
-            made[rows, :] = total
+            out_ref[rows, :] = total
 
     def some(chunk, carry):
         arriving(chunk).wait()
         for k in range(CHUNK):
             one(chunk * CHUNK + k)
-        leaving(chunk).start()
         return carry
 
     lax.fori_loop(0, chunks, some, 0)
-    for chunk in range(chunks):
-        leaving(chunk).wait()
     for extra in extras:
         extra.wait()
 
@@ -114,11 +126,10 @@
 
 def basis_kernel(
     elems, steps,
-    below_ref, own_ref, above_ref, far_low_ref, far_high_ref, shifts_ref,
+    inner_ref, own_ref, outer_ref, far_low_ref, far_high_ref, shifts_ref,
     basis_ref, gram_ref,
     vecs,
 ):
-    refs = (below_ref, own_ref, above_ref)
     level = 3 * elems + 2 * PAD
     given = (steps + 2) * level
     lane = lane_ids(8)
@@ -138,80 +149,92 @@
         vecs[pl.ds(at, 8, stride=2), :] = jnp.where(left, packed, turned)
         vecs[pl.ds(at + 1, 8, stride=2), :] = jnp.where(left, turned, packed)
 
-    for part, ref in enumerate(refs):
-        tail = elems * ROWS
-        spread(PAD + part * elems, ref[pl.ds(tail, 8), :])
-        spread(given + PAD + part * elems, ref[pl.ds(tail + 8, 8), :])
     for ref, at in ((far_low_ref, PAD - 2), (far_high_ref, PAD + 3 * elems)):
         packed = jnp.broadcast_to(ref[...], (8, LANES))
         turned = pltpu.roll(packed, WIDTH, 1)
         vecs[pl.ds(at, 1), :] = jnp.where(left, packed, turned)[:1]
         vecs[pl.ds(at + 1, 1), :] = jnp.where(left, turned, packed)[:1]
 
-    def times(part, first, at):
-        near = [vecs[pl.ds(at + (k - REACH), 1), :] for k in range(8 + 2 * REACH)]
-        terms = []
-        for k in range(8):
-            total = None
-            for band in range(BANDS):
-                rows = pl.ds((first + k) * ROWS + band * HALF, HALF)
-                term = refs[part][rows, :] * near[k + band]
-                total = term if total is None else total + term
-            top = jnp.sum(jnp.where(left_half, total, 0.0), axis=1, keepdims=True)
-            low = jnp.sum(jnp.where(left_half, 0.0, total), axis=1, keepdims=True)
-            placed = jnp.where(pick_top, top, jnp.where(pick_low, low, 0.0))
-            terms.append(jnp.sum(placed.reshape(HALF // 8, 8, LANES), axis=0))
-        return stacked_sums(terms, row)
-
-    def apply(index, groups):
-        at = pl.multiple_of(index * level + PAD, 8)
-        if isinstance(index, int):
-            opening = index == 0
-            source = given + PAD if opening else at
-            sign, scale = (-1.0, 1.0) if opening else (1.0, -shifts_ref[index - 1])
-        else:
-            opening = index == 0
-            source = pl.multiple_of(jnp.where(opening, given + PAD, at), 8)
-            sign = jnp.where(opening, jnp.float32(-1), jnp.float32(1))
-            scale = jnp.where(opening, jnp.float32(1), -shifts_ref[jnp.maximum(index - 1, 0)])
-        made = []
-        for part, first in groups:
-            place = part * elems + first
-            fresh = times(part, first, at + place)
-            made.append((place, sign * fresh + scale * vecs[pl.ds(source + place, 8), :]))
-        for place, value in made:
-            vecs[pl.ds(at + level + place, 8), :] = value
-
-    own = [(1, first) for first in range(0, elems, 8)]
-    groups = [(part, first) for part in (0, 2) for first in range(0, elems, 8)]
-    done = 0
-    while done <= steps:
-        reach = REACH * (steps - done)
-        wanted = [
-            (part, first)
-            for part, first in groups
-            if (elems - first - 8 < reach if part == 0 else first < reach)
-        ]
-        until = done
-        while until <= steps:
-            later = REACH * (steps - until)
-            if wanted != [
+    def fill(refs):
+        tail = elems * ROWS
+        for part, ref in enumerate(refs):
+            spread(PAD + part * elems, ref[pl.ds(tail, 8), :])
+            spread(given + PAD + part * elems, ref[pl.ds(tail + 8, 8), :])
+
+        def times(part, first, at):
+            near = [vecs[pl.ds(at + (k - REACH), 1), :] for k in range(8 + 2 * REACH)]
+            terms = []
+            for k in range(8):
+                total = None
+                for band in range(BANDS):
+                    rows = pl.ds((first + k) * ROWS + band * HALF, HALF)
+                    term = refs[part][rows, :] * near[k + band]
+                    total = term if total is None else total + term
+                top = jnp.sum(jnp.where(left_half, total, 0.0), axis=1, keepdims=True)
+                low = jnp.sum(jnp.where(left_half, 0.0, total), axis=1, keepdims=True)
+                placed = jnp.where(pick_top, top, jnp.where(pick_low, low, 0.0))
+                terms.append(jnp.sum(placed.reshape(HALF // 8, 8, LANES), axis=0))
+            return stacked_sums(terms, row)
+
+        def apply(index, groups):
+            at = pl.multiple_of(index * level + PAD, 8)
+            if isinstance(index, int):
+                opening = index == 0
+                source = given + PAD if opening else at
+                sign, scale = (-1.0, 1.0) if opening else (1.0, -shifts_ref[index - 1])
+            else:
+                opening = index == 0
+                source = pl.multiple_of(jnp.where(opening, given + PAD, at), 8)
+                sign = jnp.where(opening, jnp.float32(-1), jnp.float32(1))
+                scale = jnp.where(opening, jnp.float32(1), -shifts_ref[jnp.maximum(index - 1, 0)])
+            made = []
+            for part, first in groups:
+                place = part * elems + first
+                fresh = times(part, first, at + place)
+                made.append((place, sign * fresh + scale * vecs[pl.ds(source + place, 8), :]))
+            for place, value in made:
+                vecs[pl.ds(at + level + place, 8), :] = value
+
+        own = [(1, first) for first in range(0, elems, 8)]
+        groups = [(part, first) for part in (0, 2) for first in range(0, elems, 8)]
+        done = 0
+        while done <= steps:
+            reach = REACH * (steps - done)
+            wanted = [
                 (part, first)
                 for part, first in groups
-                if (elems - first - 8 < later if part == 0 else first < later)
-            ]:
-                break
-            until += 1
-
-        def turn(index, carry, wanted=wanted):
-            apply(index, wanted + own)
-            return carry
-
-        if until - done == 1:
-            apply(done, wanted + own)
-        else:
-            lax.fori_loop(done, until, turn, 0)
-        done = until
+                if (elems - first - 8 < reach if part == 0 else first < reach)
+            ]
+            until = done
+            while until <= steps:
+                later = REACH * (steps - until)
+                if wanted != [
+                    (part, first)
+                    for part, first in groups
+                    if (elems - first - 8 < later if part == 0 else first < later)
+                ]:
+                    break
+                until += 1
+
+            def turn(index, carry, wanted=wanted):
+                apply(index, wanted + own)
+                return carry
+
+            if until - done == 1:
+                apply(done, wanted + own)
+            else:
+                lax.fori_loop(done, until, turn, 0)
+            done = until
+
+    second = lax.axis_index(AXES) % 2 == 1
+
+    @pl.when(second)
+    def _():
+        fill((inner_ref, own_ref, outer_ref))
+
+    @pl.when(jnp.logical_not(second))
+    def _():
+        fill((outer_ref, own_ref, inner_ref))
 
     rows = []
     for k in range(steps + 1):
@@ -226,7 +249,8 @@
             entry = jnp.sum(rows[i] * rows[j], axis=1, keepdims=True)
             total = jnp.where(lane == number, entry, total)
             number += 1
-    gram_ref[...] = jnp.sum(total, axis=0, keepdims=True)
+    gram = jnp.sum(total, axis=0, keepdims=True)
+    gram_ref[...] = jnp.broadcast_to(gram, gram_ref.shape)
 
 
 def inverse_root(value):
@@ -308,37 +332,39 @@
 
     x = start.reshape(packed, LANES)
     b = rhs.reshape(packed, LANES)
+    sources = (operator, adjacency.T, counts, x, b)
     own = pl.pallas_call(
         band_kernel,
-        out_shape=jax.ShapeDtypeStruct((block, LANES), f32),
-        in_specs=[hbm, smem, smem, hbm, hbm],
-        out_specs=hbm,
+        out_shape=pltpu.VMEM((block, LANES), f32),
+        in_specs=[hbm] * 5,
+        out_specs=vmem,
         scratch_shapes=[
             pltpu.VMEM(operator.shape, f32),
-            pltpu.VMEM((elems * ROWS, LANES), f32),
+            pltpu.SMEM(adjacency.T.shape, jnp.int32),
+            pltpu.SMEM(counts.shape, jnp.int32),
             pltpu.SemaphoreType.DMA((elems // CHUNK,)),
-            pltpu.SemaphoreType.DMA((elems // CHUNK + 2,)),
+            pltpu.SemaphoreType.DMA((4,)),
         ],
-        compiler_params=pltpu.CompilerParams(vmem_limit_bytes=60 * mebi),
+        compiler_params=pltpu.CompilerParams(vmem_limit_bytes=16 * mebi),
         name="bands",
-    )(operator, adjacency.T, counts, x, b)
-    below = shifted(own, 1)
-    above = shifted(own, -1)
+    )(*(pltpu.with_memory_space_constraint(source, pltpu.HBM) for source in sources))
+    inner = within_chip(own)
+    outer = between_chips(own)
     far_low = shifted(x[packed - 1 :], 2)
     far_high = shifted(x[:1], -2)
     basis, gram = pl.pallas_call(
         functools.partial(basis_kernel, elems, steps),
         out_shape=(
             jax.ShapeDtypeStruct((8 * (steps + 1), LANES), f32),
-            jax.ShapeDtypeStruct((1, LANES), f32),
+            jax.ShapeDtypeStruct((devices, LANES), f32),
         ),
         in_specs=[vmem, vmem, vmem, vmem, vmem, smem],
         out_specs=(vmem, vmem),
         scratch_shapes=[pltpu.VMEM(((steps + 3) * (3 * elems + 2 * PAD), LANES), f32)],
         compiler_params=pltpu.CompilerParams(vmem_limit_bytes=16 * mebi),
         name="basis",
-    )(below, own, above, far_low, far_high, shifts)
-    gram = lax.psum(gram, AXES)
+    )(inner, own, outer, far_low, far_high, shifts)
+    parts = lax.all_to_all(gram, AXES, 0, 0, tiled=True)
     sol, res, upper = pl.pallas_call(
         functools.partial(finish_kernel, devices * elems * width, steps),
         out_shape=(
@@ -350,7 +376,7 @@
         out_specs=(vmem, vmem, vmem),
         compiler_params=pltpu.CompilerParams(vmem_limit_bytes=4 * mebi),
         name="finish",
-    )(gram, basis, x, shifts)
+    )(parts, basis, x, shifts)
     return (sol.reshape(-1), res.reshape(-1), upper)
 
 

time: 150 us -> 80.6 us (0.54)
  blocking collectives: 113 us -> 51.7 us
  waiting for transfers between devices: 9.62 us -> 5.02 us
    psum x1 -> x0, blocking collectives: 113 us -> none  [body(): gram = lax.psum(gram, AXES)]
    all_to_all x0 -> x1, blocking collectives: none -> 51.7 us  [body(): parts = lax.all_to_all(gram, AXES, 0, 0, tiled=True)]
    ppermute x4 -> x2, starting transfers between devices: 16 us -> 5.28 us  [shifted(): return lax.ppermute(array, AXES, pairs)]
    ppermute x0 -> x2, starting transfers between devices: none -> 9.53 us  [the longest x1 5.02 us: within_chip(): lax.ppermute(array, AXES, [(i, i + 1 - 2 * (i % 2)) for i in range(size)])]
    ppermute x4 -> x2, waiting for transfers between devices: 9.62 us -> 4.31 us  [shifted(): return lax.ppermute(array, AXES, pairs)]
    pallas_call x1, Pallas kernels: 3.5 us -> 1.93 us  [body(): pl.pallas_call(band_kernel, out_shape=pltpu.VMEM((block, LANES), f32), in...]
  transfers between devices with their start and end apart: 4 -> 4, of which waited for: 1 -> 2; matrix products, arithmetic and copies ran while one was open for 0% -> 0% of each run, Pallas kernels for 0% -> 0%
where the time goes in v3:
time: 80.6 us; the launch traced here: 80.3 us
  blocking collectives  51.7 us (64%)
  starting transfers between devices  14.8 us (18%)
  Pallas kernels  8.05 us (10%)
  waiting for transfers between devices  5.02 us (6%)
    all_to_all x1, blocking collectives, body(): parts = lax.all_to_all(gram, AXES, 0, 0, tiled=True)  51.7 us
    ppermute x2, starting transfers between devices, shifted(): return lax.ppermute(array, AXES, pairs)  5.28 us
    ppermute x1, starting transfers between devices, within_chip(): lax.ppermute(array, AXES, [(i, i + 1 - 2 * (i % 2)) for i in range(size)])  5.02 us
    pallas_call x1, Pallas kernels, body(): pl.pallas_call(functools.partial(basis_kernel, elems, steps), out_shape=(...  4.58 us
    ppermute x1, starting transfers between devices, between_chips(): return lax.ppermute(array, AXES, pairs)  4.51 us
    ppermute x2, waiting for transfers between devices, shifted(): return lax.ppermute(array, AXES, pairs)  4.31 us
    pallas_call x1, Pallas kernels, body(): pl.pallas_call(band_kernel, out_shape=pltpu.VMEM((block, LANES), f32), in...  1.93 us
  transfers between devices with their start and end apart: 4, of which 2 were waited for; matrix products, arithmetic and copies ran while one was open for 0% of the time, Pallas kernels for 0%

profile of v3, /device:TPU:1, one launch (start us, length us, event | category | flops | bytes accessed | tf_op | source)
XLA Modules:
  0.0 80.3 jit_solution(17891641637148018526)
XLA Ops:
  0.6 0.0 copy-start
  0.6 0.0 copy-start.1
  0.7 1.9 %bands.1.own_ref = f32[2576,128]{1,0:T(8,128)S(1)} custom-call(f32[16,64,448]{2,1,0:T(8,128)} %op_ref.1, s32[6,16]{1,0:T(8,128)} %bitcast.17, s32[16]{0:T(128)} %valid_ref.1, f32[8,128]{1,0:T(8,128)} %bitcast.15, f32[8,128]{1,0:T(8,128)} %bitcast.18), custom_call_target="tpu_custom_call" | custom-call | tf_op jit(solution)/shard_map/bands/pallas_call | solution.py:336
  2.6 4.5 %collective-permute-start.1 = (f32[2576,128]{1,0:T(8,128)S(1)}, f32[2576,128]{1,0:T(8,128)S(1)}, u32[]{:S(2)}, u32[]{:S(2)}) collective-permute-start(f32[2576,128]{1,0:T(8,128)S(1)} %bands.1.own_ref), channel_id=1, source_target_pairs={{1,2},{2,1},{3,4},{4,3},{5,6},{6,5},{7,8},{8,7},{9,10},{10,9},{11,... | collective-permute-start | bytes 3956744 | tf_op jit(solution)/shard_map/ppermute | solution.py:30
  7.1 5.0 %collective-permute-start = (f32[2576,128]{1,0:T(8,128)S(1)}, f32[2576,128]{1,0:T(8,128)S(1)}, u32[]{:S(2)}, u32[]{:S(2)}) collective-permute-start(f32[2576,128]{1,0:T(8,128)S(1)} %bands.1.own_ref), channel_id=1, source_target_pairs={{0,1},{1,0},{2,3},{3,2},{4,5},{5,4},{6,7},{7,6},{8,9},{9,8},{10,11... | collective-permute-start | bytes 3956744 | tf_op jit(solution)/shard_map/ppermute | solution.py:35
  12.1 0.0 copy-done
  12.2 1.3 %collective-permute-start.3 = (f32[1,128]{1,0:T(1,128)S(1)}, f32[1,128]{1,0:T(1,128)S(1)}, u32[]{:S(2)}, u32[]{:S(2)}) collective-permute-start(f32[1,128]{1,0:T(1,128)S(1)} %get-tuple-element.13), channel_id=1, source_target_pairs={{2,0},{3,1},{4,2},{5,3},{6,4},{7,5},{8,6},{9,7},{10,8},{11,9},{12,... | collective-permute-start | bytes 1544 | tf_op jit(solution)/shard_map/ppermute | solution.py:24
  13.5 4.0 %collective-permute-start.2 = (f32[1,128]{1,0:T(1,128)S(1)}, f32[1,128]{1,0:T(1,128)S(1)}, u32[]{:S(2)}, u32[]{:S(2)}) collective-permute-start(f32[1,128]{1,0:T(1,128)S(1)} %get-tuple-element.14), channel_id=1, source_target_pairs={{0,2},{1,3},{2,4},{3,5},{4,6},{5,7},{6,8},{7,9},{8,10},{9,11},{10,... | collective-permute-start | bytes 1544 | tf_op jit(solution)/shard_map/ppermute | solution.py:24
  17.4 0.0 collective-permute-done.3.far_high_ref
  17.5 4.3 %collective-permute-done.2.far_low_ref = f32[1,128]{1,0:T(1,128)S(1)} collective-permute-done((f32[1,128]{1,0:T(1,128)S(1)}, f32[1,128]{1,0:T(1,128)S(1)}, u32[]{:S(2)}, u32[]{:S(2)}) %collective-permute-start.2) | collective-permute-done | bytes 544 | tf_op jit(solution)/shard_map/ppermute | solution.py:24
  21.8 0.7 collective-permute-done.1.outer_ref
  22.5 0.0 collective-permute-done.inner_ref
  22.5 0.0 copy-done.1
  22.5 4.6 %basis.1 = (f32[72,128]{1,0:T(8,128)S(1)}, f32[512,128]{1,0:T(8,128)S(1)}) custom-call(f32[2576,128]{1,0:T(8,128)S(1)} %collective-permute-done.inner_ref, f32[2576,128]{1,0:T(8,128)S(1)} %bands.1.own_ref, f32[2576,128]{1,0:T(8,128)S(1)} %collective-permute-done.1.outer_ref, f32[1,128]{1,0:T(1,128)S(1)} %collective-permute-done.2.far_low_ref, ...), custom_call_target="tpu_custom_call" | custom-call | tf_op jit(solution)/shard_map/basis/pallas_call | solution.py:355
  27.1 51.7 %all_to_all.11 = f32[512,1,128]{2,1,0:T(1,128)S(1)} all-to-all(f32[512,1,128]{2,1,0:T(1,128)S(1)} %bitcast.14), channel_id=1, replica_groups=mesh['group'=16,'slab'=32] {'group','slab'}, dimensions={0} | all-to-all | bytes 524288 | tf_op jit(solution)/shard_map/all_to_all | solution.py:367
  78.8 1.5 %finish.1 = (f32[8,128]{1,0:T(8,128)}, f32[8,128]{1,0:T(8,128)}, f32[9,9]{1,0:T(8,128)}) custom-call(f32[512,128]{1,0:T(8,128)S(1)} %bitcast.13, f32[72,128]{1,0:T(8,128)S(1)} %get-tuple-element.9.basis_ref, f32[8,128]{1,0:T(8,128)S(1)} %bitcast.16, f32[8]{0:T(128)S(1)} %copy-done.1), custom_call_target="tpu_custom_call" | custom-call | tf_op jit(solution)/shard_map/finish/pallas_call | solution.py:368
  (1 shorter events, 0.0 us)
Async XLA Ops:
  0.6 11.5 %copy-start = (f32[1024]{0:T(1024)S(1)}, f32[1024]{0:T(1024)}, u32[]{:S(2)}) copy-start(f32[1024]{0:T(1024)} %param.10) | copy-start | bytes 12292
  0.6 21.8 %copy-start.1 = (f32[8]{0:T(128)S(1)}, f32[8]{0:T(128)}, u32[]{:S(2)}) copy-start(f32[8]{0:T(128)} %shifts_ref.3) | copy-start | bytes 100
  2.6 19.9 %collective-permute-start.1 = (f32[2576,128]{1,0:T(8,128)S(1)}, f32[2576,128]{1,0:T(8,128)S(1)}, u32[]{:S(2)}, u32[]{:S(2)}) collective-permute-start(f32[2576,128]{1,0:T(8,128)S(1)} %bands.1.own_ref), channel_id=1, source_target_pairs={{1,2},{2,1},{3,4},{4,3},{5,6},{6,5},{7,8},{8,7},{9,10},{10,9},{11,... | collective-permute-start | bytes 3956744 | tf_op jit(solution)/shard_map/ppermute | solution.py:30
  7.1 15.4 %collective-permute-start = (f32[2576,128]{1,0:T(8,128)S(1)}, f32[2576,128]{1,0:T(8,128)S(1)}, u32[]{:S(2)}, u32[]{:S(2)}) collective-permute-start(f32[2576,128]{1,0:T(8,128)S(1)} %bands.1.own_ref), channel_id=1, source_target_pairs={{0,1},{1,0},{2,3},{3,2},{4,5},{5,4},{6,7},{7,6},{8,9},{9,8},{10,11... | collective-permute-start | bytes 3956744 | tf_op jit(solution)/shard_map/ppermute | solution.py:35
  12.2 5.3 %collective-permute-start.3 = (f32[1,128]{1,0:T(1,128)S(1)}, f32[1,128]{1,0:T(1,128)S(1)}, u32[]{:S(2)}, u32[]{:S(2)}) collective-permute-start(f32[1,128]{1,0:T(1,128)S(1)} %get-tuple-element.13), channel_id=1, source_target_pairs={{2,0},{3,1},{4,2},{5,3},{6,4},{7,5},{8,6},{9,7},{10,8},{11,9},{12,... | collective-permute-start | bytes 1544 | tf_op jit(solution)/shard_map/ppermute | solution.py:24
  13.5 8.3 %collective-permute-start.2 = (f32[1,128]{1,0:T(1,128)S(1)}, f32[1,128]{1,0:T(1,128)S(1)}, u32[]{:S(2)}, u32[]{:S(2)}) collective-permute-start(f32[1,128]{1,0:T(1,128)S(1)} %get-tuple-element.14), channel_id=1, source_target_pairs={{0,2},{1,3},{2,4},{3,5},{4,6},{5,7},{6,8},{7,9},{8,10},{9,11},{10,... | collective-permute-start | bytes 1544 | tf_op jit(solution)/shard_map/ppermute | solution.py:24

commit v4 on v3

--- a/solution.py
+++ b/solution.py
@@ -251,6 +251,11 @@
             number += 1
     gram = jnp.sum(total, axis=0, keepdims=True)
     gram_ref[...] = jnp.broadcast_to(gram, gram_ref.shape)
+
+
+def partial_kernel(parts_ref, out_ref):
+    total = jnp.sum(parts_ref[...], axis=0, keepdims=True)
+    out_ref[...] = jnp.broadcast_to(total, out_ref.shape)
 
 
 def inverse_root(value):
@@ -322,6 +327,8 @@
     elems, width, columns = operator.shape
     steps = shifts.shape[0]
     devices = lax.axis_size(AXES)
+    slabs = lax.axis_size("slab")
+    groups = lax.axis_size("group")
     packed = elems * width // LANES
     block = elems * ROWS + 2 * packed
     vmem = pl.BlockSpec(memory_space=pltpu.VMEM)
@@ -356,7 +363,7 @@
         functools.partial(basis_kernel, elems, steps),
         out_shape=(
             jax.ShapeDtypeStruct((8 * (steps + 1), LANES), f32),
-            jax.ShapeDtypeStruct((devices, LANES), f32),
+            jax.ShapeDtypeStruct((slabs, LANES), f32),
         ),
         in_specs=[vmem, vmem, vmem, vmem, vmem, smem],
         out_specs=(vmem, vmem),
@@ -364,7 +371,16 @@
         compiler_params=pltpu.CompilerParams(vmem_limit_bytes=16 * mebi),
         name="basis",
     )(inner, own, outer, far_low, far_high, shifts)
-    parts = lax.all_to_all(gram, AXES, 0, 0, tiled=True)
+    parts = lax.all_to_all(gram, "slab", 0, 0, tiled=True)
+    parts = pl.pallas_call(
+        partial_kernel,
+        out_shape=jax.ShapeDtypeStruct((groups, LANES), f32),
+        in_specs=[vmem],
+        out_specs=vmem,
+        compiler_params=pltpu.CompilerParams(vmem_limit_bytes=4 * mebi),
+        name="partial",
+    )(parts)
+    parts = lax.all_to_all(parts, "group", 0, 0, tiled=True)
     sol, res, upper = pl.pallas_call(
         functools.partial(finish_kernel, devices * elems * width, steps),
         out_shape=(

time: 80.6 us -> 73.1 us (0.907)
  blocking collectives: 51.7 us -> 44.3 us
    all_to_all x1 -> x2, blocking collectives: 51.7 us -> 44.3 us  [the longest x1 26 us: body(): parts = lax.all_to_all(parts, 'group', 0, 0, tiled=True)]
where the time goes in v4:
time: 73.1 us; the launch traced here: 72.8 us
  blocking collectives  44.3 us (61%)
  starting transfers between devices  14.8 us (20%)
  Pallas kernels  7.97 us (11%)
  waiting for transfers between devices  5.02 us (7%)
    all_to_all x1, blocking collectives, body(): parts = lax.all_to_all(parts, 'group', 0, 0, tiled=True)  26 us
    all_to_all x1, blocking collectives, body(): parts = lax.all_to_all(gram, 'slab', 0, 0, tiled=True)  18.2 us
    ppermute x2, starting transfers between devices, shifted(): return lax.ppermute(array, AXES, pairs)  5.28 us
    ppermute x1, starting transfers between devices, within_chip(): lax.ppermute(array, AXES, [(i, i + 1 - 2 * (i % 2)) for i in range(size)])  5.02 us
    pallas_call x1, Pallas kernels, body(): pl.pallas_call(functools.partial(basis_kernel, elems, steps), out_shape=(...  4.56 us
    ppermute x1, starting transfers between devices, between_chips(): return lax.ppermute(array, AXES, pairs)  4.51 us
    ppermute x2, waiting for transfers between devices, shifted(): return lax.ppermute(array, AXES, pairs)  4.31 us
    pallas_call x1, Pallas kernels, body(): pl.pallas_call(band_kernel, out_shape=pltpu.VMEM((block, LANES), f32), in...  1.93 us
  transfers between devices with their start and end apart: 4, of which 2 were waited for; matrix products, arithmetic and copies ran while one was open for 0% of the time, Pallas kernels for 0%

profile of v4, /device:TPU:1, one launch (start us, length us, event | category | flops | bytes accessed | tf_op | source)
XLA Modules:
  0.0 72.8 jit_solution(3561456197093973449)
XLA Ops:
  0.6 0.0 copy-start
  0.6 0.0 copy-start.1
  0.7 1.9 %bands.1.own_ref = f32[2576,128]{1,0:T(8,128)S(1)} custom-call(f32[16,64,448]{2,1,0:T(8,128)} %op_ref.1, s32[6,16]{1,0:T(8,128)} %bitcast.23, s32[16]{0:T(128)} %valid_ref.1, f32[8,128]{1,0:T(8,128)} %bitcast.20, f32[8,128]{1,0:T(8,128)} %bitcast.24), custom_call_target="tpu_custom_call" | custom-call | tf_op jit(solution)/shard_map/bands/pallas_call | solution.py:343
  2.6 4.5 %collective-permute-start.1 = (f32[2576,128]{1,0:T(8,128)S(1)}, f32[2576,128]{1,0:T(8,128)S(1)}, u32[]{:S(2)}, u32[]{:S(2)}) collective-permute-start(f32[2576,128]{1,0:T(8,128)S(1)} %bands.1.own_ref), channel_id=1, source_target_pairs={{1,2},{2,1},{3,4},{4,3},{5,6},{6,5},{7,8},{8,7},{9,10},{10,9},{11,... | collective-permute-start | bytes 3956744 | tf_op jit(solution)/shard_map/ppermute | solution.py:30
  7.1 5.0 %collective-permute-start = (f32[2576,128]{1,0:T(8,128)S(1)}, f32[2576,128]{1,0:T(8,128)S(1)}, u32[]{:S(2)}, u32[]{:S(2)}) collective-permute-start(f32[2576,128]{1,0:T(8,128)S(1)} %bands.1.own_ref), channel_id=1, source_target_pairs={{0,1},{1,0},{2,3},{3,2},{4,5},{5,4},{6,7},{7,6},{8,9},{9,8},{10,11... | collective-permute-start | bytes 3956744 | tf_op jit(solution)/shard_map/ppermute | solution.py:35
  12.1 0.0 copy-done
  12.2 1.3 %collective-permute-start.3 = (f32[1,128]{1,0:T(1,128)S(1)}, f32[1,128]{1,0:T(1,128)S(1)}, u32[]{:S(2)}, u32[]{:S(2)}) collective-permute-start(f32[1,128]{1,0:T(1,128)S(1)} %get-tuple-element.13), channel_id=1, source_target_pairs={{2,0},{3,1},{4,2},{5,3},{6,4},{7,5},{8,6},{9,7},{10,8},{11,9},{12,... | collective-permute-start | bytes 1544 | tf_op jit(solution)/shard_map/ppermute | solution.py:24
  13.5 4.0 %collective-permute-start.2 = (f32[1,128]{1,0:T(1,128)S(1)}, f32[1,128]{1,0:T(1,128)S(1)}, u32[]{:S(2)}, u32[]{:S(2)}) collective-permute-start(f32[1,128]{1,0:T(1,128)S(1)} %get-tuple-element.14), channel_id=1, source_target_pairs={{0,2},{1,3},{2,4},{3,5},{4,6},{5,7},{6,8},{7,9},{8,10},{9,11},{10,... | collective-permute-start | bytes 1544 | tf_op jit(solution)/shard_map/ppermute | solution.py:24
  17.4 0.0 collective-permute-done.3.far_high_ref
  17.5 4.3 %collective-permute-done.2.far_low_ref = f32[1,128]{1,0:T(1,128)S(1)} collective-permute-done((f32[1,128]{1,0:T(1,128)S(1)}, f32[1,128]{1,0:T(1,128)S(1)}, u32[]{:S(2)}, u32[]{:S(2)}) %collective-permute-start.2) | collective-permute-done | bytes 544 | tf_op jit(solution)/shard_map/ppermute | solution.py:24
  21.8 0.7 collective-permute-done.1.outer_ref
  22.5 0.0 collective-permute-done.inner_ref
  22.5 0.0 copy-done.1
  22.5 4.6 %basis.1 = (f32[72,128]{1,0:T(8,128)S(1)}, f32[32,128]{1,0:T(8,128)S(1)}) custom-call(f32[2576,128]{1,0:T(8,128)S(1)} %collective-permute-done.inner_ref, f32[2576,128]{1,0:T(8,128)S(1)} %bands.1.own_ref, f32[2576,128]{1,0:T(8,128)S(1)} %collective-permute-done.1.outer_ref, f32[1,128]{1,0:T(1,128)S(1)} %collective-permute-done.2.far_low_ref, ...), custom_call_target="tpu_custom_call" | custom-call | tf_op jit(solution)/shard_map/basis/pallas_call | solution.py:362
  27.0 18.2 %all_to_all.22 = f32[32,1,128]{2,1,0:T(1,128)S(1)} all-to-all(f32[32,1,128]{2,1,0:T(1,128)S(1)} %bitcast.22), channel_id=1, replica_groups=mesh['group'=16,'slab'=32] {'slab'}, dimensions={0} | all-to-all | bytes 32768 | tf_op jit(solution)/shard_map/all_to_all | solution.py:374
  45.3 26.0 %all_to_all.23 = f32[16,1,128]{2,1,0:T(1,128)S(1)} all-to-all(f32[16,1,128]{2,1,0:T(1,128)S(1)} %bitcast.19), channel_id=1, replica_groups=mesh['group'=16,'slab'=32] {'group'}, dimensions={0} | all-to-all | bytes 16384 | tf_op jit(solution)/shard_map/all_to_all | solution.py:383
  71.3 1.5 %finish.1 = (f32[8,128]{1,0:T(8,128)}, f32[8,128]{1,0:T(8,128)}, f32[9,9]{1,0:T(8,128)}) custom-call(f32[16,128]{1,0:T(8,128)S(1)} %bitcast.18, f32[72,128]{1,0:T(8,128)S(1)} %get-tuple-element.9.basis_ref, f32[8,128]{1,0:T(8,128)S(1)} %bitcast.21, f32[8]{0:T(128)S(1)} %copy-done.1), custom_call_target="tpu_custom_call" | custom-call | tf_op jit(solution)/shard_map/finish/pallas_call | solution.py:384
  (2 shorter events, 0.0 us)
Async XLA Ops:
  0.6 11.5 %copy-start = (f32[1024]{0:T(1024)S(1)}, f32[1024]{0:T(1024)}, u32[]{:S(2)}) copy-start(f32[1024]{0:T(1024)} %param.10) | copy-start | bytes 12292
  0.6 21.8 %copy-start.1 = (f32[8]{0:T(128)S(1)}, f32[8]{0:T(128)}, u32[]{:S(2)}) copy-start(f32[8]{0:T(128)} %shifts_ref.3) | copy-start | bytes 100
  2.6 19.9 %collective-permute-start.1 = (f32[2576,128]{1,0:T(8,128)S(1)}, f32[2576,128]{1,0:T(8,128)S(1)}, u32[]{:S(2)}, u32[]{:S(2)}) collective-permute-start(f32[2576,128]{1,0:T(8,128)S(1)} %bands.1.own_ref), channel_id=1, source_target_pairs={{1,2},{2,1},{3,4},{4,3},{5,6},{6,5},{7,8},{8,7},{9,10},{10,9},{11,... | collective-permute-start | bytes 3956744 | tf_op jit(solution)/shard_map/ppermute | solution.py:30
  7.1 15.4 %collective-permute-start = (f32[2576,128]{1,0:T(8,128)S(1)}, f32[2576,128]{1,0:T(8,128)S(1)}, u32[]{:S(2)}, u32[]{:S(2)}) collective-permute-start(f32[2576,128]{1,0:T(8,128)S(1)} %bands.1.own_ref), channel_id=1, source_target_pairs={{0,1},{1,0},{2,3},{3,2},{4,5},{5,4},{6,7},{7,6},{8,9},{9,8},{10,11... | collective-permute-start | bytes 3956744 | tf_op jit(solution)/shard_map/ppermute | solution.py:35
  12.2 5.3 %collective-permute-start.3 = (f32[1,128]{1,0:T(1,128)S(1)}, f32[1,128]{1,0:T(1,128)S(1)}, u32[]{:S(2)}, u32[]{:S(2)}) collective-permute-start(f32[1,128]{1,0:T(1,128)S(1)} %get-tuple-element.13), channel_id=1, source_target_pairs={{2,0},{3,1},{4,2},{5,3},{6,4},{7,5},{8,6},{9,7},{10,8},{11,9},{12,... | collective-permute-start | bytes 1544 | tf_op jit(solution)/shard_map/ppermute | solution.py:24
  13.5 8.3 %collective-permute-start.2 = (f32[1,128]{1,0:T(1,128)S(1)}, f32[1,128]{1,0:T(1,128)S(1)}, u32[]{:S(2)}, u32[]{:S(2)}) collective-permute-start(f32[1,128]{1,0:T(1,128)S(1)} %get-tuple-element.14), channel_id=1, source_target_pairs={{0,2},{1,3},{2,4},{3,5},{4,6},{5,7},{6,8},{7,9},{8,10},{9,11},{10,... | collective-permute-start | bytes 1544 | tf_op jit(solution)/shard_map/ppermute | solution.py:24

commit v5 on v3

--- a/solution.py
+++ b/solution.py
@@ -249,8 +249,7 @@
             entry = jnp.sum(rows[i] * rows[j], axis=1, keepdims=True)
             total = jnp.where(lane == number, entry, total)
             number += 1
-    gram = jnp.sum(total, axis=0, keepdims=True)
-    gram_ref[...] = jnp.broadcast_to(gram, gram_ref.shape)
+    gram_ref[...] = jnp.sum(total, axis=0, keepdims=True)
 
 
 def inverse_root(value):
@@ -356,7 +355,7 @@
         functools.partial(basis_kernel, elems, steps),
         out_shape=(
             jax.ShapeDtypeStruct((8 * (steps + 1), LANES), f32),
-            jax.ShapeDtypeStruct((devices, LANES), f32),
+            jax.ShapeDtypeStruct((1, LANES), f32),
         ),
         in_specs=[vmem, vmem, vmem, vmem, vmem, smem],
         out_specs=(vmem, vmem),
@@ -364,7 +363,7 @@
         compiler_params=pltpu.CompilerParams(vmem_limit_bytes=16 * mebi),
         name="basis",
     )(inner, own, outer, far_low, far_high, shifts)
-    parts = lax.all_to_all(gram, AXES, 0, 0, tiled=True)
+    parts = lax.all_gather(gram, AXES, axis=0, tiled=True)
     sol, res, upper = pl.pallas_call(
         functools.partial(finish_kernel, devices * elems * width, steps),
         out_shape=(

time: 80.6 us -> 145 us (1.80)
  blocking collectives: 51.7 us -> 117 us
    all_gather x0 -> x1, blocking collectives: none -> 117 us  [body(): parts = lax.all_gather(gram, AXES, axis=0, tiled=True)]
    all_to_all x1 -> x0, blocking collectives: 51.7 us -> none  [body(): parts = lax.all_to_all(gram, AXES, 0, 0, tiled=True)]
where the time goes in v5:
time: 145 us
  blocking collectives  117 us (81%)
  starting transfers between devices  14.8 us (10%)
  Pallas kernels  8.03 us (6%)
  waiting for transfers between devices  5.02 us (3%)
    all_gather x1, blocking collectives, body(): parts = lax.all_gather(gram, AXES, axis=0, tiled=True)  117 us
    ppermute x2, starting transfers between devices, shifted(): return lax.ppermute(array, AXES, pairs)  5.28 us
    ppermute x1, starting transfers between devices, within_chip(): lax.ppermute(array, AXES, [(i, i + 1 - 2 * (i % 2)) for i in range(size)])  5.02 us
    pallas_call x1, Pallas kernels, body(): pl.pallas_call(functools.partial(basis_kernel, elems, steps), out_shape=(...  4.56 us
    ppermute x1, starting transfers between devices, between_chips(): return lax.ppermute(array, AXES, pairs)  4.51 us
    ppermute x2, waiting for transfers between devices, shifted(): return lax.ppermute(array, AXES, pairs)  4.31 us
  transfers between devices with their start and end apart: 4, of which 2 were waited for; matrix products, arithmetic and copies ran while one was open for 0% of the time, Pallas kernels for 0%

profile of v5, /device:TPU:1, one launch (start us, length us, event | category | flops | bytes accessed | tf_op | source)
XLA Modules:
  0.0 145.1 jit_solution(14229475759771333466)
XLA Ops:
  0.6 0.0 copy-start
  0.6 0.0 copy-start.1
  0.7 1.9 %bands.1.own_ref = f32[2576,128]{1,0:T(8,128)S(1)} custom-call(f32[16,64,448]{2,1,0:T(8,128)} %op_ref.1, s32[6,16]{1,0:T(8,128)} %bitcast.15, s32[16]{0:T(128)} %valid_ref.1, f32[8,128]{1,0:T(8,128)} %bitcast.12, f32[8,128]{1,0:T(8,128)} %bitcast.16), custom_call_target="tpu_custom_call" | custom-call | tf_op jit(solution)/shard_map/bands/pallas_call | solution.py:335
  2.6 4.5 %collective-permute-start.1 = (f32[2576,128]{1,0:T(8,128)S(1)}, f32[2576,128]{1,0:T(8,128)S(1)}, u32[]{:S(2)}, u32[]{:S(2)}) collective-permute-start(f32[2576,128]{1,0:T(8,128)S(1)} %bands.1.own_ref), channel_id=1, source_target_pairs={{1,2},{2,1},{3,4},{4,3},{5,6},{6,5},{7,8},{8,7},{9,10},{10,9},{11,... | collective-permute-start | bytes 3956744 | tf_op jit(solution)/shard_map/ppermute | solution.py:30
  7.1 5.0 %collective-permute-start = (f32[2576,128]{1,0:T(8,128)S(1)}, f32[2576,128]{1,0:T(8,128)S(1)}, u32[]{:S(2)}, u32[]{:S(2)}) collective-permute-start(f32[2576,128]{1,0:T(8,128)S(1)} %bands.1.own_ref), channel_id=1, source_target_pairs={{0,1},{1,0},{2,3},{3,2},{4,5},{5,4},{6,7},{7,6},{8,9},{9,8},{10,11... | collective-permute-start | bytes 3956744 | tf_op jit(solution)/shard_map/ppermute | solution.py:35
  12.1 0.0 copy-done
  12.2 1.3 collective-permute-start.3
  13.5 4.0 %collective-permute-start.2 = (f32[1,128]{1,0:T(1,128)S(1)}, f32[1,128]{1,0:T(1,128)S(1)}, u32[]{:S(2)}, u32[]{:S(2)}) collective-permute-start(f32[1,128]{1,0:T(1,128)S(1)} %get-tuple-element.14), channel_id=1, source_target_pairs={{0,2},{1,3},{2,4},{3,5},{4,6},{5,7},{6,8},{7,9},{8,10},{9,11},{10,... | collective-permute-start | bytes 1544 | tf_op jit(solution)/shard_map/ppermute | solution.py:24
  17.4 0.0 collective-permute-done.3.far_high_ref
  17.5 4.3 %collective-permute-done.2.far_low_ref = f32[1,128]{1,0:T(1,128)S(1)} collective-permute-done((f32[1,128]{1,0:T(1,128)S(1)}, f32[1,128]{1,0:T(1,128)S(1)}, u32[]{:S(2)}, u32[]{:S(2)}) %collective-permute-start.2) | collective-permute-done | bytes 544 | tf_op jit(solution)/shard_map/ppermute | solution.py:24
  21.8 0.7 collective-permute-done.1.outer_ref
  22.5 0.0 collective-permute-done.inner_ref
  22.5 0.0 copy-done.1
  22.5 4.6 %basis.1 = (f32[72,128]{1,0:T(8,128)S(1)}, f32[1,128]{1,0:T(1,128)S(1)}) custom-call(f32[2576,128]{1,0:T(8,128)S(1)} %collective-permute-done.inner_ref, f32[2576,128]{1,0:T(8,128)S(1)} %bands.1.own_ref, f32[2576,128]{1,0:T(8,128)S(1)} %collective-permute-done.1.outer_ref, f32[1,128]{1,0:T(1,128)S(1)} %collective-permute-done.2.far_low_ref, ...), custom_call_target="tpu_custom_call" | custom-call | tf_op jit(solution)/shard_map/basis/pallas_call | solution.py:354
  27.0 116.6 %all-gather = f32[512,1,128]{2,1,0:T(1,128)S(1)} all-gather(f32[1,1,128]{2,1,0:T(1,128)S(1)} %bitcast.14), channel_id=1, replica_groups=mesh['group'=16,'slab'=32] {'group','slab'}, dimensions={0}, use_global_device_ids=true | all-gather | bytes 262656 | tf_op jit(solution)/shard_map/all_gather | solution.py:366
  143.6 1.5 %finish.1 = (f32[8,128]{1,0:T(8,128)}, f32[8,128]{1,0:T(8,128)}, f32[9,9]{1,0:T(8,128)}) custom-call(f32[512,128]{1,0:T(8,128)S(1)} %bitcast.11, f32[72,128]{1,0:T(8,128)S(1)} %get-tuple-element.9.basis_ref, f32[8,128]{1,0:T(8,128)S(1)} %bitcast.13, f32[8]{0:T(128)S(1)} %copy-done.1), custom_call_target="tpu_custom_call" | custom-call | tf_op jit(solution)/shard_map/finish/pallas_call | solution.py:367
  (1 shorter events, 0.0 us)
Async XLA Ops:
  0.6 11.5 %copy-start = (f32[1024]{0:T(1024)S(1)}, f32[1024]{0:T(1024)}, u32[]{:S(2)}) copy-start(f32[1024]{0:T(1024)} %param.10) | copy-start | bytes 12292
  0.6 21.8 %copy-start.1 = (f32[8]{0:T(128)S(1)}, f32[8]{0:T(128)}, u32[]{:S(2)}) copy-start(f32[8]{0:T(128)} %shifts_ref.3) | copy-start | bytes 100
  2.6 19.9 %collective-permute-start.1 = (f32[2576,128]{1,0:T(8,128)S(1)}, f32[2576,128]{1,0:T(8,128)S(1)}, u32[]{:S(2)}, u32[]{:S(2)}) collective-permute-start(f32[2576,128]{1,0:T(8,128)S(1)} %bands.1.own_ref), channel_id=1, source_target_pairs={{1,2},{2,1},{3,4},{4,3},{5,6},{6,5},{7,8},{8,7},{9,10},{10,9},{11,... | collective-permute-start | bytes 3956744 | tf_op jit(solution)/shard_map/ppermute | solution.py:30
  7.1 15.4 %collective-permute-start = (f32[2576,128]{1,0:T(8,128)S(1)}, f32[2576,128]{1,0:T(8,128)S(1)}, u32[]{:S(2)}, u32[]{:S(2)}) collective-permute-start(f32[2576,128]{1,0:T(8,128)S(1)} %bands.1.own_ref), channel_id=1, source_target_pairs={{0,1},{1,0},{2,3},{3,2},{4,5},{5,4},{6,7},{7,6},{8,9},{9,8},{10,11... | collective-permute-start | bytes 3956744 | tf_op jit(solution)/shard_map/ppermute | solution.py:35
  12.2 5.3 %collective-permute-start.3 = (f32[1,128]{1,0:T(1,128)S(1)}, f32[1,128]{1,0:T(1,128)S(1)}, u32[]{:S(2)}, u32[]{:S(2)}) collective-permute-start(f32[1,128]{1,0:T(1,128)S(1)} %get-tuple-element.13), channel_id=1, source_target_pairs={{2,0},{3,1},{4,2},{5,3},{6,4},{7,5},{8,6},{9,7},{10,8},{11,9},{12,... | collective-permute-start | bytes 1544 | tf_op jit(solution)/shard_map/ppermute | solution.py:24
  13.5 8.3 %collective-permute-start.2 = (f32[1,128]{1,0:T(1,128)S(1)}, f32[1,128]{1,0:T(1,128)S(1)}, u32[]{:S(2)}, u32[]{:S(2)}) collective-permute-start(f32[1,128]{1,0:T(1,128)S(1)} %get-tuple-element.14), channel_id=1, source_target_pairs={{0,2},{1,3},{2,4},{3,5},{4,6},{5,7},{6,8},{7,9},{8,10},{9,11},{10,... | collective-permute-start | bytes 1544 | tf_op jit(solution)/shard_map/ppermute | solution.py:24

commit v6 on v4

v6 whole, which is shorter than its diff:
```python
import functools

import jax
import jax.numpy as jnp
from jax import lax
from jax.experimental import pallas as pl
from jax.experimental.pallas import tpu as pltpu
from jax.sharding import PartitionSpec as P

AXES = ("group", "slab")
WIDTH = 64
LANES = 128
REACH = 2
BANDS = 2 * REACH + 1
HALF = WIDTH // 2
ROWS = BANDS * HALF
CHUNK = 4
GROUP = 8


def between_chips(array):
    size = lax.axis_size(AXES)
    pairs = [(i, i + 1 if i % 2 else i - 1) for i in range(1, size - 1)]
    return lax.ppermute(array, AXES, pairs)


def within_chip(array):
    size = lax.axis_size(AXES)
    return lax.ppermute(array, AXES, [(i, i + 1 - 2 * (i % 2)) for i in range(size)])


def lane_ids(rows):
    return lax.broadcasted_iota(jnp.int32, (rows, LANES), 1)


def band_kernel(
    op_ref, adjacency_ref, valid_ref, start_ref, rhs_ref, outer_ref, inner_ref,
    held, adj_ref, counts_ref, in_sems, other_sems,
):
    elems, _, columns = op_ref.shape
    faces = columns // WIDTH - 1
    chunks = elems // CHUNK
    device = lax.axis_index(AXES)
    base = device * elems
    second = device % 2
    left = lane_ids(HALF) < WIDTH
    tail = GROUP * ROWS

    def origin(slot):
        half = slot // GROUP
        return slot - half * GROUP + GROUP * jnp.where(second == half, 0, 1)

    def arriving(chunk):
        source = op_ref.at[pl.ds(origin(chunk * CHUNK), CHUNK)]
        return pltpu.make_async_copy(source, held.at[pl.ds(chunk * CHUNK, CHUNK)], in_sems.at[chunk])

    for chunk in range(chunks):
        arriving(chunk).start()
    scalars = [
        pltpu.make_async_copy(adjacency_ref, adj_ref, other_sems.at[0]),
        pltpu.make_async_copy(valid_ref, counts_ref, other_sems.at[1]),
    ]
    extras = []
    for number, source in enumerate((start_ref, rhs_ref)):
        for place, target in enumerate((outer_ref, inner_ref)):
            rows = pl.ds(tail + 8 * number, 8)
            sem = other_sems.at[2 + 2 * number + place]
            extras.append(pltpu.make_async_copy(source, target.at[rows, :], sem))
    for copy in scalars + extras:
        copy.start()
    for copy in scalars:
        copy.wait()

    def one(slot, target, at):
        e = origin(slot)
        blocks = []
        for tile in range(columns // LANES):
            lanes = pl.ds(tile * LANES, LANES)
            top = held[slot, pl.ds(0, HALF), lanes]
            low = held[slot, pl.ds(HALF, HALF), lanes]
            blocks.append(jnp.where(left, top, pltpu.roll(low, WIDTH, 1)))
            blocks.append(jnp.where(left, pltpu.roll(top, WIDTH, 1), low))
        if columns % LANES:
            lanes = pl.ds(columns - WIDTH, WIDTH)
            top = held[slot, pl.ds(0, HALF), lanes]
            low = held[slot, pl.ds(HALF, HALF), lanes]
            blocks.append(jnp.concatenate([top, low], axis=1))
        count = counts_ref[e]
        place = []
        for face in range(faces):
            offset = adj_ref[face, e] - (base + e) + REACH
            place.append(jnp.where(face < count, offset, -1))
        for band in range(BANDS):
            rows = pl.ds(pl.multiple_of(at * ROWS + band * HALF, HALF), HALF)
            total = blocks[0] if band == REACH else None
            if band != REACH:
                for face in range(faces):
                    weight = jnp.where(place[face] == band, jnp.float32(1), jnp.float32(0))
                    term = blocks[face + 1] * weight
                    total = term if total is None else total + term
            target[rows, :] = total

    for half, target in enumerate((outer_ref, inner_ref)):

        def some(part, carry, half=half, target=target):
            chunk = half * (GROUP // CHUNK) + part
            arriving(chunk).wait()
            for k in range(CHUNK):
                at = part * CHUNK + k
                one(half * GROUP + at, target, at)
            return carry

        lax.fori_loop(0, GROUP // CHUNK, some, 0)
    for extra in extras:
        extra.wait()


def stacked_sums(terms, row):
    for span in (4, 2, 1):
        low = (row & span) == 0
        half = len(terms) // 2
        merged = []
        for a, b in zip(terms[:half], terms[half:]):
            kept = jnp.where(low, a, b)
            if span == 4:
                moved = pltpu.roll(jnp.where(low, b, a), 4, 0)
            else:
                moved = jnp.where(low, pltpu.roll(a, 8 - span, 0), pltpu.roll(b, span, 0))
            merged.append(kept + moved)
        terms = merged
    return terms[0]


def spread(ref, at, packed):
    left = lane_ids(8) < WIDTH
    turned = pltpu.roll(packed, WIDTH, 1)
    ref[pl.ds(at, 8, stride=2), :] = jnp.where(left, packed, turned)
    ref[pl.ds(at + 1, 8, stride=2), :] = jnp.where(left, turned, packed)


def times(ref, vecs, at):
    row = lax.broadcasted_iota(jnp.int32, (8, LANES), 0)
    half = lane_ids(HALF)
    left = half < WIDTH
    spot = half % WIDTH - lax.broadcasted_iota(jnp.int32, (HALF, LANES), 0)
    near = [vecs[pl.ds(at + (k - REACH), 1), :] for k in range(GROUP + 2 * REACH)]
    terms = []
    for k in range(GROUP):
        total = None
        for band in range(BANDS):
            rows = pl.ds(k * ROWS + band * HALF, HALF)
            term = ref[rows, :] * near[k + band]
            total = term if total is None else total + term
        top = jnp.sum(jnp.where(left, total, 0.0), axis=1, keepdims=True)
        low = jnp.sum(jnp.where(left, 0.0, total), axis=1, keepdims=True)
        placed = jnp.where(spot == 0, top, jnp.where(spot == HALF, low, 0.0))
        terms.append(jnp.sum(placed.reshape(HALF // 8, 8, LANES), axis=0))
    return stacked_sums(terms, row)


def applications(first, last, refs, vecs, level, shifts_ref):
    given = (last - first + 1) * level

    def apply(index, groups):
        at = pl.multiple_of((index - first) * level, 8)
        if first == 0:
            opening = index == 0
            source = pl.multiple_of(jnp.where(opening, given, at), 8)
            sign = jnp.where(opening, jnp.float32(-1), jnp.float32(1))
            scale = jnp.where(opening, jnp.float32(1), -shifts_ref[jnp.maximum(index - 1, 0)])
        else:
            source, sign, scale = at, None, -shifts_ref[index - 1]
        made = []
        for group in groups:
            place = GROUP * (group + 1)
            fresh = times(refs[group], vecs, at + place)
            if sign is not None:
                fresh = sign * fresh
            made.append((place, fresh + scale * vecs[pl.ds(source + place, 8), :]))
        for place, value in made:
            vecs[pl.ds(at + level + place, 8), :] = value

    def turn(index, carry):
        apply(index, range(4))
        return carry

    lax.fori_loop(first, last - 1, turn, 0)
    apply(last - 1, (1, 2))


def by_core(run, outer, own, inner):
    second = lax.axis_index(AXES) % 2 == 1

    @pl.when(second)
    def _():
        run(inner, own[::-1], outer)

    @pl.when(jnp.logical_not(second))
    def _():
        run(outer, own, inner)


def packed_rows(vecs, at):
    left = lane_ids(8) < WIDTH
    return jnp.where(left, vecs[pl.ds(at, 8, stride=2), :], vecs[pl.ds(at + 1, 8, stride=2), :])


def early_kernel(
    count, got_inner, own_inner, own_outer, got_outer, shifts_ref, basis_ref, last_ref, vecs
):
    level = 6 * GROUP

    def run(before, own, after):
        refs = (before, *own, after)
        tail = GROUP * ROWS
        for part, ref in enumerate((before, own[0], after)):
            spread(vecs, part * 2 * GROUP, ref[pl.ds(tail, 8), :])
            spread(vecs, (count + 1) * level + part * 2 * GROUP, ref[pl.ds(tail + 8, 8), :])
        applications(0, count, refs, vecs, level, shifts_ref)

    by_core(run, got_outer, (own_outer, own_inner), got_inner)
    for k in range(count):
        row = packed_rows(vecs, (k + 1) * level + 2 * GROUP)
        basis_ref[pl.ds(8 * k, 8), :] = row
        if k == count - 1:
            last_ref[...] = row


def late_kernel(
    count, size, vec_inner, vec_own, vec_outer, got_inner, own_inner, own_outer, got_outer,
    early_ref, shifts_ref, basis_ref, gram_ref, vecs,
):
    level = 6 * GROUP

    def run(before, own, after):
        refs = (before[1], *own, after[1])
        for part, ref in enumerate((before[0], vec_own, after[0])):
            spread(vecs, part * 2 * GROUP, ref[...])
        applications(count, size, refs, vecs, level, shifts_ref)

    by_core(run, (vec_outer, got_outer), (own_outer, own_inner), (vec_inner, got_inner))
    rows = [early_ref[pl.ds(8 * k, 8), :] for k in range(count)]
    for k in range(size - count):
        rows.append(packed_rows(vecs, (k + 1) * level + 2 * GROUP))
        basis_ref[pl.ds(8 * k, 8), :] = rows[-1]
    lane = lane_ids(8)
    total = jnp.zeros((8, LANES), jnp.float32)
    number = 0
    for i in range(size):
        for j in range(i, size):
            entry = jnp.sum(rows[i] * rows[j], axis=1, keepdims=True)
            total = jnp.where(lane == number, entry, total)
            number += 1
    gram = jnp.sum(total, axis=0, keepdims=True)
    gram_ref[...] = jnp.broadcast_to(gram, gram_ref.shape)


def partial_kernel(parts_ref, out_ref):
    total = jnp.sum(parts_ref[...], axis=0, keepdims=True)
    out_ref[...] = jnp.broadcast_to(total, out_ref.shape)


def inverse_root(value):
    guess = lax.rsqrt(value)
    return guess * (1.5 - 0.5 * value * guess * guess)


def finish_kernel(count, steps, parts_ref, early_ref, late_ref, start_ref, shifts_ref, sol_ref, res_ref, upper_ref):
    size = steps + 1
    lane = lane_ids(8)
    summed = jnp.broadcast_to(jnp.sum(parts_ref[...], axis=0, keepdims=True), (8, LANES))
    gram = {}
    number = 0
    for i in range(size):
        for j in range(i, size):
            entry = jnp.sum(jnp.where(lane == number, summed, 0.0), axis=1, keepdims=True)
            gram[i, j] = jnp.broadcast_to(entry, (8, LANES))
            number += 1
    factor = {}
    for k in range(size):
        turn = inverse_root(gram[k, k])
        for j in range(k, size):
            factor[k, j] = gram[k, j] * turn
        for i in range(k + 1, size):
            for j in range(i, size):
                gram[i, j] = gram[i, j] - factor[k, i] * factor[k, j]
    hess = {}
    for k in range(steps):
        for i in range(k + 1):
            hess[i, k] = factor[i, k] * shifts_ref[k] + factor[i, k + 1]
        hess[k + 1, k] = factor[k + 1, k + 1]
    target = [factor[0, 0]] + [jnp.zeros((8, LANES), jnp.float32)] * steps
    inverse = []
    for k in range(steps):
        a, b = hess[k, k], hess[k + 1, k]
        scale = inverse_root(a * a + b * b)
        cos, sin = a * scale, b * scale
        inverse.append(scale)
        for j in range(k + 1, steps):
            up, down = hess[k, j], hess[k + 1, j]
            hess[k, j] = cos * up + sin * down
            hess[k + 1, j] = cos * down - sin * up
        target[k], target[k + 1] = cos * target[k], -(sin * target[k])
    coeffs = [None] * steps
    for k in range(steps - 1, -1, -1):
        value = target[k]
        for j in range(k + 1, steps):
            value = value - hess[k, j] * coeffs[j]
        coeffs[k] = value * inverse[k]
    rows = []
    for ref in (early_ref, late_ref):
        rows += [ref[pl.ds(at, 8), :] for at in range(0, ref.shape[0], 8)]
    sol, res = 0.0, 0.0
    for k in range(steps):
        sol = sol + coeffs[k] * rows[k]
        res = res + coeffs[k] * (rows[k + 1] + shifts_ref[k] * rows[k])
    sol_ref[...] = start_ref[...] + sol
    res_ref[...] = rows[0] - res
    wide = lane_ids(16)
    tall = lax.broadcasted_iota(jnp.int32, (16, LANES), 0)
    scale = 1.0 / (count ** 0.5)
    upper = jnp.zeros((16, LANES), jnp.float32)
    for i in range(size):
        for j in range(i, size):
            entry = jnp.concatenate([factor[i, j]] * 2, axis=0) * scale
            upper = jnp.where((wide == j) & (tall == i), entry, upper)
    upper_ref[...] = upper[:size, :size]


def body(operator, adjacency, counts, rhs, start, shifts):
    elems, width, columns = operator.shape
    steps = shifts.shape[0]
    devices = lax.axis_size(AXES)
    slabs = lax.axis_size("slab")
    groups = lax.axis_size("group")
    packed = elems * width // LANES
    size = steps + 1
    early = size // 2
    block = GROUP * ROWS + 2 * packed
    level = 6 * GROUP
    vmem = pl.BlockSpec(memory_space=pltpu.VMEM)
    smem = pl.BlockSpec(memory_space=pltpu.SMEM)
    hbm = pl.BlockSpec(memory_space=pl.ANY)
    mebi = 1024 * 1024
    f32 = jnp.float32

    x = start.reshape(packed, LANES)
    b = rhs.reshape(packed, LANES)
    sources = (operator, adjacency.T, counts, x, b)
    own_outer, own_inner = pl.pallas_call(
        band_kernel,
        out_shape=(pltpu.VMEM((block, LANES), f32), pltpu.VMEM((block, LANES), f32)),
        in_specs=[hbm] * 5,
        out_specs=(vmem, vmem),
        scratch_shapes=[
            pltpu.VMEM(operator.shape, f32),
            pltpu.SMEM(adjacency.T.shape, jnp.int32),
            pltpu.SMEM(counts.shape, jnp.int32),
            pltpu.SemaphoreType.DMA((elems // CHUNK,)),
            pltpu.SemaphoreType.DMA((6,)),
        ],
        compiler_params=pltpu.CompilerParams(vmem_limit_bytes=16 * mebi),
        name="bands",
    )(*(pltpu.with_memory_space_constraint(source, pltpu.HBM) for source in sources))
    bands = (within_chip(own_inner), own_inner, own_outer, between_chips(own_outer))
    first, last = pl.pallas_call(
        functools.partial(early_kernel, early),
        out_shape=(
            jax.ShapeDtypeStruct((8 * early, LANES), f32),
            jax.ShapeDtypeStruct((packed, LANES), f32),
        ),
        in_specs=[vmem] * 4 + [smem],
        out_specs=(vmem, vmem),
        scratch_shapes=[pltpu.VMEM(((early + 2) * level, LANES), f32)],
        compiler_params=pltpu.CompilerParams(vmem_limit_bytes=16 * mebi),
        name="early",
    )(*bands, shifts)
    rest, gram = pl.pallas_call(
        functools.partial(late_kernel, early, size),
        out_shape=(
            jax.ShapeDtypeStruct((8 * (size - early), LANES), f32),
            jax.ShapeDtypeStruct((slabs, LANES), f32),
        ),
        in_specs=[vmem] * 8 + [smem],
        out_specs=(vmem, vmem),
        scratch_shapes=[pltpu.VMEM(((size - early + 1) * level, LANES), f32)],
        compiler_params=pltpu.CompilerParams(vmem_limit_bytes=16 * mebi),
        name="late",
    )(within_chip(last), last, between_chips(last), *bands, first, shifts)
    parts = lax.all_to_all(gram, "slab", 0, 0, tiled=True)
    parts = pl.pallas_call(
        partial_kernel,
        out_shape=jax.ShapeDtypeStruct((groups, LANES), f32),
        in_specs=[vmem],
        out_specs=vmem,
        compiler_params=pltpu.CompilerParams(vmem_limit_bytes=4 * mebi),
        name="partial",
    )(parts)
    parts = lax.all_to_all(parts, "group", 0, 0, tiled=True)
    sol, res, upper = pl.pallas_call(
        functools.partial(finish_kernel, devices * elems * width, steps),
        out_shape=(
            jax.ShapeDtypeStruct((packed, LANES), f32),
            jax.ShapeDtypeStruct((packed, LANES), f32),
            jax.ShapeDtypeStruct((steps + 1, steps + 1), f32),
        ),
        in_specs=[vmem, vmem, vmem, vmem, smem],
        out_specs=(vmem, vmem, vmem),
        compiler_params=pltpu.CompilerParams(vmem_limit_bytes=4 * mebi),
        name="finish",
    )(parts, first, rest, x, shifts)
    return (sol.reshape(-1), res.reshape(-1), upper)


def solution(mesh):
    split = P(AXES)
    return jax.shard_map(
        body,
        mesh=mesh,
        in_specs=(P(AXES, None, None), P(AXES, None), split, split, split, P()),
        out_specs=(split, split, P()),
        check_vma=False,
    )
```

time: 73.1 us -> 78.3 us (1.071)
  waiting for transfers between devices: 5.02 us -> 11.2 us
    ppermute x1 -> x2, waiting for transfers between devices: 0.71 us -> 11.1 us  [between_chips(): return lax.ppermute(array, AXES, pairs)]
    ppermute x1 -> x2, starting transfers between devices: 5.02 us -> 10.7 us  [within_chip(): lax.ppermute(array, AXES, [(i, i + 1 - 2 * (i % 2)) for i in range(size)])]
    ppermute x2 -> x0, starting transfers between devices: 5.28 us -> none  [shifted(): return lax.ppermute(array, AXES, pairs)]
    ppermute x2 -> x0, waiting for transfers between devices: 4.31 us -> none  [shifted(): return lax.ppermute(array, AXES, pairs)]
    all_to_all x1, blocking collectives: 18.2 us -> 16.5 us  [body(): parts = lax.all_to_all(gram, 'slab', 0, 0, tiled=True)]
    all_to_all x1, blocking collectives: 26 us -> 27.1 us  [body(): parts = lax.all_to_all(parts, 'group', 0, 0, tiled=True)]
    ppermute x1 -> x2, starting transfers between devices: 4.51 us -> 3.85 us  [between_chips(): return lax.ppermute(array, AXES, pairs)]
    pallas_call x2 -> x3, Pallas kernels: 6.48 us -> 6.45 us  [the longest x1 2.47 us: body(): pl.pallas_call(functools.partial(late_kernel, early, size), out_shape=(ja...]
  transfers between devices with their start and end apart: 4 -> 4, of which waited for: 2 -> 3; matrix products, arithmetic and copies ran while one was open for 0% -> 0% of each run, Pallas kernels for 0% -> 0%
where the time goes in v6:
time: 78.3 us; the launch traced here: 78 us
  blocking collectives  43.6 us (56%)
  starting transfers between devices  14.6 us (19%)
  waiting for transfers between devices  11.2 us (14%)
  Pallas kernels  7.94 us (10%)
    all_to_all x1, blocking collectives, body(): parts = lax.all_to_all(parts, 'group', 0, 0, tiled=True)  27.1 us
    all_to_all x1, blocking collectives, body(): parts = lax.all_to_all(gram, 'slab', 0, 0, tiled=True)  16.5 us
    ppermute x2, waiting for transfers between devices, between_chips(): return lax.ppermute(array, AXES, pairs)  11.1 us
    ppermute x2, starting transfers between devices, within_chip(): lax.ppermute(array, AXES, [(i, i + 1 - 2 * (i % 2)) for i in range(size)])  10.7 us
    ppermute x2, starting transfers between devices, between_chips(): return lax.ppermute(array, AXES, pairs)  3.85 us
    pallas_call x1, Pallas kernels, body(): pl.pallas_call(functools.partial(late_kernel, early, size), out_shape=(ja...  2.47 us
    pallas_call x1, Pallas kernels, body(): pl.pallas_call(band_kernel, out_shape=(pltpu.VMEM((block, LANES), f32), p...  2.01 us
    pallas_call x1, Pallas kernels, body(): pl.pallas_call(functools.partial(early_kernel, early), out_shape=(jax.Sha...  1.97 us
  transfers between devices with their start and end apart: 4, of which 3 were waited for; matrix products, arithmetic and copies ran while one was open for 0% of the time, Pallas kernels for 0%

profile of v6, /device:TPU:1, one launch (start us, length us, event | category | flops | bytes accessed | tf_op | source)
XLA Modules:
  0.0 78.0 jit_solution(11431009972148695931)
XLA Ops:
  0.6 0.0 copy-start.1
  0.6 2.0 %bands.1 = (f32[1296,128]{1,0:T(8,128)S(1)}, f32[1296,128]{1,0:T(8,128)S(1)}) custom-call(f32[16,64,448]{2,1,0:T(8,128)} %op_ref.1, s32[6,16]{1,0:T(8,128)} %bitcast.19, s32[16]{0:T(128)} %valid_ref.1, f32[8,128]{1,0:T(8,128)} %bitcast.16, f32[8,128]{1,0:T(8,128)} %bitcast.20), custom_call_target="tpu_custom_call" | custom-call | tf_op jit(solution)/shard_map/bands/pallas_call | solution.py:350
  2.7 8.8 %collective-permute-start = (f32[1296,128]{1,0:T(8,128)S(1)}, f32[1296,128]{1,0:T(8,128)S(1)}, u32[]{:S(2)}, u32[]{:S(2)}) collective-permute-start(f32[1296,128]{1,0:T(8,128)S(1)} %get-tuple-element.12.own_inner), channel_id=1, source_target_pairs={{0,1},{1,0},{2,3},{3,2},{4,5},{5,4},{6,7},{7,6},{8,9},{9,8},{10,11... | collective-permute-start | bytes 1990664 | tf_op jit(solution)/shard_map/ppermute | solution.py:29
  11.5 0.0 copy-start
  11.5 1.9 %collective-permute-start.1 = (f32[1296,128]{1,0:T(8,128)S(1)}, f32[1296,128]{1,0:T(8,128)S(1)}, u32[]{:S(2)}, u32[]{:S(2)}) collective-permute-start(f32[1296,128]{1,0:T(8,128)S(1)} %get-tuple-element.13.own_outer), channel_id=1, source_target_pairs={{1,2},{2,1},{3,4},{4,3},{5,6},{6,5},{7,8},{8,7},{9,10},{10,9},{11,... | collective-permute-start | bytes 1990664 | tf_op jit(solution)/shard_map/ppermute | solution.py:24
  13.4 0.0 collective-permute-done.got_inner
  13.4 10.1 %collective-permute-done.1.got_outer = f32[1296,128]{1,0:T(8,128)S(1)} collective-permute-done((f32[1296,128]{1,0:T(8,128)S(1)}, f32[1296,128]{1,0:T(8,128)S(1)}, u32[]{:S(2)}, u32[]{:S(2)}) %collective-permute-start.1) | collective-permute-done | bytes 663584 | tf_op jit(solution)/shard_map/ppermute | solution.py:24
  23.5 0.0 copy-done.1
  23.5 2.0 %early.1 = (f32[32,128]{1,0:T(8,128)S(1)}, f32[8,128]{1,0:T(8,128)S(1)}) custom-call(f32[1296,128]{1,0:T(8,128)S(1)} %collective-permute-done.got_inner, f32[1296,128]{1,0:T(8,128)S(1)} %get-tuple-element.12.own_inner, f32[1296,128]{1,0:T(8,128)S(1)} %get-tuple-element.13.own_outer, f32[1296,128]{1,0:T(8,128)S(1)} %collective-permute-done.1.got_outer, ...), custom_call_target="tpu_custom_call" | custom-call | tf_op jit(solution)/shard_map/early/pallas_call | solution.py:366
  25.4 1.9 %collective-permute-start.3 = (f32[8,128]{1,0:T(8,128)S(1)}, f32[8,128]{1,0:T(8,128)S(1)}, u32[]{:S(2)}, u32[]{:S(2)}) collective-permute-start(f32[8,128]{1,0:T(8,128)S(1)} %get-tuple-element.14.vec_own), channel_id=1, source_target_pairs={{1,2},{2,1},{3,4},{4,3},{5,6},{6,5},{7,8},{8,7},{9,10},{10,9},{11,... | collective-permute-start | bytes 12296 | tf_op jit(solution)/shard_map/ppermute | solution.py:24
  27.4 1.9 %collective-permute-start.2 = (f32[8,128]{1,0:T(8,128)S(1)}, f32[8,128]{1,0:T(8,128)S(1)}, u32[]{:S(2)}, u32[]{:S(2)}) collective-permute-start(f32[8,128]{1,0:T(8,128)S(1)} %get-tuple-element.14.vec_own), channel_id=1, source_target_pairs={{0,1},{1,0},{2,3},{3,2},{4,5},{5,4},{6,7},{7,6},{8,9},{9,8},{10,11... | collective-permute-start | bytes 12296 | tf_op jit(solution)/shard_map/ppermute | solution.py:29
  29.3 1.1 %collective-permute-done.3.vec_outer = f32[8,128]{1,0:T(8,128)S(1)} collective-permute-done((f32[8,128]{1,0:T(8,128)S(1)}, f32[8,128]{1,0:T(8,128)S(1)}, u32[]{:S(2)}, u32[]{:S(2)}) %collective-permute-start.3) | collective-permute-done | bytes 4128 | tf_op jit(solution)/shard_map/ppermute | solution.py:24
  30.4 0.1 collective-permute-done.2.vec_inner
  30.4 2.5 %late.1 = (f32[40,128]{1,0:T(8,128)S(1)}, f32[32,128]{1,0:T(8,128)S(1)}) custom-call(f32[8,128]{1,0:T(8,128)S(1)} %collective-permute-done.2.vec_inner, f32[8,128]{1,0:T(8,128)S(1)} %get-tuple-element.14.vec_own, f32[8,128]{1,0:T(8,128)S(1)} %collective-permute-done.3.vec_outer, f32[1296,128]{1,0:T(8,128)S(1)} %collective-permute-done.got_inner, ...), custom_call_target="tpu_custom_call" | custom-call | tf_op jit(solution)/shard_map/late/pallas_call | solution.py:378
  32.9 16.5 %all_to_all.22 = f32[32,1,128]{2,1,0:T(1,128)S(1)} all-to-all(f32[32,1,128]{2,1,0:T(1,128)S(1)} %bitcast.18), channel_id=1, replica_groups=mesh['group'=16,'slab'=32] {'slab'}, dimensions={0} | all-to-all | bytes 32768 | tf_op jit(solution)/shard_map/all_to_all | solution.py:390
  49.4 27.1 %all_to_all.23 = f32[16,1,128]{2,1,0:T(1,128)S(1)} all-to-all(f32[16,1,128]{2,1,0:T(1,128)S(1)} %bitcast.15), channel_id=1, replica_groups=mesh['group'=16,'slab'=32] {'group'}, dimensions={0} | all-to-all | bytes 16384 | tf_op jit(solution)/shard_map/all_to_all | solution.py:399
  76.5 0.0 copy-done
  76.5 1.5 %finish.1 = (f32[8,128]{1,0:T(8,128)}, f32[8,128]{1,0:T(8,128)}, f32[9,9]{1,0:T(8,128)}) custom-call(f32[16,128]{1,0:T(8,128)S(1)} %bitcast.14, f32[32,128]{1,0:T(8,128)S(1)} %get-tuple-element.15.early_ref, f32[40,128]{1,0:T(8,128)S(1)} %get-tuple-element.17.late_ref, f32[8,128]{1,0:T(8,128)S(1)} %bitcast.17, f32[8]{0:T(128)S(1)} %copy-done.1), custom_call_target="tpu_custom_call" | custom-call | tf_op jit(solution)/shard_map/finish/pallas_call | solution.py:400
  (1 shorter events, 0.0 us)
Async XLA Ops:
  0.6 22.8 %copy-start.1 = (f32[8]{0:T(128)S(1)}, f32[8]{0:T(128)}, u32[]{:S(2)}) copy-start(f32[8]{0:T(128)} %shifts_ref.5) | copy-start | bytes 100
  2.7 10.7 %collective-permute-start = (f32[1296,128]{1,0:T(8,128)S(1)}, f32[1296,128]{1,0:T(8,128)S(1)}, u32[]{:S(2)}, u32[]{:S(2)}) collective-permute-start(f32[1296,128]{1,0:T(8,128)S(1)} %get-tuple-element.12.own_inner), channel_id=1, source_target_pairs={{0,1},{1,0},{2,3},{3,2},{4,5},{5,4},{6,7},{7,6},{8,9},{9,8},{10,11... | collective-permute-start | bytes 1990664 | tf_op jit(solution)/shard_map/ppermute | solution.py:29
  11.5 65.1 %copy-start = (f32[1024]{0:T(1024)S(1)}, f32[1024]{0:T(1024)}, u32[]{:S(2)}) copy-start(f32[1024]{0:T(1024)} %param.10) | copy-start | bytes 12292
  11.5 12.0 %collective-permute-start.1 = (f32[1296,128]{1,0:T(8,128)S(1)}, f32[1296,128]{1,0:T(8,128)S(1)}, u32[]{:S(2)}, u32[]{:S(2)}) collective-permute-start(f32[1296,128]{1,0:T(8,128)S(1)} %get-tuple-element.13.own_outer), channel_id=1, source_target_pairs={{1,2},{2,1},{3,4},{4,3},{5,6},{6,5},{7,8},{8,7},{9,10},{10,9},{11,... | collective-permute-start | bytes 1990664 | tf_op jit(solution)/shard_map/ppermute | solution.py:24
  25.4 4.9 %collective-permute-start.3 = (f32[8,128]{1,0:T(8,128)S(1)}, f32[8,128]{1,0:T(8,128)S(1)}, u32[]{:S(2)}, u32[]{:S(2)}) collective-permute-start(f32[8,128]{1,0:T(8,128)S(1)} %get-tuple-element.14.vec_own), channel_id=1, source_target_pairs={{1,2},{2,1},{3,4},{4,3},{5,6},{6,5},{7,8},{8,7},{9,10},{10,9},{11,... | collective-permute-start | bytes 12296 | tf_op jit(solution)/shard_map/ppermute | solution.py:24
  27.4 3.1 %collective-permute-start.2 = (f32[8,128]{1,0:T(8,128)S(1)}, f32[8,128]{1,0:T(8,128)S(1)}, u32[]{:S(2)}, u32[]{:S(2)}) collective-permute-start(f32[8,128]{1,0:T(8,128)S(1)} %get-tuple-element.14.vec_own), channel_id=1, source_target_pairs={{0,1},{1,0},{2,3},{3,2},{4,5},{5,4},{6,7},{7,6},{8,9},{9,8},{10,11... | collective-permute-start | bytes 12296 | tf_op jit(solution)/shard_map/ppermute | solution.py:29

commit v7 on v6

--- a/solution.py
+++ b/solution.py
@@ -15,6 +15,7 @@
 HALF = WIDTH // 2
 ROWS = BANDS * HALF
 CHUNK = 4
+PAD = 8
 GROUP = 8
 
 
@@ -27,6 +28,12 @@
 def within_chip(array):
     size = lax.axis_size(AXES)
     return lax.ppermute(array, AXES, [(i, i + 1 - 2 * (i % 2)) for i in range(size)])
+
+
+def across(array, toward):
+    size = lax.axis_size(AXES)
+    pairs = [(i, i + toward * (4 * (i % 2) - 2)) for i in range(size)]
+    return lax.ppermute(array, AXES, [(i, j) for i, j in pairs if 0 <= j < size])
 
 
 def lane_ids(rows):
@@ -115,6 +122,9 @@
         extra.wait()
 
 
+LEVEL = 6 * GROUP + 2 * PAD
+
+
 def stacked_sums(terms, row):
     for span in (4, 2, 1):
         low = (row & span) == 0
@@ -158,90 +168,100 @@
     return stacked_sums(terms, row)
 
 
-def applications(first, last, refs, vecs, level, shifts_ref):
-    given = (last - first + 1) * level
-
-    def apply(index, groups):
-        at = pl.multiple_of((index - first) * level, 8)
-        if first == 0:
-            opening = index == 0
-            source = pl.multiple_of(jnp.where(opening, given, at), 8)
-            sign = jnp.where(opening, jnp.float32(-1), jnp.float32(1))
-            scale = jnp.where(opening, jnp.float32(1), -shifts_ref[jnp.maximum(index - 1, 0)])
+def application(index, groups, refs, vecs, shifts_ref):
+    levels = vecs.shape[0] // LEVEL
+    at = pl.multiple_of(index * LEVEL, 8)
+    opening = index == 0
+    source = pl.multiple_of(jnp.where(opening, (levels - 1) * LEVEL, at), 8)
+    sign = jnp.where(opening, jnp.float32(-1), jnp.float32(1))
+    scale = jnp.where(opening, jnp.float32(1), -shifts_ref[jnp.maximum(index - 1, 0)])
+    made = []
+    for group in groups:
+        place = PAD + GROUP * group
+        fresh = times(refs[group], vecs, at + place)
+        made.append((place, sign * fresh + scale * vecs[pl.ds(source + place, 8), :]))
+    for place, value in made:
+        vecs[pl.ds(at + LEVEL + place, 8), :] = value
+
+
+def applications(plan, refs, vecs, shifts_ref):
+    for first, last, groups in plan:
+
+        def turn(index, carry, groups=groups):
+            application(index, groups, refs, vecs, shifts_ref)
+            return carry
+
+        if last - first == 1:
+            turn(jnp.int32(first), 0)
         else:
-            source, sign, scale = at, None, -shifts_ref[index - 1]
-        made = []
-        for group in groups:
-            place = GROUP * (group + 1)
-            fresh = times(refs[group], vecs, at + place)
-            if sign is not None:
-                fresh = sign * fresh
-            made.append((place, fresh + scale * vecs[pl.ds(source + place, 8), :]))
-        for place, value in made:
-            vecs[pl.ds(at + level + place, 8), :] = value
-
-    def turn(index, carry):
-        apply(index, range(4))
-        return carry
-
-    lax.fori_loop(first, last - 1, turn, 0)
-    apply(last - 1, (1, 2))
-
-
-def by_core(run, outer, own, inner):
+            lax.fori_loop(first, last, turn, 0)
+
+
+def by_core(run):
     second = lax.axis_index(AXES) % 2 == 1
 
     @pl.when(second)
     def _():
-        run(inner, own[::-1], outer)
+        run(lambda items: items[::-1], True)
 
     @pl.when(jnp.logical_not(second))
     def _():
-        run(outer, own, inner)
-
-
-def packed_rows(vecs, at):
+        run(lambda items: items, False)
+
+
+def fill_far(vecs, row, at):
+    packed = jnp.broadcast_to(row, (8, LANES))
+    turned = pltpu.roll(packed, WIDTH, 1)
     left = lane_ids(8) < WIDTH
-    return jnp.where(left, vecs[pl.ds(at, 8, stride=2), :], vecs[pl.ds(at + 1, 8, stride=2), :])
+    vecs[pl.ds(at, 1), :] = jnp.where(left, packed, turned)[:1]
+    vecs[pl.ds(at + 1, 1), :] = jnp.where(left, turned, packed)[:1]
 
 
 def early_kernel(
-    count, got_inner, own_inner, own_outer, got_outer, shifts_ref, basis_ref, last_ref, vecs
+    plan, other_far, other_near, own_inner, own_outer, near_ref, shifts_ref, vecs
 ):
-    level = 6 * GROUP
-
-    def run(before, own, after):
-        refs = (before, *own, after)
+    empty = jnp.zeros((8, LANES), jnp.float32)
+    for at in range(0, vecs.shape[0], 8):
+        vecs[pl.ds(at, 8), :] = empty
+
+    def run(order, turned):
+        refs = order([None, near_ref, own_outer, own_inner, other_near, other_far])
         tail = GROUP * ROWS
-        for part, ref in enumerate((before, own[0], after)):
-            spread(vecs, part * 2 * GROUP, ref[pl.ds(tail, 8), :])
-            spread(vecs, (count + 1) * level + part * 2 * GROUP, ref[pl.ds(tail + 8, 8), :])
-        applications(0, count, refs, vecs, level, shifts_ref)
-
-    by_core(run, got_outer, (own_outer, own_inner), got_inner)
-    for k in range(count):
-        row = packed_rows(vecs, (k + 1) * level + 2 * GROUP)
-        basis_ref[pl.ds(8 * k, 8), :] = row
-        if k == count - 1:
-            last_ref[...] = row
+        given = vecs.shape[0] - LEVEL
+        for part, ref in enumerate(order([near_ref, own_outer, other_near])):
+            at = PAD + part * 2 * GROUP
+            spread(vecs, at, ref[pl.ds(tail, 8), :])
+            spread(vecs, given + at, ref[pl.ds(tail + 8, 8), :])
+        applications([(i, j, order_groups(groups, turned)) for i, j, groups in plan], refs, vecs, shifts_ref)
+
+    by_core(run)
+
+
+def order_groups(groups, turned):
+    return [5 - group for group in groups] if turned else groups
 
 
 def late_kernel(
-    count, size, vec_inner, vec_own, vec_outer, got_inner, own_inner, own_outer, got_outer,
+    plan, size, far_outer, far_inner, other_far, other_near, own_inner, own_outer, near_ref, rim_ref,
     early_ref, shifts_ref, basis_ref, gram_ref, vecs,
 ):
-    level = 6 * GROUP
-
-    def run(before, own, after):
-        refs = (before[1], *own, after[1])
-        for part, ref in enumerate((before[0], vec_own, after[0])):
-            spread(vecs, part * 2 * GROUP, ref[...])
-        applications(count, size, refs, vecs, level, shifts_ref)
-
-    by_core(run, (vec_outer, got_outer), (own_outer, own_inner), (vec_inner, got_inner))
-    rows = [early_ref[pl.ds(8 * k, 8), :] for k in range(count)]
-    for k in range(size - count):
-        rows.append(packed_rows(vecs, (k + 1) * level + 2 * GROUP))
+    for at in range(0, vecs.shape[0], 8):
+        vecs[pl.ds(at, 8), :] = early_ref[pl.ds(at, 8), :]
+
+    def run(order, turned):
+        refs = order([rim_ref, near_ref, own_outer, own_inner, other_near, other_far])
+        before, after = order([far_outer, far_inner])
+        fill_far(vecs, before[pl.ds(7, 1), :], PAD - 2)
+        fill_far(vecs, after[pl.ds(0, 1), :], PAD + 6 * GROUP)
+        applications([(i, j, order_groups(groups, turned)) for i, j, groups in plan], refs, vecs, shifts_ref)
+
+    by_core(run)
+    left = lane_ids(8) < WIDTH
+    rows = []
+    for k in range(size):
+        at = (k + 1) * LEVEL + PAD + 2 * GROUP
+        even, odd = vecs[pl.ds(at, 8, stride=2), :], vecs[pl.ds(at + 1, 8, stride=2), :]
+        rows.append(jnp.where(left, even, odd))
         basis_ref[pl.ds(8 * k, 8), :] = rows[-1]
     lane = lane_ids(8)
     total = jnp.zeros((8, LANES), jnp.float32)
@@ -255,6 +275,24 @@
     gram_ref[...] = jnp.broadcast_to(gram, gram_ref.shape)
 
 
+def plans(size):
+    early, late = [], []
+    for k in range(size):
+        low, high = REACH * k - 2 * GROUP, 4 * GROUP - 1 - REACH * k
+        ranges = [[(low + GROUP, high - REACH)], [(low, low + GROUP - 1), (high - REACH + 1, high)]]
+        for plan, wanted in zip((early, late), ranges):
+            groups = [
+                g
+                for g in range(6)
+                if any(8 * g - 9 >= start and 8 * g - 16 <= end for start, end in wanted)
+            ]
+            if plan and plan[-1][2] == groups:
+                plan[-1] = (plan[-1][0], k + 1, groups)
+            else:
+                plan.append((k, k + 1, groups))
+    return early, late
+
+
 def partial_kernel(parts_ref, out_ref):
     total = jnp.sum(parts_ref[...], axis=0, keepdims=True)
     out_ref[...] = jnp.broadcast_to(total, out_ref.shape)
@@ -265,7 +303,7 @@
     return guess * (1.5 - 0.5 * value * guess * guess)
 
 
-def finish_kernel(count, steps, parts_ref, early_ref, late_ref, start_ref, shifts_ref, sol_ref, res_ref, upper_ref):
+def finish_kernel(count, steps, parts_ref, basis_ref, start_ref, shifts_ref, sol_ref, res_ref, upper_ref):
     size = steps + 1
     lane = lane_ids(8)
     summed = jnp.broadcast_to(jnp.sum(parts_ref[...], axis=0, keepdims=True), (8, LANES))
@@ -307,9 +345,7 @@
         for j in range(k + 1, steps):
             value = value - hess[k, j] * coeffs[j]
         coeffs[k] = value * inverse[k]
-    rows = []
-    for ref in (early_ref, late_ref):
-        rows += [ref[pl.ds(at, 8), :] for at in range(0, ref.shape[0], 8)]
+    rows = [basis_ref[pl.ds(8 * k, 8), :] for k in range(size)]
     sol, res = 0.0, 0.0
     for k in range(steps):
         sol = sol + coeffs[k] * rows[k]
@@ -335,9 +371,9 @@
     groups = lax.axis_size("group")
     packed = elems * width // LANES
     size = steps + 1
-    early = size // 2
+    early, late = plans(size)
     block = GROUP * ROWS + 2 * packed
-    level = 6 * GROUP
+    rows = (size + 2) * LEVEL
     vmem = pl.BlockSpec(memory_space=pltpu.VMEM)
     smem = pl.BlockSpec(memory_space=pltpu.SMEM)
     hbm = pl.BlockSpec(memory_space=pl.ANY)
@@ -362,31 +398,33 @@
         compiler_params=pltpu.CompilerParams(vmem_limit_bytes=16 * mebi),
         name="bands",
     )(*(pltpu.with_memory_space_constraint(source, pltpu.HBM) for source in sources))
-    bands = (within_chip(own_inner), own_inner, own_outer, between_chips(own_outer))
-    first, last = pl.pallas_call(
+    other_far = within_chip(own_outer)
+    other_near = within_chip(own_inner)
+    rim = between_chips(own_inner)
+    near = between_chips(own_outer)
+    held = pl.pallas_call(
         functools.partial(early_kernel, early),
-        out_shape=(
-            jax.ShapeDtypeStruct((8 * early, LANES), f32),
-            jax.ShapeDtypeStruct((packed, LANES), f32),
-        ),
-        in_specs=[vmem] * 4 + [smem],
-        out_specs=(vmem, vmem),
-        scratch_shapes=[pltpu.VMEM(((early + 2) * level, LANES), f32)],
+        out_shape=jax.ShapeDtypeStruct((rows, LANES), f32),
+        in_specs=[vmem] * 5 + [smem],
+        out_specs=vmem,
         compiler_params=pltpu.CompilerParams(vmem_limit_bytes=16 * mebi),
         name="early",
-    )(*bands, shifts)
-    rest, gram = pl.pallas_call(
-        functools.partial(late_kernel, early, size),
+    )(other_far, other_near, own_inner, own_outer, near, shifts)
+    basis, gram = pl.pallas_call(
+        functools.partial(late_kernel, late, size),
         out_shape=(
-            jax.ShapeDtypeStruct((8 * (size - early), LANES), f32),
+            jax.ShapeDtypeStruct((8 * size, LANES), f32),
             jax.ShapeDtypeStruct((slabs, LANES), f32),
         ),
-        in_specs=[vmem] * 8 + [smem],
+        in_specs=[vmem] * 9 + [smem],
         out_specs=(vmem, vmem),
-        scratch_shapes=[pltpu.VMEM(((size - early + 1) * level, LANES), f32)],
+        scratch_shapes=[pltpu.VMEM((rows, LANES), f32)],
         compiler_params=pltpu.CompilerParams(vmem_limit_bytes=16 * mebi),
         name="late",
-    )(within_chip(last), last, between_chips(last), *bands, first, shifts)
+    )(
+        across(x, -1), across(x, 1), other_far, other_near, own_inner, own_outer, near, rim,
+        held, shifts,
+    )
     parts = lax.all_to_all(gram, "slab", 0, 0, tiled=True)
     parts = pl.pallas_call(
         partial_kernel,
@@ -404,11 +442,11 @@
             jax.ShapeDtypeStruct((packed, LANES), f32),
             jax.ShapeDtypeStruct((steps + 1, steps + 1), f32),
         ),
-        in_specs=[vmem, vmem, vmem, vmem, smem],
+        in_specs=[vmem, vmem, vmem, smem],
         out_specs=(vmem, vmem, vmem),
         compiler_params=pltpu.CompilerParams(vmem_limit_bytes=4 * mebi),
         name="finish",
-    )(parts, first, rest, x, shifts)
+    )(parts, basis, x, shifts)
     return (sol.reshape(-1), res.reshape(-1), upper)
 
 

time: 78.3 us -> 73.9 us (0.944)
  waiting for transfers between devices: 11.2 us -> 3.76 us
  Pallas kernels: 7.94 us -> 10.3 us
  starting transfers between devices: 14.6 us -> 16 us
  blocking collectives: 43.6 us -> 42.7 us
    ppermute x2, waiting for transfers between devices: 11.1 us -> 2.42 us  [between_chips(): return lax.ppermute(array, AXES, pairs)]
    ppermute x2, starting transfers between devices: 10.7 us -> 6.9 us  [within_chip(): lax.ppermute(array, AXES, [(i, i + 1 - 2 * (i % 2)) for i in range(size)])]
    ppermute x0 -> x2, starting transfers between devices: none -> 2.64 us  [across(): lax.ppermute(array, AXES, [(i, j) for i, j in pairs if 0 <= j < size])]
    ppermute x2, starting transfers between devices: 3.85 us -> 6.43 us  [between_chips(): return lax.ppermute(array, AXES, pairs)]
    pallas_call x2, Pallas kernels: 4.43 us -> 6.83 us  [the longest x1 3.64 us: body(): pl.pallas_call(functools.partial(early_kernel, early), out_shape=jax.Shap...]
    ppermute x0 -> x2, waiting for transfers between devices: none -> 1.33 us  [across(): lax.ppermute(array, AXES, [(i, j) for i, j in pairs if 0 <= j < size])]
  transfers between devices with their start and end apart: 4 -> 6, of which waited for: 3 -> 2; matrix products, arithmetic and copies ran while one was open for 0% -> 0% of each run, Pallas kernels for 0% -> 5%
where the time goes in v7:
time: 73.9 us; the launch traced here: 73.6 us
  blocking collectives  42.7 us (58%)
  starting transfers between devices  16 us (22%)
  Pallas kernels  10.3 us (14%)
  waiting for transfers between devices  3.76 us (5%)
  between operations  0.76 us (1%)
    all_to_all x1, blocking collectives, body(): parts = lax.all_to_all(parts, 'group', 0, 0, tiled=True)  27 us
    all_to_all x1, blocking collectives, body(): parts = lax.all_to_all(gram, 'slab', 0, 0, tiled=True)  15.7 us
    ppermute x2, starting transfers between devices, within_chip(): lax.ppermute(array, AXES, [(i, i + 1 - 2 * (i % 2)) for i in range(size)])  6.9 us
    ppermute x2, starting transfers between devices, between_chips(): return lax.ppermute(array, AXES, pairs)  6.43 us
    pallas_call x1, Pallas kernels, body(): pl.pallas_call(functools.partial(early_kernel, early), out_shape=jax.Shap...  3.64 us
    pallas_call x1, Pallas kernels, body(): pl.pallas_call(functools.partial(late_kernel, late, size), out_shape=(jax...  3.19 us
    ppermute x2, starting transfers between devices, across(): lax.ppermute(array, AXES, [(i, j) for i, j in pairs if 0 <= j < size])  2.64 us
    ppermute x2, waiting for transfers between devices, between_chips(): return lax.ppermute(array, AXES, pairs)  2.42 us
  transfers between devices with their start and end apart: 6, of which 2 were waited for; matrix products, arithmetic and copies ran while one was open for 0% of the time, Pallas kernels for 5%

profile of v7, /device:TPU:1, one launch (start us, length us, event | category | flops | bytes accessed | tf_op | source)
XLA Modules:
  0.0 73.6 jit_solution(4617737364320712431)
XLA Ops:
  0.6 0.0 copy-start
  0.6 0.0 copy-start.1
  0.7 2.0 %bands.1 = (f32[1296,128]{1,0:T(8,128)S(1)}, f32[1296,128]{1,0:T(8,128)S(1)}) custom-call(f32[16,64,448]{2,1,0:T(8,128)} %op_ref.1, s32[6,16]{1,0:T(8,128)} %bitcast.21, s32[16]{0:T(128)} %valid_ref.1, f32[8,128]{1,0:T(8,128)} %bitcast.16, f32[8,128]{1,0:T(8,128)} %bitcast.22), custom_call_target="tpu_custom_call" | custom-call | tf_op jit(solution)/shard_map/bands/pallas_call | solution.py:386
  2.7 4.5 %collective-permute-start.4 = (f32[1296,128]{1,0:T(8,128)S(1)}, f32[1296,128]{1,0:T(8,128)S(1)}, u32[]{:S(2)}, u32[]{:S(2)}) collective-permute-start(f32[1296,128]{1,0:T(8,128)S(1)} %get-tuple-element.10.own_outer), channel_id=1, source_target_pairs={{1,2},{2,1},{3,4},{4,3},{5,6},{6,5},{7,8},{8,7},{9,10},{10,9},{11,... | collective-permute-start | bytes 1990664 | tf_op jit(solution)/shard_map/ppermute | solution.py:25
  7.2 5.0 %collective-permute-start.2 = (f32[1296,128]{1,0:T(8,128)S(1)}, f32[1296,128]{1,0:T(8,128)S(1)}, u32[]{:S(2)}, u32[]{:S(2)}) collective-permute-start(f32[1296,128]{1,0:T(8,128)S(1)} %get-tuple-element.10.own_outer), channel_id=1, source_target_pairs={{0,1},{1,0},{2,3},{3,2},{4,5},{5,4},{6,7},{7,6},{8,9},{9,8},{10,11... | collective-permute-start | bytes 1990664 | tf_op jit(solution)/shard_map/ppermute | solution.py:30
  12.2 1.9 %collective-permute-start.3 = (f32[1296,128]{1,0:T(8,128)S(1)}, f32[1296,128]{1,0:T(8,128)S(1)}, u32[]{:S(2)}, u32[]{:S(2)}) collective-permute-start(f32[1296,128]{1,0:T(8,128)S(1)} %get-tuple-element.11.own_inner), channel_id=1, source_target_pairs={{0,1},{1,0},{2,3},{3,2},{4,5},{5,4},{6,7},{7,6},{8,9},{9,8},{10,11... | collective-permute-start | bytes 1990664 | tf_op jit(solution)/shard_map/ppermute | solution.py:30
  14.1 1.9 %collective-permute-start.5 = (f32[1296,128]{1,0:T(8,128)S(1)}, f32[1296,128]{1,0:T(8,128)S(1)}, u32[]{:S(2)}, u32[]{:S(2)}) collective-permute-start(f32[1296,128]{1,0:T(8,128)S(1)} %get-tuple-element.11.own_inner), channel_id=1, source_target_pairs={{1,2},{2,1},{3,4},{4,3},{5,6},{6,5},{7,8},{8,7},{9,10},{10,9},{11,... | collective-permute-start | bytes 1990664 | tf_op jit(solution)/shard_map/ppermute | solution.py:25
  16.0 0.0 copy-done
  16.1 1.3 %collective-permute-start.1 = (f32[8,128]{1,0:T(8,128)S(1)}, f32[8,128]{1,0:T(8,128)S(1)}, u32[]{:S(2)}, u32[]{:S(2)}) collective-permute-start(f32[8,128]{1,0:T(8,128)S(1)} %bitcast.17), channel_id=1, source_target_pairs={{1,3},{2,0},{3,5},{4,2},{5,7},{6,4},{7,9},{8,6},{9,11},{10,8},{11,... | collective-permute-start | bytes 12296 | tf_op jit(solution)/shard_map/ppermute | solution.py:36
  17.4 0.0 collective-permute-done.4.near_ref
  17.4 1.3 %collective-permute-start = (f32[8,128]{1,0:T(8,128)S(1)}, f32[8,128]{1,0:T(8,128)S(1)}, u32[]{:S(2)}, u32[]{:S(2)}) collective-permute-start(f32[8,128]{1,0:T(8,128)S(1)} %bitcast.18), channel_id=1, source_target_pairs={{0,2},{2,4},{3,1},{4,6},{5,3},{6,8},{7,5},{8,10},{9,7},{10,12},{11... | collective-permute-start | bytes 12296 | tf_op jit(solution)/shard_map/ppermute | solution.py:36
  18.7 0.0 collective-permute-done.2.other_far
  18.7 0.0 collective-permute-done.3.other_near
  18.7 0.0 copy-done.1
  18.7 3.6 %early.1.early_ref = f32[704,128]{1,0:T(8,128)S(1)} custom-call(f32[1296,128]{1,0:T(8,128)S(1)} %collective-permute-done.2.other_far, f32[1296,128]{1,0:T(8,128)S(1)} %collective-permute-done.3.other_near, f32[1296,128]{1,0:T(8,128)S(1)} %get-tuple-element.11.own_inner, f32[1296,128]{1,0:T(8,128)S(1)} %get-tuple-element.10.own_outer, ...), custom_call_target="tpu_custom_call" | custom-call | tf_op jit(solution)/shard_map/early/pallas_call | solution.py:405
  22.4 1.3 %collective-permute-done.1.far_inner = f32[8,128]{1,0:T(8,128)S(1)} collective-permute-done((f32[8,128]{1,0:T(8,128)S(1)}, f32[8,128]{1,0:T(8,128)S(1)}, u32[]{:S(2)}, u32[]{:S(2)}) %collective-permute-start.1) | collective-permute-done | bytes 4128 | tf_op jit(solution)/shard_map/ppermute | solution.py:36
  23.7 0.0 collective-permute-done.far_outer
  23.7 2.4 %collective-permute-done.5.rim_ref = f32[1296,128]{1,0:T(8,128)S(1)} collective-permute-done((f32[1296,128]{1,0:T(8,128)S(1)}, f32[1296,128]{1,0:T(8,128)S(1)}, u32[]{:S(2)}, u32[]{:S(2)}) %collective-permute-start.5) | collective-permute-done | bytes 663584 | tf_op jit(solution)/shard_map/ppermute | solution.py:25
  26.2 3.2 %late.1 = (f32[72,128]{1,0:T(8,128)S(1)}, f32[32,128]{1,0:T(8,128)S(1)}) custom-call(f32[8,128]{1,0:T(8,128)S(1)} %collective-permute-done.far_outer, f32[8,128]{1,0:T(8,128)S(1)} %collective-permute-done.1.far_inner, f32[1296,128]{1,0:T(8,128)S(1)} %collective-permute-done.2.other_far, f32[1296,128]{1,0:T(8,128)S(1)} %collective-permute-done.3.other_near, ...), custom_call_target="tpu_custom_call" | custom-call | tf_op jit(solution)/shard_map/late/pallas_call | solution.py:413
  29.3 15.7 %all_to_all.22 = f32[32,1,128]{2,1,0:T(1,128)S(1)} all-to-all(f32[32,1,128]{2,1,0:T(1,128)S(1)} %bitcast.20), channel_id=1, replica_groups=mesh['group'=16,'slab'=32] {'slab'}, dimensions={0} | all-to-all | bytes 32768 | tf_op jit(solution)/shard_map/all_to_all | solution.py:428
  45.1 27.0 %all_to_all.23 = f32[16,1,128]{2,1,0:T(1,128)S(1)} all-to-all(f32[16,1,128]{2,1,0:T(1,128)S(1)} %bitcast.15), channel_id=1, replica_groups=mesh['group'=16,'slab'=32] {'group'}, dimensions={0} | all-to-all | bytes 16384 | tf_op jit(solution)/shard_map/all_to_all | solution.py:437
  72.1 1.5 %finish.1 = (f32[8,128]{1,0:T(8,128)}, f32[8,128]{1,0:T(8,128)}, f32[9,9]{1,0:T(8,128)}) custom-call(f32[16,128]{1,0:T(8,128)S(1)} %bitcast.14, f32[72,128]{1,0:T(8,128)S(1)} %get-tuple-element.13.basis_ref, f32[8,128]{1,0:T(8,128)S(1)} %bitcast.19, f32[8]{0:T(128)S(1)} %copy-done.1), custom_call_target="tpu_custom_call" | custom-call | tf_op jit(solution)/shard_map/finish/pallas_call | solution.py:438
  (1 shorter events, 0.0 us)
Async XLA Ops:
  0.6 15.4 %copy-start = (f32[1024]{0:T(1024)S(1)}, f32[1024]{0:T(1024)}, u32[]{:S(2)}) copy-start(f32[1024]{0:T(1024)} %param.10) | copy-start | bytes 12292
  0.6 18.1 %copy-start.1 = (f32[8]{0:T(128)S(1)}, f32[8]{0:T(128)}, u32[]{:S(2)}) copy-start(f32[8]{0:T(128)} %shifts_ref.5) | copy-start | bytes 100
  2.7 14.7 %collective-permute-start.4 = (f32[1296,128]{1,0:T(8,128)S(1)}, f32[1296,128]{1,0:T(8,128)S(1)}, u32[]{:S(2)}, u32[]{:S(2)}) collective-permute-start(f32[1296,128]{1,0:T(8,128)S(1)} %get-tuple-element.10.own_outer), channel_id=1, source_target_pairs={{1,2},{2,1},{3,4},{4,3},{5,6},{6,5},{7,8},{8,7},{9,10},{10,9},{11,... | collective-permute-start | bytes 1990664 | tf_op jit(solution)/shard_map/ppermute | solution.py:25
  7.2 11.5 %collective-permute-start.2 = (f32[1296,128]{1,0:T(8,128)S(1)}, f32[1296,128]{1,0:T(8,128)S(1)}, u32[]{:S(2)}, u32[]{:S(2)}) collective-permute-start(f32[1296,128]{1,0:T(8,128)S(1)} %get-tuple-element.10.own_outer), channel_id=1, source_target_pairs={{0,1},{1,0},{2,3},{3,2},{4,5},{5,4},{6,7},{7,6},{8,9},{9,8},{10,11... | collective-permute-start | bytes 1990664 | tf_op jit(solution)/shard_map/ppermute | solution.py:30
  12.2 6.5 %collective-permute-start.3 = (f32[1296,128]{1,0:T(8,128)S(1)}, f32[1296,128]{1,0:T(8,128)S(1)}, u32[]{:S(2)}, u32[]{:S(2)}) collective-permute-start(f32[1296,128]{1,0:T(8,128)S(1)} %get-tuple-element.11.own_inner), channel_id=1, source_target_pairs={{0,1},{1,0},{2,3},{3,2},{4,5},{5,4},{6,7},{7,6},{8,9},{9,8},{10,11... | collective-permute-start | bytes 1990664 | tf_op jit(solution)/shard_map/ppermute | solution.py:30
  14.1 12.0 %collective-permute-start.5 = (f32[1296,128]{1,0:T(8,128)S(1)}, f32[1296,128]{1,0:T(8,128)S(1)}, u32[]{:S(2)}, u32[]{:S(2)}) collective-permute-start(f32[1296,128]{1,0:T(8,128)S(1)} %get-tuple-element.11.own_inner), channel_id=1, source_target_pairs={{1,2},{2,1},{3,4},{4,3},{5,6},{6,5},{7,8},{8,7},{9,10},{10,9},{11,... | collective-permute-start | bytes 1990664 | tf_op jit(solution)/shard_map/ppermute | solution.py:25
  16.1 7.7 %collective-permute-start.1 = (f32[8,128]{1,0:T(8,128)S(1)}, f32[8,128]{1,0:T(8,128)S(1)}, u32[]{:S(2)}, u32[]{:S(2)}) collective-permute-start(f32[8,128]{1,0:T(8,128)S(1)} %bitcast.17), channel_id=1, source_target_pairs={{1,3},{2,0},{3,5},{4,2},{5,7},{6,4},{7,9},{8,6},{9,11},{10,8},{11,... | collective-permute-start | bytes 12296 | tf_op jit(solution)/shard_map/ppermute | solution.py:36
  17.4 6.3 %collective-permute-start = (f32[8,128]{1,0:T(8,128)S(1)}, f32[8,128]{1,0:T(8,128)S(1)}, u32[]{:S(2)}, u32[]{:S(2)}) collective-permute-start(f32[8,128]{1,0:T(8,128)S(1)} %bitcast.18), channel_id=1, source_target_pairs={{0,2},{2,4},{3,1},{4,6},{5,3},{6,8},{7,5},{8,10},{9,7},{10,12},{11... | collective-permute-start | bytes 12296 | tf_op jit(solution)/shard_map/ppermute | solution.py:36

commit v8 on v6

v8 whole, which is shorter than its diff:
```python
import functools

import jax
import jax.numpy as jnp
from jax import lax
from jax.experimental import pallas as pl
from jax.experimental.pallas import tpu as pltpu
from jax.sharding import PartitionSpec as P

AXES = ("group", "slab")
WIDTH = 64
LANES = 128
REACH = 2
BANDS = 2 * REACH + 1
HALF = WIDTH // 2
ROWS = BANDS * HALF
CHUNK = 4
GROUP = 8
RIM = 2
BODY = 10
INNER = 12
PAD = 4
LEVEL = 56


def between_chips(array):
    size = lax.axis_size(AXES)
    pairs = [(i, i + 1 if i % 2 else i - 1) for i in range(1, size - 1)]
    return lax.ppermute(array, AXES, pairs)


def within_chip(array):
    size = lax.axis_size(AXES)
    return lax.ppermute(array, AXES, [(i, i + 1 - 2 * (i % 2)) for i in range(size)])


def lane_ids(rows):
    return lax.broadcasted_iota(jnp.int32, (rows, LANES), 1)


def band_kernel(
    op_ref, adjacency_ref, valid_ref, start_ref, rhs_ref, rim_ref, body_ref, inner_ref,
    held, adj_ref, counts_ref, in_sems, other_sems,
):
    elems, _, columns = op_ref.shape
    faces = columns // WIDTH - 1
    chunks = elems // CHUNK
    device = lax.axis_index(AXES)
    base = device * elems
    second = device % 2
    left = lane_ids(HALF) < WIDTH

    def origin(chunk):
        return jnp.where(second == 1, elems - CHUNK * (chunk + 1), CHUNK * chunk)

    def arriving(chunk):
        part = pl.ds(origin(chunk), CHUNK)
        return pltpu.make_async_copy(op_ref.at[part], held.at[part], in_sems.at[chunk])

    for chunk in range(chunks):
        arriving(chunk).start()
    scalars = [
        pltpu.make_async_copy(adjacency_ref, adj_ref, other_sems.at[0]),
        pltpu.make_async_copy(valid_ref, counts_ref, other_sems.at[1]),
    ]
    extras = []
    for number, source in enumerate((start_ref, rhs_ref)):
        for place, (target, size) in enumerate(((rim_ref, RIM), (inner_ref, INNER))):
            rows = pl.ds(size * ROWS + 8 * number, 8)
            sem = other_sems.at[2 + 2 * number + place]
            extras.append(pltpu.make_async_copy(source, target.at[rows, :], sem))
    for copy in scalars + extras:
        copy.start()
    for copy in scalars:
        copy.wait()

    def one(e, targets):
        blocks = []
        for tile in range(columns // LANES):
            lanes = pl.ds(tile * LANES, LANES)
            top = held[e, pl.ds(0, HALF), lanes]
            low = held[e, pl.ds(HALF, HALF), lanes]
            blocks.append(jnp.where(left, top, pltpu.roll(low, WIDTH, 1)))
            blocks.append(jnp.where(left, pltpu.roll(top, WIDTH, 1), low))
        if columns % LANES:
            lanes = pl.ds(columns - WIDTH, WIDTH)
            top = held[e, pl.ds(0, HALF), lanes]
            low = held[e, pl.ds(HALF, HALF), lanes]
            blocks.append(jnp.concatenate([top, low], axis=1))
        count = counts_ref[e]
        place = []
        for face in range(faces):
            offset = adj_ref[face, e] - (base + e) + REACH
            place.append(jnp.where(face < count, offset, -1))
        for band in range(BANDS):
            total = blocks[0] if band == REACH else None
            if band != REACH:
                for face in range(faces):
                    weight = jnp.where(place[face] == band, jnp.float32(1), jnp.float32(0))
                    term = blocks[face + 1] * weight
                    total = term if total is None else total + term
            for target, at in targets:
                target[pl.ds(pl.multiple_of(at * ROWS + band * HALF, HALF), HALF), :] = total

    in_body = jnp.where(second == 1, elems - RIM - BODY, RIM)
    in_inner = jnp.where(second == 1, 0, elems - INNER)
    arriving(0).wait()
    for k in range(RIM):
        e = jnp.where(second == 1, elems - RIM, 0) + k
        one(e, [(rim_ref, k)])
    for k in range(CHUNK - RIM):
        e = jnp.where(second == 1, elems - CHUNK, RIM) + k
        one(e, [(body_ref, e - in_body)])

    def some(chunk, carry):
        arriving(chunk).wait()
        for k in range(CHUNK):
            e = origin(chunk) + k
            one(e, [(body_ref, e - in_body), (inner_ref, e - in_inner)])
        return carry

    lax.fori_loop(1, chunks - 1, some, 0)
    arriving(chunks - 1).wait()
    for k in range(CHUNK):
        e = origin(chunks - 1) + k
        one(e, [(inner_ref, e - in_inner)])
    for extra in extras:
        extra.wait()


def stacked_sums(terms, row):
    for span in (4, 2, 1):
        low = (row & span) == 0
        half = len(terms) // 2
        merged = []
        for a, b in zip(terms[:half], terms[half:]):
            kept = jnp.where(low, a, b)
            if span == 4:
                moved = pltpu.roll(jnp.where(low, b, a), 4, 0)
            else:
                moved = jnp.where(low, pltpu.roll(a, 8 - span, 0), pltpu.roll(b, span, 0))
            merged.append(kept + moved)
        terms = merged
    return terms[0]


def spread(ref, at, packed):
    left = lane_ids(8) < WIDTH
    turned = pltpu.roll(packed, WIDTH, 1)
    ref[pl.ds(at, 8, stride=2), :] = jnp.where(left, packed, turned)
    ref[pl.ds(at + 1, 8, stride=2), :] = jnp.where(left, turned, packed)


def times(find, place, vecs, at):
    row = lax.broadcasted_iota(jnp.int32, (8, LANES), 0)
    half = lane_ids(HALF)
    left = half < WIDTH
    spot = half % WIDTH - lax.broadcasted_iota(jnp.int32, (HALF, LANES), 0)
    near = [vecs[pl.ds(at + (k - REACH), 1), :] for k in range(GROUP + 2 * REACH)]
    terms = []
    for k in range(GROUP):
        ref, spare = find(place + k)
        total = None
        for band in range(BANDS):
            rows = pl.ds(spare * ROWS + band * HALF, HALF)
            term = ref[rows, :] * near[k + band]
            total = term if total is None else total + term
        top = jnp.sum(jnp.where(left, total, 0.0), axis=1, keepdims=True)
        low = jnp.sum(jnp.where(left, 0.0, total), axis=1, keepdims=True)
        placed = jnp.where(spot == 0, top, jnp.where(spot == HALF, low, 0.0))
        terms.append(jnp.sum(placed.reshape(HALF // 8, 8, LANES), axis=0))
    return stacked_sums(terms, row)


def row_of(place):
    return PAD + 2 * GROUP + place


def application(at, find, places, vecs, combine):
    made = []
    for place in places:
        fresh = times(find, place, vecs, at + row_of(place))
        made.append((row_of(place), combine(fresh, row_of(place))))
    for row, value in made:
        vecs[pl.ds(at + LEVEL + row, 8), :] = value


def by_core(run):
    second = lax.axis_index(AXES) % 2 == 1
    pl.when(second)(lambda: run(True))
    pl.when(jnp.logical_not(second))(lambda: run(False))


def finder(turned, rim, body, inner, far_rim, far_body, far_inner):
    def find(place):
        out = 15 - place if turned else place
        if out < -RIM:
            ref, first, size = far_body, -RIM - BODY, BODY
        elif out < 0:
            ref, first, size = far_rim, -RIM, RIM
        elif out < RIM:
            ref, first, size = rim, 0, RIM
        elif out < 16 - INNER:
            ref, first, size = body, RIM, BODY
        elif out < 16:
            ref, first, size = inner, 16 - INNER, INNER
        else:
            ref, first, size = far_inner, 16, INNER
        spare = out - first
        assert 0 <= spare < size
        return ref, size - 1 - spare if turned else spare

    return find


def packed_rows(vecs, level):
    left = lane_ids(8) < WIDTH
    at = level * LEVEL + row_of(0)
    return jnp.where(left, vecs[pl.ds(at, 8, stride=2), :], vecs[pl.ds(at + 1, 8, stride=2), :])


def early_kernel(rim, body, inner, far_rim, far_inner, shifts_ref, basis_ref, last_ref, vecs):
    def run(turned):
        find = finder(turned, rim, body, inner, far_rim, None, far_inner)
        tails = [(far_rim, RIM), (rim, RIM), (far_inner, INNER)]
        for part, (ref, size) in enumerate(tails[::-1] if turned else tails):
            at = PAD + part * 2 * GROUP
            spread(vecs, at, ref[pl.ds(size * ROWS, 8), :])
            spread(vecs, 3 * LEVEL + at, ref[pl.ds(size * ROWS + 8, 8), :])
        places = [GROUP * k + (-6 if turned else -2) for k in range(3)]
        application(
            0, find, places, vecs, lambda fresh, row: vecs[pl.ds(3 * LEVEL + row, 8), :] - fresh
        )
        shift = shifts_ref[0]
        application(
            LEVEL, find, (0, GROUP), vecs, lambda fresh, row: fresh - shift * vecs[pl.ds(LEVEL + row, 8), :]
        )

    by_core(run)
    basis_ref[pl.ds(0, 8), :] = packed_rows(vecs, 1)
    last = packed_rows(vecs, 2)
    basis_ref[pl.ds(8, 8), :] = last
    last_ref[...] = last


def late_kernel(
    size, vec_inner, vec_outer, rim, body, inner, far_rim, far_inner, far_body,
    early_ref, shifts_ref, basis_ref, gram_ref, vecs,
):
    known = early_ref.shape[0] // 8

    def run(turned):
        find = finder(turned, rim, body, inner, far_rim, far_body, far_inner)
        vectors = [vec_outer[...], early_ref[pl.ds(8 * known - 8, 8), :], vec_inner[...]]
        for part, vector in enumerate(vectors[::-1] if turned else vectors):
            spread(vecs, PAD + part * 2 * GROUP, vector)

        def turn(index, carry, places):
            at = pl.multiple_of((index - known) * LEVEL, 8)
            shift = shifts_ref[index - 1]
            application(
                at, find, places, vecs, lambda fresh, row: fresh - shift * vecs[pl.ds(at + row, 8), :]
            )
            return carry

        wide = [GROUP * k - RIM - BODY for k in range(5)]
        narrow = wide[1:4]
        split = next(k for k in range(known, size) if REACH * (size - 1 - k) <= -narrow[0])
        lax.fori_loop(known, split, functools.partial(turn, places=wide), 0)
        lax.fori_loop(split, size, functools.partial(turn, places=narrow), 0)

    by_core(run)
    rows = [early_ref[pl.ds(8 * k, 8), :] for k in range(known)]
    rows += [packed_rows(vecs, k - known + 1) for k in range(known, size)]
    for k in range(size):
        basis_ref[pl.ds(8 * k, 8), :] = rows[k]
    lane = lane_ids(8)
    total = jnp.zeros((8, LANES), jnp.float32)
    number = 0
    for i in range(size):
        for j in range(i, size):
            entry = jnp.sum(rows[i] * rows[j], axis=1, keepdims=True)
            total = jnp.where(lane == number, entry, total)
            number += 1
    gram = jnp.sum(total, axis=0, keepdims=True)
    gram_ref[...] = jnp.broadcast_to(gram, gram_ref.shape)


def partial_kernel(parts_ref, out_ref):
    total = jnp.sum(parts_ref[...], axis=0, keepdims=True)
    out_ref[...] = jnp.broadcast_to(total, out_ref.shape)


def inverse_root(value):
    guess = lax.rsqrt(value)
    return guess * (1.5 - 0.5 * value * guess * guess)


def finish_kernel(count, steps, parts_ref, basis_ref, start_ref, shifts_ref, sol_ref, res_ref, upper_ref):
    size = steps + 1
    lane = lane_ids(8)
    summed = jnp.broadcast_to(jnp.sum(parts_ref[...], axis=0, keepdims=True), (8, LANES))
    gram = {}
    number = 0
    for i in range(size):
        for j in range(i, size):
            entry = jnp.sum(jnp.where(lane == number, summed, 0.0), axis=1, keepdims=True)
            gram[i, j] = jnp.broadcast_to(entry, (8, LANES))
            number += 1
    factor = {}
    for k in range(size):
        turn = inverse_root(gram[k, k])
        for j in range(k, size):
            factor[k, j] = gram[k, j] * turn
        for i in range(k + 1, size):
            for j in range(i, size):
                gram[i, j] = gram[i, j] - factor[k, i] * factor[k, j]
    hess = {}
    for k in range(steps):
        for i in range(k + 1):
            hess[i, k] = factor[i, k] * shifts_ref[k] + factor[i, k + 1]
        hess[k + 1, k] = factor[k + 1, k + 1]
    target = [factor[0, 0]] + [jnp.zeros((8, LANES), jnp.float32)] * steps
    inverse = []
    for k in range(steps):
        a, b = hess[k, k], hess[k + 1, k]
        scale = inverse_root(a * a + b * b)
        cos, sin = a * scale, b * scale
        inverse.append(scale)
        for j in range(k + 1, steps):
            up, down = hess[k, j], hess[k + 1, j]
            hess[k, j] = cos * up + sin * down
            hess[k + 1, j] = cos * down - sin * up
        target[k], target[k + 1] = cos * target[k], -(sin * target[k])
    coeffs = [None] * steps
    for k in range(steps - 1, -1, -1):
        value = target[k]
        for j in range(k + 1, steps):
            value = value - hess[k, j] * coeffs[j]
        coeffs[k] = value * inverse[k]
    rows = [basis_ref[pl.ds(8 * k, 8), :] for k in range(size)]
    sol, res = 0.0, 0.0
    for k in range(steps):
        sol = sol + coeffs[k] * rows[k]
        res = res + coeffs[k] * (rows[k + 1] + shifts_ref[k] * rows[k])
    sol_ref[...] = start_ref[...] + sol
    res_ref[...] = rows[0] - res
    wide = lane_ids(16)
    tall = lax.broadcasted_iota(jnp.int32, (16, LANES), 0)
    scale = 1.0 / (count ** 0.5)
    upper = jnp.zeros((16, LANES), jnp.float32)
    for i in range(size):
        for j in range(i, size):
            entry = jnp.concatenate([factor[i, j]] * 2, axis=0) * scale
            upper = jnp.where((wide == j) & (tall == i), entry, upper)
    upper_ref[...] = upper[:size, :size]


def body(operator, adjacency, counts, rhs, start, shifts):
    elems, width, columns = operator.shape
    steps = shifts.shape[0]
    devices = lax.axis_size(AXES)
    slabs = lax.axis_size("slab")
    groups = lax.axis_size("group")
    packed = elems * width // LANES
    size = steps + 1
    vmem = pl.BlockSpec(memory_space=pltpu.VMEM)
    smem = pl.BlockSpec(memory_space=pltpu.SMEM)
    hbm = pl.BlockSpec(memory_space=pl.ANY)
    mebi = 1024 * 1024
    f32 = jnp.float32

    x = start.reshape(packed, LANES)
    b = rhs.reshape(packed, LANES)
    sources = (operator, adjacency.T, counts, x, b)
    made = (RIM * ROWS + 2 * packed, BODY * ROWS, INNER * ROWS + 2 * packed)
    rim, middle, inner = pl.pallas_call(
        band_kernel,
        out_shape=tuple(pltpu.VMEM((rows, LANES), f32) for rows in made),
        in_specs=[hbm] * 5,
        out_specs=(vmem, vmem, vmem),
        scratch_shapes=[
            pltpu.VMEM(operator.shape, f32),
            pltpu.SMEM(adjacency.T.shape, jnp.int32),
            pltpu.SMEM(counts.shape, jnp.int32),
            pltpu.SemaphoreType.DMA((elems // CHUNK,)),
            pltpu.SemaphoreType.DMA((6,)),
        ],
        compiler_params=pltpu.CompilerParams(vmem_limit_bytes=16 * mebi),
        name="bands",
    )(*(pltpu.with_memory_space_constraint(source, pltpu.HBM) for source in sources))
    far_rim = between_chips(rim)
    far_body = between_chips(middle)
    far_inner = within_chip(inner)
    first, last = pl.pallas_call(
        early_kernel,
        out_shape=(
            jax.ShapeDtypeStruct((16, LANES), f32),
            jax.ShapeDtypeStruct((packed, LANES), f32),
        ),
        in_specs=[vmem] * 5 + [smem],
        out_specs=(vmem, vmem),
        scratch_shapes=[pltpu.VMEM((4 * LEVEL, LANES), f32)],
        compiler_params=pltpu.CompilerParams(vmem_limit_bytes=16 * mebi),
        cost_estimate=pl.CostEstimate(flops=20 * 10**9, bytes_accessed=0, transcendentals=0),
        name="early",
    )(rim, middle, inner, far_rim, far_inner, shifts)
    basis, gram = pl.pallas_call(
        functools.partial(late_kernel, size),
        out_shape=(
            jax.ShapeDtypeStruct((8 * size, LANES), f32),
            jax.ShapeDtypeStruct((slabs, LANES), f32),
        ),
        in_specs=[vmem] * 9 + [smem],
        out_specs=(vmem, vmem),
        scratch_shapes=[pltpu.VMEM(((size - 1) * LEVEL, LANES), f32)],
        compiler_params=pltpu.CompilerParams(vmem_limit_bytes=16 * mebi),
        name="late",
    )(
        within_chip(last), between_chips(last), rim, middle, inner, far_rim, far_inner, far_body,
        first, shifts,
    )
    parts = lax.all_to_all(gram, "slab", 0, 0, tiled=True)
    parts = pl.pallas_call(
        partial_kernel,
        out_shape=jax.ShapeDtypeStruct((groups, LANES), f32),
        in_specs=[vmem],
        out_specs=vmem,
        compiler_params=pltpu.CompilerParams(vmem_limit_bytes=4 * mebi),
        name="partial",
    )(parts)
    parts = lax.all_to_all(parts, "group", 0, 0, tiled=True)
    sol, res, upper = pl.pallas_call(
        functools.partial(finish_kernel, devices * elems * width, steps),
        out_shape=(
            jax.ShapeDtypeStruct((packed, LANES), f32),
            jax.ShapeDtypeStruct((packed, LANES), f32),
            jax.ShapeDtypeStruct((steps + 1, steps + 1), f32),
        ),
        in_specs=[vmem, vmem, vmem, smem],
        out_specs=(vmem, vmem, vmem),
        compiler_params=pltpu.CompilerParams(vmem_limit_bytes=4 * mebi),
        name="finish",
    )(parts, basis, x, shifts)
    return (sol.reshape(-1), res.reshape(-1), upper)


def solution(mesh):
    split = P(AXES)
    return jax.shard_map(
        body,
        mesh=mesh,
        in_specs=(P(AXES, None, None), P(AXES, None), split, split, split, P()),
        out_specs=(split, split, P()),
        check_vma=False,
    )
```

time: 78.3 us -> 73.1 us (0.934)
  waiting for transfers between devices: 11.2 us -> 5.07 us
  starting transfers between devices: 14.6 us -> 18.2 us
  blocking collectives: 43.6 us -> 40.8 us
    ppermute x2 -> x3, waiting for transfers between devices: 11.1 us -> 5.07 us  [between_chips(): return lax.ppermute(array, AXES, pairs)]
    ppermute x2 -> x3, starting transfers between devices: 3.85 us -> 7.48 us  [between_chips(): return lax.ppermute(array, AXES, pairs)]
    all_to_all x1, blocking collectives: 16.5 us -> 13.7 us  [body(): parts = lax.all_to_all(gram, 'slab', 0, 0, tiled=True)]
  transfers between devices with their start and end apart: 4 -> 5, of which waited for: 3 -> 2; matrix products, arithmetic and copies ran while one was open for 0% -> 0% of each run, Pallas kernels for 0% -> 2%
where the time goes in v8:
time: 73.1 us; the launch traced here: 72.8 us
  blocking collectives  40.8 us (56%)
  starting transfers between devices  18.2 us (25%)
  Pallas kernels  8.03 us (11%)
  waiting for transfers between devices  5.07 us (7%)
    all_to_all x1, blocking collectives, body(): parts = lax.all_to_all(parts, 'group', 0, 0, tiled=True)  27.1 us
    all_to_all x1, blocking collectives, body(): parts = lax.all_to_all(gram, 'slab', 0, 0, tiled=True)  13.7 us
    ppermute x2, starting transfers between devices, within_chip(): lax.ppermute(array, AXES, [(i, i + 1 - 2 * (i % 2)) for i in range(size)])  10.7 us
    ppermute x3, starting transfers between devices, between_chips(): return lax.ppermute(array, AXES, pairs)  7.48 us
    ppermute x3, waiting for transfers between devices, between_chips(): return lax.ppermute(array, AXES, pairs)  5.07 us
    pallas_call x1, Pallas kernels, body(): pl.pallas_call(functools.partial(late_kernel, size), out_shape=(jax.Shape...  3.41 us
    pallas_call x1, Pallas kernels, body(): pl.pallas_call(band_kernel, out_shape=tuple((pltpu.VMEM((rows, LANES), f3...  2.03 us
    pallas_call x1, Pallas kernels, body(): pl.pallas_call(functools.partial(finish_kernel, devices * elems * width,...  1.48 us
  transfers between devices with their start and end apart: 5, of which 2 were waited for; matrix products, arithmetic and copies ran while one was open for 0% of the time, Pallas kernels for 2%

profile of v8, /device:TPU:1, one launch (start us, length us, event | category | flops | bytes accessed | tf_op | source)
XLA Modules:
  0.0 72.8 jit_solution(2600297739705602710)
XLA Ops:
  0.6 0.0 copy-start.1
  0.6 2.0 %bands.1 = (f32[336,128]{1,0:T(8,128)S(1)}, f32[1600,128]{1,0:T(8,128)S(1)}, f32[1936,128]{1,0:T(8,128)S(1)}) custom-call(f32[16,64,448]{2,1,0:T(8,128)} %op_ref.1, s32[6,16]{1,0:T(8,128)} %bitcast.19, s32[16]{0:T(128)} %valid_ref.1, f32[8,128]{1,0:T(8,128)} %bitcast.16, f32[8,128]{1,0:T(8,128)} %bitcast.20), custom_call_target="tpu_custom_call" | custom-call | tf_op jit(solution)/shard_map/bands/pallas_call | solution.py:377
  2.7 8.8 %collective-permute-start.1 = (f32[1936,128]{1,0:T(8,128)S(1)}, f32[1936,128]{1,0:T(8,128)S(1)}, u32[]{:S(2)}, u32[]{:S(2)}) collective-permute-start(f32[1936,128]{1,0:T(8,128)S(1)} %get-tuple-element.15.inner), channel_id=1, source_target_pairs={{0,1},{1,0},{2,3},{3,2},{4,5},{5,4},{6,7},{7,6},{8,9},{9,8},{10,11... | collective-permute-start | bytes 2973704 | tf_op jit(solution)/shard_map/ppermute | solution.py:34
  11.5 1.9 %collective-permute-start = (f32[336,128]{1,0:T(8,128)S(1)}, f32[336,128]{1,0:T(8,128)S(1)}, u32[]{:S(2)}, u32[]{:S(2)}) collective-permute-start(f32[336,128]{1,0:T(8,128)S(1)} %get-tuple-element.13.rim), channel_id=1, source_target_pairs={{1,2},{2,1},{3,4},{4,3},{5,6},{6,5},{7,8},{8,7},{9,10},{10,9},{11,... | collective-permute-start | bytes 516104 | tf_op jit(solution)/shard_map/ppermute | solution.py:29
  13.4 3.6 %collective-permute-start.4 = (f32[1600,128]{1,0:T(8,128)S(1)}, f32[1600,128]{1,0:T(8,128)S(1)}, u32[]{:S(2)}, u32[]{:S(2)}) collective-permute-start(f32[1600,128]{1,0:T(8,128)S(1)} %get-tuple-element.14.body), channel_id=1, source_target_pairs={{1,2},{2,1},{3,4},{4,3},{5,6},{6,5},{7,8},{8,7},{9,10},{10,9},{11,... | collective-permute-start | bytes 2457608 | tf_op jit(solution)/shard_map/ppermute | solution.py:29
  17.1 1.1 %collective-permute-done.far_rim = f32[336,128]{1,0:T(8,128)S(1)} collective-permute-done((f32[336,128]{1,0:T(8,128)S(1)}, f32[336,128]{1,0:T(8,128)S(1)}, u32[]{:S(2)}, u32[]{:S(2)}) %collective-permute-start) | collective-permute-done | bytes 172064 | tf_op jit(solution)/shard_map/ppermute | solution.py:29
  18.2 0.0 collective-permute-done.1.far_inner
  18.2 0.0 copy-done.1
  18.2 1.1 %early.1 = (f32[16,128]{1,0:T(8,128)S(1)}, f32[8,128]{1,0:T(8,128)S(1)}) custom-call(f32[336,128]{1,0:T(8,128)S(1)} %get-tuple-element.13.rim, f32[1600,128]{1,0:T(8,128)S(1)} %get-tuple-element.14.body, f32[1936,128]{1,0:T(8,128)S(1)} %get-tuple-element.15.inner, f32[336,128]{1,0:T(8,128)S(1)} %collective-permute-done.far_rim, ...), custom_call_target="tpu_custom_call" | custom-call | flops 20000000000 | tf_op jit(solution)/shard_map/early/pallas_call | solution.py:395
  19.3 0.0 copy-start
  19.3 1.9 %collective-permute-start.3 = (f32[8,128]{1,0:T(8,128)S(1)}, f32[8,128]{1,0:T(8,128)S(1)}, u32[]{:S(2)}, u32[]{:S(2)}) collective-permute-start(f32[8,128]{1,0:T(8,128)S(1)} %get-tuple-element.16), channel_id=1, source_target_pairs={{1,2},{2,1},{3,4},{4,3},{5,6},{6,5},{7,8},{8,7},{9,10},{10,9},{11,... | collective-permute-start | bytes 12296 | tf_op jit(solution)/shard_map/ppermute | solution.py:29
  21.3 1.9 %collective-permute-start.2 = (f32[8,128]{1,0:T(8,128)S(1)}, f32[8,128]{1,0:T(8,128)S(1)}, u32[]{:S(2)}, u32[]{:S(2)}) collective-permute-start(f32[8,128]{1,0:T(8,128)S(1)} %get-tuple-element.16), channel_id=1, source_target_pairs={{0,1},{1,0},{2,3},{3,2},{4,5},{5,4},{6,7},{7,6},{8,9},{9,8},{10,11... | collective-permute-start | bytes 12296 | tf_op jit(solution)/shard_map/ppermute | solution.py:34
  23.2 3.9 %collective-permute-done.4.far_body = f32[1600,128]{1,0:T(8,128)S(1)} collective-permute-done((f32[1600,128]{1,0:T(8,128)S(1)}, f32[1600,128]{1,0:T(8,128)S(1)}, u32[]{:S(2)}, u32[]{:S(2)}) %collective-permute-start.4) | collective-permute-done | bytes 819232 | tf_op jit(solution)/shard_map/ppermute | solution.py:29
  27.1 0.0 collective-permute-done.3.vec_outer
  27.1 0.0 collective-permute-done.2.vec_inner
  27.1 3.4 %late.1 = (f32[72,128]{1,0:T(8,128)S(1)}, f32[32,128]{1,0:T(8,128)S(1)}) custom-call(f32[8,128]{1,0:T(8,128)S(1)} %collective-permute-done.2.vec_inner, f32[8,128]{1,0:T(8,128)S(1)} %collective-permute-done.3.vec_outer, f32[336,128]{1,0:T(8,128)S(1)} %get-tuple-element.13.rim, f32[1600,128]{1,0:T(8,128)S(1)} %get-tuple-element.14.body, ...), custom_call_target="tpu_custom_call" | custom-call | tf_op jit(solution)/shard_map/late/pallas_call | solution.py:408
  30.5 13.7 %all_to_all.22 = f32[32,1,128]{2,1,0:T(1,128)S(1)} all-to-all(f32[32,1,128]{2,1,0:T(1,128)S(1)} %bitcast.18), channel_id=1, replica_groups=mesh['group'=16,'slab'=32] {'slab'}, dimensions={0} | all-to-all | bytes 32768 | tf_op jit(solution)/shard_map/all_to_all | solution.py:423
  44.2 27.1 %all_to_all.23 = f32[16,1,128]{2,1,0:T(1,128)S(1)} all-to-all(f32[16,1,128]{2,1,0:T(1,128)S(1)} %bitcast.15), channel_id=1, replica_groups=mesh['group'=16,'slab'=32] {'group'}, dimensions={0} | all-to-all | bytes 16384 | tf_op jit(solution)/shard_map/all_to_all | solution.py:432
  71.3 0.0 copy-done
  71.3 1.5 %finish.1 = (f32[8,128]{1,0:T(8,128)}, f32[8,128]{1,0:T(8,128)}, f32[9,9]{1,0:T(8,128)}) custom-call(f32[16,128]{1,0:T(8,128)S(1)} %bitcast.14, f32[72,128]{1,0:T(8,128)S(1)} %get-tuple-element.19.basis_ref, f32[8,128]{1,0:T(8,128)S(1)} %bitcast.17, f32[8]{0:T(128)S(1)} %copy-done.1), custom_call_target="tpu_custom_call" | custom-call | tf_op jit(solution)/shard_map/finish/pallas_call | solution.py:433
  (1 shorter events, 0.0 us)
Async XLA Ops:
  0.6 17.6 %copy-start.1 = (f32[8]{0:T(128)S(1)}, f32[8]{0:T(128)}, u32[]{:S(2)}) copy-start(f32[8]{0:T(128)} %shifts_ref.5) | copy-start | bytes 100
  2.7 15.5 %collective-permute-start.1 = (f32[1936,128]{1,0:T(8,128)S(1)}, f32[1936,128]{1,0:T(8,128)S(1)}, u32[]{:S(2)}, u32[]{:S(2)}) collective-permute-start(f32[1936,128]{1,0:T(8,128)S(1)} %get-tuple-element.15.inner), channel_id=1, source_target_pairs={{0,1},{1,0},{2,3},{3,2},{4,5},{5,4},{6,7},{7,6},{8,9},{9,8},{10,11... | collective-permute-start | bytes 2973704 | tf_op jit(solution)/shard_map/ppermute | solution.py:34
  11.5 6.7 %collective-permute-start = (f32[336,128]{1,0:T(8,128)S(1)}, f32[336,128]{1,0:T(8,128)S(1)}, u32[]{:S(2)}, u32[]{:S(2)}) collective-permute-start(f32[336,128]{1,0:T(8,128)S(1)} %get-tuple-element.13.rim), channel_id=1, source_target_pairs={{1,2},{2,1},{3,4},{4,3},{5,6},{6,5},{7,8},{8,7},{9,10},{10,9},{11,... | collective-permute-start | bytes 516104 | tf_op jit(solution)/shard_map/ppermute | solution.py:29
  13.4 13.7 %collective-permute-start.4 = (f32[1600,128]{1,0:T(8,128)S(1)}, f32[1600,128]{1,0:T(8,128)S(1)}, u32[]{:S(2)}, u32[]{:S(2)}) collective-permute-start(f32[1600,128]{1,0:T(8,128)S(1)} %get-tuple-element.14.body), channel_id=1, source_target_pairs={{1,2},{2,1},{3,4},{4,3},{5,6},{6,5},{7,8},{8,7},{9,10},{10,9},{11,... | collective-permute-start | bytes 2457608 | tf_op jit(solution)/shard_map/ppermute | solution.py:29
  19.3 52.0 %copy-start = (f32[1024]{0:T(1024)S(1)}, f32[1024]{0:T(1024)}, u32[]{:S(2)}) copy-start(f32[1024]{0:T(1024)} %param.10) | copy-start | bytes 12292
  19.3 7.8 %collective-permute-start.3 = (f32[8,128]{1,0:T(8,128)S(1)}, f32[8,128]{1,0:T(8,128)S(1)}, u32[]{:S(2)}, u32[]{:S(2)}) collective-permute-start(f32[8,128]{1,0:T(8,128)S(1)} %get-tuple-element.16), channel_id=1, source_target_pairs={{1,2},{2,1},{3,4},{4,3},{5,6},{6,5},{7,8},{8,7},{9,10},{10,9},{11,... | collective-permute-start | bytes 12296 | tf_op jit(solution)/shard_map/ppermute | solution.py:29
  21.3 5.9 %collective-permute-start.2 = (f32[8,128]{1,0:T(8,128)S(1)}, f32[8,128]{1,0:T(8,128)S(1)}, u32[]{:S(2)}, u32[]{:S(2)}) collective-permute-start(f32[8,128]{1,0:T(8,128)S(1)} %get-tuple-element.16), channel_id=1, source_target_pairs={{0,1},{1,0},{2,3},{3,2},{4,5},{5,4},{6,7},{7,6},{8,9},{9,8},{10,11... | collective-permute-start | bytes 12296 | tf_op jit(solution)/shard_map/ppermute | solution.py:34

commit v9 on v8

--- a/solution.py
+++ b/solution.py
@@ -16,10 +16,8 @@
 ROWS = BANDS * HALF
 CHUNK = 4
 GROUP = 8
-RIM = 2
-BODY = 10
-INNER = 12
-PAD = 4
+MOST = 14
+PAD = 6
 LEVEL = 56
 
 
@@ -34,12 +32,18 @@
     return lax.ppermute(array, AXES, [(i, i + 1 - 2 * (i % 2)) for i in range(size)])
 
 
+def across(array):
+    size = lax.axis_size(AXES)
+    pairs = [(i, i + 4 * (i % 2) - 2) for i in range(size)]
+    return lax.ppermute(array, AXES, [(i, j) for i, j in pairs if 0 <= j < size])
+
+
 def lane_ids(rows):
     return lax.broadcasted_iota(jnp.int32, (rows, LANES), 1)
 
 
 def band_kernel(
-    op_ref, adjacency_ref, valid_ref, start_ref, rhs_ref, rim_ref, body_ref, inner_ref,
+    op_ref, adjacency_ref, valid_ref, start_ref, rhs_ref, most_ref, outer_ref, inner_ref,
     held, adj_ref, counts_ref, in_sems, other_sems,
 ):
     elems, _, columns = op_ref.shape
@@ -65,7 +69,7 @@
     ]
     extras = []
     for number, source in enumerate((start_ref, rhs_ref)):
-        for place, (target, size) in enumerate(((rim_ref, RIM), (inner_ref, INNER))):
+        for place, (target, size) in enumerate(((most_ref, MOST), (inner_ref, GROUP))):
             rows = pl.ds(size * ROWS + 8 * number, 8)
             sem = other_sems.at[2 + 2 * number + place]
             extras.append(pltpu.make_async_copy(source, target.at[rows, :], sem))
@@ -102,28 +106,26 @@
             for target, at in targets:
                 target[pl.ds(pl.multiple_of(at * ROWS + band * HALF, HALF), HALF), :] = total
 
-    in_body = jnp.where(second == 1, elems - RIM - BODY, RIM)
-    in_inner = jnp.where(second == 1, 0, elems - INNER)
-    arriving(0).wait()
-    for k in range(RIM):
-        e = jnp.where(second == 1, elems - RIM, 0) + k
-        one(e, [(rim_ref, k)])
-    for k in range(CHUNK - RIM):
-        e = jnp.where(second == 1, elems - CHUNK, RIM) + k
-        one(e, [(body_ref, e - in_body)])
-
-    def some(chunk, carry):
+    in_most = jnp.where(second == 1, elems - MOST, 0)
+    in_outer = jnp.where(second == 1, GROUP, 0)
+    in_inner = GROUP - in_outer
+
+    def some(chunk, carry, target=outer_ref, start=in_outer):
         arriving(chunk).wait()
         for k in range(CHUNK):
             e = origin(chunk) + k
-            one(e, [(body_ref, e - in_body), (inner_ref, e - in_inner)])
+            one(e, [(most_ref, e - in_most), (target, e - start)])
         return carry
 
-    lax.fori_loop(1, chunks - 1, some, 0)
-    arriving(chunks - 1).wait()
+    lax.fori_loop(0, 2, some, 0)
+    some(2, 0, target=inner_ref, start=in_inner)
+    arriving(3).wait()
     for k in range(CHUNK):
-        e = origin(chunks - 1) + k
-        one(e, [(inner_ref, e - in_inner)])
+        e = jnp.where(second == 1, CHUNK - 1 - k, elems - CHUNK + k)
+        targets = [(inner_ref, e - in_inner)]
+        if k < MOST - 3 * CHUNK:
+            targets.append((most_ref, e - in_most))
+        one(e, targets)
     for extra in extras:
         extra.wait()
 
@@ -191,24 +193,15 @@
     pl.when(jnp.logical_not(second))(lambda: run(False))
 
 
-def finder(turned, rim, body, inner, far_rim, far_body, far_inner):
+def finder(turned, outer, inner, far_inner, far_outer, far_most):
+    arrays = ((far_most, -MOST, MOST), (outer, 0, 8), (inner, 8, 8), (far_inner, 16, 8), (far_outer, 24, 8))
+
     def find(place):
         out = 15 - place if turned else place
-        if out < -RIM:
-            ref, first, size = far_body, -RIM - BODY, BODY
-        elif out < 0:
-            ref, first, size = far_rim, -RIM, RIM
-        elif out < RIM:
-            ref, first, size = rim, 0, RIM
-        elif out < 16 - INNER:
-            ref, first, size = body, RIM, BODY
-        elif out < 16:
-            ref, first, size = inner, 16 - INNER, INNER
-        else:
-            ref, first, size = far_inner, 16, INNER
-        spare = out - first
-        assert 0 <= spare < size
-        return ref, size - 1 - spare if turned else spare
+        for ref, first, size in arrays:
+            if first <= out < first + size:
+                return ref, first + size - 1 - out if turned else out - first
+        raise ValueError(place)
 
     return find
 
@@ -219,59 +212,78 @@
     return jnp.where(left, vecs[pl.ds(at, 8, stride=2), :], vecs[pl.ds(at + 1, 8, stride=2), :])
 
 
-def early_kernel(rim, body, inner, far_rim, far_inner, shifts_ref, basis_ref, last_ref, vecs):
+def levels(plan, turned, find, vecs, shifts_ref):
+    given = vecs.shape[0] - LEVEL
+
+    def turn(index, carry, places):
+        at = pl.multiple_of(index * LEVEL, 8)
+        opening = index == 0
+        source = pl.multiple_of(jnp.where(opening, given, at), 8)
+        sign = jnp.where(opening, jnp.float32(-1), jnp.float32(1))
+        scale = jnp.where(opening, jnp.float32(1), -shifts_ref[jnp.maximum(index - 1, 0)])
+        application(
+            at, find, places, vecs,
+            lambda fresh, row: sign * fresh + scale * vecs[pl.ds(source + row, 8), :],
+        )
+        return carry
+
+    for first, last, places in plan:
+        if turned:
+            places = [8 - place for place in places]
+        if last - first == 1:
+            turn(jnp.int32(first), 0, places)
+        else:
+            lax.fori_loop(first, last, functools.partial(turn, places=places), 0)
+
+
+def two_rows(vecs, row, packed):
+    packed = jnp.broadcast_to(packed, (8, LANES))
+    turned = pltpu.roll(packed, WIDTH, 1)
+    left = lane_ids(8) < WIDTH
+    vecs[pl.ds(row, 1), :] = jnp.where(left, packed, turned)[:1]
+    vecs[pl.ds(row + 1, 1), :] = jnp.where(left, turned, packed)[:1]
+
+
+def early_kernel(plan, outer, inner, far_inner, far_outer, shifts_ref, vecs, opening_ref):
+    empty = jnp.zeros((8, LANES), jnp.float32)
+    for at in range(0, vecs.shape[0], 8):
+        vecs[pl.ds(at, 8), :] = empty
+    given = vecs.shape[0] - LEVEL
+
     def run(turned):
-        find = finder(turned, rim, body, inner, far_rim, None, far_inner)
-        tails = [(far_rim, RIM), (rim, RIM), (far_inner, INNER)]
-        for part, (ref, size) in enumerate(tails[::-1] if turned else tails):
-            at = PAD + part * 2 * GROUP
-            spread(vecs, at, ref[pl.ds(size * ROWS, 8), :])
-            spread(vecs, 3 * LEVEL + at, ref[pl.ds(size * ROWS + 8, 8), :])
-        places = [GROUP * k + (-6 if turned else -2) for k in range(3)]
-        application(
-            0, find, places, vecs, lambda fresh, row: vecs[pl.ds(3 * LEVEL + row, 8), :] - fresh
-        )
-        shift = shifts_ref[0]
-        application(
-            LEVEL, find, (0, GROUP), vecs, lambda fresh, row: fresh - shift * vecs[pl.ds(LEVEL + row, 8), :]
-        )
+        find = finder(turned, outer, inner, far_inner, far_outer, None)
+        for ref, place in ((inner, 0), (far_inner, -16 if turned else 16)):
+            spread(vecs, row_of(place), ref[pl.ds(GROUP * ROWS, 8), :])
+            spread(vecs, given + row_of(place), ref[pl.ds(GROUP * ROWS + 8, 8), :])
+        levels(plan, turned, find, vecs, shifts_ref)
 
     by_core(run)
-    basis_ref[pl.ds(0, 8), :] = packed_rows(vecs, 1)
-    last = packed_rows(vecs, 2)
-    basis_ref[pl.ds(8, 8), :] = last
-    last_ref[...] = last
+    opening_ref[...] = packed_rows(vecs, 1)
 
 
 def late_kernel(
-    size, vec_inner, vec_outer, rim, body, inner, far_rim, far_inner, far_body,
-    early_ref, shifts_ref, basis_ref, gram_ref, vecs,
+    plan, size, far_x, outer, inner, far_inner, far_outer, far_opening, far_most, early_ref, shifts_ref,
+    basis_ref, gram_ref, vecs,
 ):
-    known = early_ref.shape[0] // 8
+    for at in range(0, vecs.shape[0], 8):
+        vecs[pl.ds(at, 8), :] = early_ref[pl.ds(at, 8), :]
+    given = vecs.shape[0] - LEVEL
 
     def run(turned):
-        find = finder(turned, rim, body, inner, far_rim, far_body, far_inner)
-        vectors = [vec_outer[...], early_ref[pl.ds(8 * known - 8, 8), :], vec_inner[...]]
-        for part, vector in enumerate(vectors[::-1] if turned else vectors):
-            spread(vecs, PAD + part * 2 * GROUP, vector)
-
-        def turn(index, carry, places):
-            at = pl.multiple_of((index - known) * LEVEL, 8)
-            shift = shifts_ref[index - 1]
-            application(
-                at, find, places, vecs, lambda fresh, row: fresh - shift * vecs[pl.ds(at + row, 8), :]
-            )
-            return carry
-
-        wide = [GROUP * k - RIM - BODY for k in range(5)]
-        narrow = wide[1:4]
-        split = next(k for k in range(known, size) if REACH * (size - 1 - k) <= -narrow[0])
-        lax.fori_loop(known, split, functools.partial(turn, places=wide), 0)
-        lax.fori_loop(split, size, functools.partial(turn, places=narrow), 0)
+        find = finder(turned, outer, inner, far_inner, far_outer, far_most)
+        place = 16 if turned else -16
+        spread(vecs, row_of(place), far_most[pl.ds(MOST * ROWS, 8), :])
+        spread(vecs, given + row_of(place), far_most[pl.ds(MOST * ROWS + 8, 8), :])
+        if turned:
+            two_rows(vecs, row_of(-18), far_x[pl.ds(7, 1), :])
+            two_rows(vecs, LEVEL + row_of(30), far_opening[pl.ds(7, 1), :])
+        else:
+            two_rows(vecs, row_of(32), far_x[pl.ds(0, 1), :])
+            two_rows(vecs, LEVEL + row_of(-16), far_opening[pl.ds(0, 1), :])
+        levels(plan, turned, find, vecs, shifts_ref)
 
     by_core(run)
-    rows = [early_ref[pl.ds(8 * k, 8), :] for k in range(known)]
-    rows += [packed_rows(vecs, k - known + 1) for k in range(known, size)]
+    rows = [packed_rows(vecs, k + 1) for k in range(size)]
     for k in range(size):
         basis_ref[pl.ds(8 * k, 8), :] = rows[k]
     lane = lane_ids(8)
@@ -284,6 +296,23 @@
             number += 1
     gram = jnp.sum(total, axis=0, keepdims=True)
     gram_ref[...] = jnp.broadcast_to(gram, gram_ref.shape)
+
+
+def plans(size):
+    early, late = [], []
+    for k in range(size):
+        low, high = REACH * (k + 1), 30 - REACH * k
+        first = [p for p in (2, 10, 18, 24) if p + 8 > low and p < high and low < high]
+        if 24 in first and 26 >= high:
+            first.remove(24)
+        last = [p for p in (-14, -6, 2, 10) if p < low and p + 8 > max(-14, low - 18)]
+        last += [p for p in (16, 24) if p <= high < p + 8]
+        for plan, places in ((early, first), (late, last)):
+            if plan and plan[-1][2] == places:
+                plan[-1] = (plan[-1][0], k + 1, places)
+            elif places:
+                plan.append((k, k + 1, places))
+    return early, late
 
 
 def partial_kernel(parts_ref, out_ref):
@@ -373,10 +402,12 @@
     x = start.reshape(packed, LANES)
     b = rhs.reshape(packed, LANES)
     sources = (operator, adjacency.T, counts, x, b)
-    made = (RIM * ROWS + 2 * packed, BODY * ROWS, INNER * ROWS + 2 * packed)
-    rim, middle, inner = pl.pallas_call(
+    early, late = plans(size)
+    rows = (size + 2) * LEVEL
+    made = (MOST * ROWS + 2 * packed, GROUP * ROWS, GROUP * ROWS + 2 * packed)
+    most, outer, inner = pl.pallas_call(
         band_kernel,
-        out_shape=tuple(pltpu.VMEM((rows, LANES), f32) for rows in made),
+        out_shape=tuple(pltpu.VMEM((count, LANES), f32) for count in made),
         in_specs=[hbm] * 5,
         out_specs=(vmem, vmem, vmem),
         scratch_shapes=[
@@ -389,37 +420,31 @@
         compiler_params=pltpu.CompilerParams(vmem_limit_bytes=16 * mebi),
         name="bands",
     )(*(pltpu.with_memory_space_constraint(source, pltpu.HBM) for source in sources))
-    far_rim = between_chips(rim)
-    far_body = between_chips(middle)
-    far_inner = within_chip(inner)
-    first, last = pl.pallas_call(
-        early_kernel,
+    far_most = between_chips(most)
+    chip = (outer, inner, within_chip(inner), within_chip(outer))
+    held, opening = pl.pallas_call(
+        functools.partial(early_kernel, early),
         out_shape=(
-            jax.ShapeDtypeStruct((16, LANES), f32),
+            jax.ShapeDtypeStruct((rows, LANES), f32),
             jax.ShapeDtypeStruct((packed, LANES), f32),
         ),
-        in_specs=[vmem] * 5 + [smem],
+        in_specs=[vmem] * 4 + [smem],
         out_specs=(vmem, vmem),
-        scratch_shapes=[pltpu.VMEM((4 * LEVEL, LANES), f32)],
         compiler_params=pltpu.CompilerParams(vmem_limit_bytes=16 * mebi),
-        cost_estimate=pl.CostEstimate(flops=20 * 10**9, bytes_accessed=0, transcendentals=0),
         name="early",
-    )(rim, middle, inner, far_rim, far_inner, shifts)
+    )(*chip, shifts)
     basis, gram = pl.pallas_call(
-        functools.partial(late_kernel, size),
+        functools.partial(late_kernel, late, size),
         out_shape=(
             jax.ShapeDtypeStruct((8 * size, LANES), f32),
             jax.ShapeDtypeStruct((slabs, LANES), f32),
         ),
-        in_specs=[vmem] * 9 + [smem],
+        in_specs=[vmem] * 8 + [smem],
         out_specs=(vmem, vmem),
-        scratch_shapes=[pltpu.VMEM(((size - 1) * LEVEL, LANES), f32)],
+        scratch_shapes=[pltpu.VMEM((rows, LANES), f32)],
         compiler_params=pltpu.CompilerParams(vmem_limit_bytes=16 * mebi),
         name="late",
-    )(
-        within_chip(last), between_chips(last), rim, middle, inner, far_rim, far_inner, far_body,
-        first, shifts,
-    )
+    )(across(x), *chip, between_chips(opening), far_most, held, shifts)
     parts = lax.all_to_all(gram, "slab", 0, 0, tiled=True)
     parts = pl.pallas_call(
         partial_kernel,

time: 73.1 us -> 75.4 us (1.031)
  blocking collectives: 40.8 us -> 45.6 us
  waiting for transfers between devices: 5.07 us -> 2.03 us
  Pallas kernels: 8.03 us -> 10.1 us
  starting transfers between devices: 18.2 us -> 16.7 us
    all_to_all x1, blocking collectives: 13.7 us -> 18.5 us  [body(): parts = lax.all_to_all(gram, 'slab', 0, 0, tiled=True)]
    ppermute x3 -> x2, waiting for transfers between devices: 5.07 us -> 1.27 us  [between_chips(): return lax.ppermute(array, AXES, pairs)]
    ppermute x2, starting transfers between devices: 10.7 us -> 6.93 us  [within_chip(): lax.ppermute(array, AXES, [(i, i + 1 - 2 * (i % 2)) for i in range(size)])]
    pallas_call x3, Pallas kernels: 6.54 us -> 8.57 us  [the longest x1 3.94 us: body(): pl.pallas_call(functools.partial(late_kernel, late, size), out_shape=(jax...]
    ppermute x0 -> x1, starting transfers between devices: none -> 1.29 us  [across(): lax.ppermute(array, AXES, [(i, j) for i, j in pairs if 0 <= j < size])]
    ppermute x3 -> x2, starting transfers between devices: 7.48 us -> 8.43 us  [between_chips(): return lax.ppermute(array, AXES, pairs)]
  transfers between devices with their start and end apart: 5 -> 5, of which waited for: 2 -> 2; matrix products, arithmetic and copies ran while one was open for 0% -> 0% of each run, Pallas kernels for 2% -> 3%
where the time goes in v9:
time: 75.4 us; the launch traced here: 75.1 us
  blocking collectives  45.6 us (60%)
  starting transfers between devices  16.7 us (22%)
  Pallas kernels  10.1 us (13%)
  waiting for transfers between devices  2.03 us (3%)
    all_to_all x1, blocking collectives, body(): parts = lax.all_to_all(parts, 'group', 0, 0, tiled=True)  27.1 us
    all_to_all x1, blocking collectives, body(): parts = lax.all_to_all(gram, 'slab', 0, 0, tiled=True)  18.5 us
    ppermute x2, starting transfers between devices, between_chips(): return lax.ppermute(array, AXES, pairs)  8.43 us
    ppermute x2, starting transfers between devices, within_chip(): lax.ppermute(array, AXES, [(i, i + 1 - 2 * (i % 2)) for i in range(size)])  6.93 us
    pallas_call x1, Pallas kernels, body(): pl.pallas_call(functools.partial(late_kernel, late, size), out_shape=(jax...  3.94 us
    pallas_call x1, Pallas kernels, body(): pl.pallas_call(functools.partial(early_kernel, early), out_shape=(jax.Sha...  2.58 us
    pallas_call x1, Pallas kernels, body(): pl.pallas_call(band_kernel, out_shape=tuple((pltpu.VMEM((count, LANES), f...  2.05 us
  transfers between devices with their start and end apart: 5, of which 2 were waited for; matrix products, arithmetic and copies ran while one was open for 0% of the time, Pallas kernels for 3%

profile of v9, /device:TPU:1, one launch (start us, length us, event | category | flops | bytes accessed | tf_op | source)
XLA Modules:
  0.0 75.1 jit_solution(6128527885195425235)
XLA Ops:
  0.6 0.0 copy-start
  0.6 0.0 copy-start.1
  0.7 2.1 %bands.1 = (f32[2256,128]{1,0:T(8,128)S(1)}, f32[1280,128]{1,0:T(8,128)S(1)}, f32[1296,128]{1,0:T(8,128)S(1)}) custom-call(f32[16,64,448]{2,1,0:T(8,128)} %op_ref.1, s32[6,16]{1,0:T(8,128)} %bitcast.20, s32[16]{0:T(128)} %valid_ref.1, f32[8,128]{1,0:T(8,128)} %bitcast.16, f32[8,128]{1,0:T(8,128)} %bitcast.21), custom_call_target="tpu_custom_call" | custom-call | tf_op jit(solution)/shard_map/bands/pallas_call | solution.py:408
  2.7 4.5 %collective-permute-start.4 = (f32[2256,128]{1,0:T(8,128)S(1)}, f32[2256,128]{1,0:T(8,128)S(1)}, u32[]{:S(2)}, u32[]{:S(2)}) collective-permute-start(f32[2256,128]{1,0:T(8,128)S(1)} %get-tuple-element.16), channel_id=1, source_target_pairs={{1,2},{2,1},{3,4},{4,3},{5,6},{6,5},{7,8},{8,7},{9,10},{10,9},{11,... | collective-permute-start | bytes 3465224 | tf_op jit(solution)/shard_map/ppermute | solution.py:27
  7.2 5.0 %collective-permute-start.1 = (f32[1296,128]{1,0:T(8,128)S(1)}, f32[1296,128]{1,0:T(8,128)S(1)}, u32[]{:S(2)}, u32[]{:S(2)}) collective-permute-start(f32[1296,128]{1,0:T(8,128)S(1)} %get-tuple-element.14.inner), channel_id=1, source_target_pairs={{0,1},{1,0},{2,3},{3,2},{4,5},{5,4},{6,7},{7,6},{8,9},{9,8},{10,11... | collective-permute-start | bytes 1990664 | tf_op jit(solution)/shard_map/ppermute | solution.py:32
  12.2 1.9 %collective-permute-start.2 = (f32[1280,128]{1,0:T(8,128)S(1)}, f32[1280,128]{1,0:T(8,128)S(1)}, u32[]{:S(2)}, u32[]{:S(2)}) collective-permute-start(f32[1280,128]{1,0:T(8,128)S(1)} %get-tuple-element.13.outer), channel_id=1, source_target_pairs={{0,1},{1,0},{2,3},{3,2},{4,5},{5,4},{6,7},{7,6},{8,9},{9,8},{10,11... | collective-permute-start | bytes 1966088 | tf_op jit(solution)/shard_map/ppermute | solution.py:32
  14.2 0.0 copy-done
  14.2 1.3 %collective-permute-start = (f32[8,128]{1,0:T(8,128)S(1)}, f32[8,128]{1,0:T(8,128)S(1)}, u32[]{:S(2)}, u32[]{:S(2)}) collective-permute-start(f32[8,128]{1,0:T(8,128)S(1)} %bitcast.17), channel_id=1, source_target_pairs={{1,3},{2,0},{3,5},{4,2},{5,7},{6,4},{7,9},{8,6},{9,11},{10,8},{11,... | collective-permute-start | bytes 12296 | tf_op jit(solution)/shard_map/ppermute | solution.py:38
  15.5 0.8 %collective-permute-done.2.far_outer = f32[1280,128]{1,0:T(8,128)S(1)} collective-permute-done((f32[1280,128]{1,0:T(8,128)S(1)}, f32[1280,128]{1,0:T(8,128)S(1)}, u32[]{:S(2)}, u32[]{:S(2)}) %collective-permute-start.2) | collective-permute-done | bytes 655392 | tf_op jit(solution)/shard_map/ppermute | solution.py:32
  16.2 0.0 collective-permute-done.1.far_inner
  16.2 0.0 copy-done.1
  16.2 2.6 %early.1 = (f32[616,128]{1,0:T(8,128)S(1)}, f32[8,128]{1,0:T(8,128)S(1)}) custom-call(f32[1280,128]{1,0:T(8,128)S(1)} %get-tuple-element.13.outer, f32[1296,128]{1,0:T(8,128)S(1)} %get-tuple-element.14.inner, f32[1296,128]{1,0:T(8,128)S(1)} %collective-permute-done.1.far_inner, f32[1280,128]{1,0:T(8,128)S(1)} %collective-permute-done.2.far_outer, f32[8]{0:T(128)S(1)} %copy-done.1), custom_call_target="tpu_custom_call" | custom-call | tf_op jit(solution)/shard_map/early/pallas_call | solution.py:425
  18.8 3.9 %collective-permute-start.3 = (f32[8,128]{1,0:T(8,128)S(1)}, f32[8,128]{1,0:T(8,128)S(1)}, u32[]{:S(2)}, u32[]{:S(2)}) collective-permute-start(f32[8,128]{1,0:T(8,128)S(1)} %get-tuple-element.15), channel_id=1, source_target_pairs={{1,2},{2,1},{3,4},{4,3},{5,6},{6,5},{7,8},{8,7},{9,10},{10,9},{11,... | collective-permute-start | bytes 12296 | tf_op jit(solution)/shard_map/ppermute | solution.py:27
  22.8 0.0 collective-permute-done.far_x
  22.8 1.3 %collective-permute-done.3.far_opening = f32[8,128]{1,0:T(8,128)S(1)} collective-permute-done((f32[8,128]{1,0:T(8,128)S(1)}, f32[8,128]{1,0:T(8,128)S(1)}, u32[]{:S(2)}, u32[]{:S(2)}) %collective-permute-start.3) | collective-permute-done | bytes 4128 | tf_op jit(solution)/shard_map/ppermute | solution.py:27
  24.0 0.0 collective-permute-done.4.far_most
  24.0 3.9 %late.1 = (f32[72,128]{1,0:T(8,128)S(1)}, f32[32,128]{1,0:T(8,128)S(1)}) custom-call(f32[8,128]{1,0:T(8,128)S(1)} %collective-permute-done.far_x, f32[1280,128]{1,0:T(8,128)S(1)} %get-tuple-element.13.outer, f32[1296,128]{1,0:T(8,128)S(1)} %get-tuple-element.14.inner, f32[1296,128]{1,0:T(8,128)S(1)} %collective-permute-done.1.far_inner, ...), custom_call_target="tpu_custom_call" | custom-call | tf_op jit(solution)/shard_map/late/pallas_call | solution.py:436
  28.0 18.5 %all_to_all.22 = f32[32,1,128]{2,1,0:T(1,128)S(1)} all-to-all(f32[32,1,128]{2,1,0:T(1,128)S(1)} %bitcast.19), channel_id=1, replica_groups=mesh['group'=16,'slab'=32] {'slab'}, dimensions={0} | all-to-all | bytes 32768 | tf_op jit(solution)/shard_map/all_to_all | solution.py:448
  46.5 27.1 %all_to_all.23 = f32[16,1,128]{2,1,0:T(1,128)S(1)} all-to-all(f32[16,1,128]{2,1,0:T(1,128)S(1)} %bitcast.15), channel_id=1, replica_groups=mesh['group'=16,'slab'=32] {'group'}, dimensions={0} | all-to-all | bytes 16384 | tf_op jit(solution)/shard_map/all_to_all | solution.py:457
  73.6 1.5 %finish.1 = (f32[8,128]{1,0:T(8,128)}, f32[8,128]{1,0:T(8,128)}, f32[9,9]{1,0:T(8,128)}) custom-call(f32[16,128]{1,0:T(8,128)S(1)} %bitcast.14, f32[72,128]{1,0:T(8,128)S(1)} %get-tuple-element.19.basis_ref, f32[8,128]{1,0:T(8,128)S(1)} %bitcast.18, f32[8]{0:T(128)S(1)} %copy-done.1), custom_call_target="tpu_custom_call" | custom-call | tf_op jit(solution)/shard_map/finish/pallas_call | solution.py:458
  (1 shorter events, 0.0 us)
Async XLA Ops:
  0.6 13.5 %copy-start = (f32[1024]{0:T(1024)S(1)}, f32[1024]{0:T(1024)}, u32[]{:S(2)}) copy-start(f32[1024]{0:T(1024)} %param.10) | copy-start | bytes 12292
  0.6 15.6 %copy-start.1 = (f32[8]{0:T(128)S(1)}, f32[8]{0:T(128)}, u32[]{:S(2)}) copy-start(f32[8]{0:T(128)} %shifts_ref.5) | copy-start | bytes 100
  2.7 21.3 %collective-permute-start.4 = (f32[2256,128]{1,0:T(8,128)S(1)}, f32[2256,128]{1,0:T(8,128)S(1)}, u32[]{:S(2)}, u32[]{:S(2)}) collective-permute-start(f32[2256,128]{1,0:T(8,128)S(1)} %get-tuple-element.16), channel_id=1, source_target_pairs={{1,2},{2,1},{3,4},{4,3},{5,6},{6,5},{7,8},{8,7},{9,10},{10,9},{11,... | collective-permute-start | bytes 3465224 | tf_op jit(solution)/shard_map/ppermute | solution.py:27
  7.2 9.0 %collective-permute-start.1 = (f32[1296,128]{1,0:T(8,128)S(1)}, f32[1296,128]{1,0:T(8,128)S(1)}, u32[]{:S(2)}, u32[]{:S(2)}) collective-permute-start(f32[1296,128]{1,0:T(8,128)S(1)} %get-tuple-element.14.inner), channel_id=1, source_target_pairs={{0,1},{1,0},{2,3},{3,2},{4,5},{5,4},{6,7},{7,6},{8,9},{9,8},{10,11... | collective-permute-start | bytes 1990664 | tf_op jit(solution)/shard_map/ppermute | solution.py:32
  12.2 4.0 %collective-permute-start.2 = (f32[1280,128]{1,0:T(8,128)S(1)}, f32[1280,128]{1,0:T(8,128)S(1)}, u32[]{:S(2)}, u32[]{:S(2)}) collective-permute-start(f32[1280,128]{1,0:T(8,128)S(1)} %get-tuple-element.13.outer), channel_id=1, source_target_pairs={{0,1},{1,0},{2,3},{3,2},{4,5},{5,4},{6,7},{7,6},{8,9},{9,8},{10,11... | collective-permute-start | bytes 1966088 | tf_op jit(solution)/shard_map/ppermute | solution.py:32
  14.2 8.6 %collective-permute-start = (f32[8,128]{1,0:T(8,128)S(1)}, f32[8,128]{1,0:T(8,128)S(1)}, u32[]{:S(2)}, u32[]{:S(2)}) collective-permute-start(f32[8,128]{1,0:T(8,128)S(1)} %bitcast.17), channel_id=1, source_target_pairs={{1,3},{2,0},{3,5},{4,2},{5,7},{6,4},{7,9},{8,6},{9,11},{10,8},{11,... | collective-permute-start | bytes 12296 | tf_op jit(solution)/shard_map/ppermute | solution.py:38
  18.8 5.2 %collective-permute-start.3 = (f32[8,128]{1,0:T(8,128)S(1)}, f32[8,128]{1,0:T(8,128)S(1)}, u32[]{:S(2)}, u32[]{:S(2)}) collective-permute-start(f32[8,128]{1,0:T(8,128)S(1)} %get-tuple-element.15), channel_id=1, source_target_pairs={{1,2},{2,1},{3,4},{4,3},{5,6},{6,5},{7,8},{8,7},{9,10},{10,9},{11,... | collective-permute-start | bytes 12296 | tf_op jit(solution)/shard_map/ppermute | solution.py:27

commit v10 on v9

--- a/solution.py
+++ b/solution.py
@@ -244,25 +244,38 @@
     vecs[pl.ds(row + 1, 1), :] = jnp.where(left, turned, packed)[:1]
 
 
-def early_kernel(plan, outer, inner, far_inner, far_outer, shifts_ref, vecs, opening_ref):
+def start_levels(vecs, turned, inner, far_inner):
     empty = jnp.zeros((8, LANES), jnp.float32)
     for at in range(0, vecs.shape[0], 8):
         vecs[pl.ds(at, 8), :] = empty
     given = vecs.shape[0] - LEVEL
-
+    for ref, place in ((inner, 0), (far_inner, -16 if turned else 16)):
+        spread(vecs, row_of(place), ref[pl.ds(GROUP * ROWS, 8), :])
+        spread(vecs, given + row_of(place), ref[pl.ds(GROUP * ROWS + 8, 8), :])
+
+
+def opening_kernel(inner, far_inner, shifts_ref, opening_ref, start_ref, vecs):
     def run(turned):
-        find = finder(turned, outer, inner, far_inner, far_outer, None)
-        for ref, place in ((inner, 0), (far_inner, -16 if turned else 16)):
-            spread(vecs, row_of(place), ref[pl.ds(GROUP * ROWS, 8), :])
-            spread(vecs, given + row_of(place), ref[pl.ds(GROUP * ROWS + 8, 8), :])
-        levels(plan, turned, find, vecs, shifts_ref)
+        start_levels(vecs, turned, inner, far_inner)
+        find = finder(turned, None, inner, far_inner, None, None)
+        levels([(0, 1, [10])], turned, find, vecs, shifts_ref)
 
     by_core(run)
     opening_ref[...] = packed_rows(vecs, 1)
+    start_ref[...] = inner[pl.ds(GROUP * ROWS, 8), :]
+
+
+def early_kernel(plan, outer, inner, far_inner, far_outer, shifts_ref, vecs):
+    def run(turned):
+        start_levels(vecs, turned, inner, far_inner)
+        find = finder(turned, outer, inner, far_inner, far_outer, None)
+        levels(plan, turned, find, vecs, shifts_ref)
+
+    by_core(run)
 
 
 def late_kernel(
-    plan, size, far_x, outer, inner, far_inner, far_outer, far_opening, far_most, early_ref, shifts_ref,
+    plan, size, far_opening, outer, inner, far_inner, far_outer, far_x, far_most, early_ref, shifts_ref,
     basis_ref, gram_ref, vecs,
 ):
     for at in range(0, vecs.shape[0], 8):
@@ -422,14 +435,20 @@
     )(*(pltpu.with_memory_space_constraint(source, pltpu.HBM) for source in sources))
     far_most = between_chips(most)
     chip = (outer, inner, within_chip(inner), within_chip(outer))
-    held, opening = pl.pallas_call(
+    opening, sent = pl.pallas_call(
+        opening_kernel,
+        out_shape=(jax.ShapeDtypeStruct((packed, LANES), f32),) * 2,
+        in_specs=[vmem] * 2 + [smem],
+        out_specs=(vmem, vmem),
+        scratch_shapes=[pltpu.VMEM((3 * LEVEL, LANES), f32)],
+        compiler_params=pltpu.CompilerParams(vmem_limit_bytes=16 * mebi),
+        name="opening",
+    )(chip[1], chip[2], shifts)
+    held = pl.pallas_call(
         functools.partial(early_kernel, early),
-        out_shape=(
-            jax.ShapeDtypeStruct((rows, LANES), f32),
-            jax.ShapeDtypeStruct((packed, LANES), f32),
-        ),
+        out_shape=jax.ShapeDtypeStruct((rows, LANES), f32),
         in_specs=[vmem] * 4 + [smem],
-        out_specs=(vmem, vmem),
+        out_specs=vmem,
         compiler_params=pltpu.CompilerParams(vmem_limit_bytes=16 * mebi),
         name="early",
     )(*chip, shifts)
@@ -444,7 +463,7 @@
         scratch_shapes=[pltpu.VMEM((rows, LANES), f32)],
         compiler_params=pltpu.CompilerParams(vmem_limit_bytes=16 * mebi),
         name="late",
-    )(across(x), *chip, between_chips(opening), far_most, held, shifts)
+    )(between_chips(opening), *chip, across(sent), far_most, held, shifts)
     parts = lax.all_to_all(gram, "slab", 0, 0, tiled=True)
     parts = pl.pallas_call(
         partial_kernel,

time: 75.4 us -> 70.9 us (0.940)
  waiting for transfers between devices: 2.03 us -> 0.02 us
  starting transfers between devices: 16.7 us -> 14.7 us
  blocking collectives: 45.6 us -> 44.3 us
  Pallas kernels: 10.1 us -> 10.9 us
    ppermute x2, starting transfers between devices: 8.43 us -> 6.43 us  [between_chips(): return lax.ppermute(array, AXES, pairs)]
    ppermute x2, waiting for transfers between devices: 1.27 us -> 0.01 us  [between_chips(): return lax.ppermute(array, AXES, pairs)]
    all_to_all x1, blocking collectives: 27.1 us -> 26 us  [body(): parts = lax.all_to_all(parts, 'group', 0, 0, tiled=True)]
    pallas_call x1 -> x2, Pallas kernels: 2.58 us -> 3.4 us  [the longest x1 2.59 us: body(): pl.pallas_call(functools.partial(early_kernel, early), out_shape=jax.Shap...]
  transfers between devices with their start and end apart: 5 -> 5, of which waited for: 2 -> 0; matrix products, arithmetic and copies ran while one was open for 0% -> 0% of each run, Pallas kernels for 3% -> 5%
where the time goes in v10:
time: 70.9 us; the launch traced here: 70.6 us
  blocking collectives  44.3 us (62%)
  starting transfers between devices  14.7 us (21%)
  Pallas kernels  10.9 us (15%)
  between operations  0.76 us (1%)
    all_to_all x1, blocking collectives, body(): parts = lax.all_to_all(parts, 'group', 0, 0, tiled=True)  26 us
    all_to_all x1, blocking collectives, body(): parts = lax.all_to_all(gram, 'slab', 0, 0, tiled=True)  18.3 us
    ppermute x2, starting transfers between devices, within_chip(): lax.ppermute(array, AXES, [(i, i + 1 - 2 * (i % 2)) for i in range(size)])  6.93 us
    ppermute x2, starting transfers between devices, between_chips(): return lax.ppermute(array, AXES, pairs)  6.43 us
    pallas_call x1, Pallas kernels, body(): pl.pallas_call(functools.partial(late_kernel, late, size), out_shape=(jax...  3.93 us
    pallas_call x1, Pallas kernels, body(): pl.pallas_call(functools.partial(early_kernel, early), out_shape=jax.Shap...  2.59 us
    pallas_call x1, Pallas kernels, body(): pl.pallas_call(band_kernel, out_shape=tuple((pltpu.VMEM((count, LANES), f...  2.05 us
    pallas_call x1, Pallas kernels, body(): pl.pallas_call(functools.partial(finish_kernel, devices * elems * width,...  1.48 us
  transfers between devices with their start and end apart: 5, of which 0 were waited for; matrix products, arithmetic and copies ran while one was open for 0% of the time, Pallas kernels for 5%

profile of v10, /device:TPU:1, one launch (start us, length us, event | category | flops | bytes accessed | tf_op | source)
XLA Modules:
  0.0 70.6 jit_solution(8713645465544376273)
XLA Ops:
  0.6 0.0 copy-start.1
  0.6 2.0 %bands.1 = (f32[2256,128]{1,0:T(8,128)S(1)}, f32[1280,128]{1,0:T(8,128)S(1)}, f32[1296,128]{1,0:T(8,128)S(1)}) custom-call(f32[16,64,448]{2,1,0:T(8,128)} %op_ref.1, s32[6,16]{1,0:T(8,128)} %bitcast.19, s32[16]{0:T(128)} %valid_ref.1, f32[8,128]{1,0:T(8,128)} %bitcast.16, f32[8,128]{1,0:T(8,128)} %bitcast.20), custom_call_target="tpu_custom_call" | custom-call | tf_op jit(solution)/shard_map/bands/pallas_call | solution.py:421
  2.7 4.5 %collective-permute-start.4 = (f32[2256,128]{1,0:T(8,128)S(1)}, f32[2256,128]{1,0:T(8,128)S(1)}, u32[]{:S(2)}, u32[]{:S(2)}) collective-permute-start(f32[2256,128]{1,0:T(8,128)S(1)} %get-tuple-element.17), channel_id=1, source_target_pairs={{1,2},{2,1},{3,4},{4,3},{5,6},{6,5},{7,8},{8,7},{9,10},{10,9},{11,... | collective-permute-start | bytes 3465224 | tf_op jit(solution)/shard_map/ppermute | solution.py:27
  7.2 5.0 %collective-permute-start = (f32[1296,128]{1,0:T(8,128)S(1)}, f32[1296,128]{1,0:T(8,128)S(1)}, u32[]{:S(2)}, u32[]{:S(2)}) collective-permute-start(f32[1296,128]{1,0:T(8,128)S(1)} %get-tuple-element.13.inner), channel_id=1, source_target_pairs={{0,1},{1,0},{2,3},{3,2},{4,5},{5,4},{6,7},{7,6},{8,9},{9,8},{10,11... | collective-permute-start | bytes 1990664 | tf_op jit(solution)/shard_map/ppermute | solution.py:32
  12.2 1.9 %collective-permute-start.2 = (f32[1280,128]{1,0:T(8,128)S(1)}, f32[1280,128]{1,0:T(8,128)S(1)}, u32[]{:S(2)}, u32[]{:S(2)}) collective-permute-start(f32[1280,128]{1,0:T(8,128)S(1)} %get-tuple-element.15.outer), channel_id=1, source_target_pairs={{0,1},{1,0},{2,3},{3,2},{4,5},{5,4},{6,7},{7,6},{8,9},{9,8},{10,11... | collective-permute-start | bytes 1966088 | tf_op jit(solution)/shard_map/ppermute | solution.py:32
  14.2 0.0 collective-permute-done.far_inner
  14.2 0.0 copy-done.1
  14.2 0.8 %opening.1 = (f32[8,128]{1,0:T(8,128)S(1)}, f32[8,128]{1,0:T(8,128)S(1)}) custom-call(f32[1296,128]{1,0:T(8,128)S(1)} %get-tuple-element.13.inner, f32[1296,128]{1,0:T(8,128)S(1)} %collective-permute-done.far_inner, f32[8]{0:T(128)S(1)} %copy-done.1), custom_call_target="tpu_custom_call" | custom-call | tf_op jit(solution)/shard_map/opening/pallas_call | solution.py:438
  15.0 1.9 %collective-permute-start.1 = (f32[8,128]{1,0:T(8,128)S(1)}, f32[8,128]{1,0:T(8,128)S(1)}, u32[]{:S(2)}, u32[]{:S(2)}) collective-permute-start(f32[8,128]{1,0:T(8,128)S(1)} %get-tuple-element.14), channel_id=1, source_target_pairs={{1,2},{2,1},{3,4},{4,3},{5,6},{6,5},{7,8},{8,7},{9,10},{10,9},{11,... | collective-permute-start | bytes 12296 | tf_op jit(solution)/shard_map/ppermute | solution.py:27
  16.9 1.3 %collective-permute-start.3 = (f32[8,128]{1,0:T(8,128)S(1)}, f32[8,128]{1,0:T(8,128)S(1)}, u32[]{:S(2)}, u32[]{:S(2)}) collective-permute-start(f32[8,128]{1,0:T(8,128)S(1)} %get-tuple-element.16), channel_id=1, source_target_pairs={{1,3},{2,0},{3,5},{4,2},{5,7},{6,4},{7,9},{8,6},{9,11},{10,8},{11,... | collective-permute-start | bytes 12296 | tf_op jit(solution)/shard_map/ppermute | solution.py:38
  18.2 0.0 collective-permute-done.2.far_outer
  18.2 2.6 %early.1.early_ref = f32[616,128]{1,0:T(8,128)S(1)} custom-call(f32[1280,128]{1,0:T(8,128)S(1)} %get-tuple-element.15.outer, f32[1296,128]{1,0:T(8,128)S(1)} %get-tuple-element.13.inner, f32[1296,128]{1,0:T(8,128)S(1)} %collective-permute-done.far_inner, f32[1280,128]{1,0:T(8,128)S(1)} %collective-permute-done.2.far_outer, f32[8]{0:T(128)S(1)} %copy-done.1), custom_call_target="tpu_custom_call" | custom-call | tf_op jit(solution)/shard_map/early/pallas_call | solution.py:447
  20.8 0.0 copy-start
  20.9 0.0 collective-permute-done.1.far_opening
  20.9 0.0 collective-permute-done.3.far_x
  20.9 0.0 collective-permute-done.4.far_most
  20.9 3.9 %late.1 = (f32[72,128]{1,0:T(8,128)S(1)}, f32[32,128]{1,0:T(8,128)S(1)}) custom-call(f32[8,128]{1,0:T(8,128)S(1)} %collective-permute-done.1.far_opening, f32[1280,128]{1,0:T(8,128)S(1)} %get-tuple-element.15.outer, f32[1296,128]{1,0:T(8,128)S(1)} %get-tuple-element.13.inner, f32[1296,128]{1,0:T(8,128)S(1)} %collective-permute-done.far_inner, ...), custom_call_target="tpu_custom_call" | custom-call | tf_op jit(solution)/shard_map/late/pallas_call | solution.py:455
  24.8 18.3 %all_to_all.22 = f32[32,1,128]{2,1,0:T(1,128)S(1)} all-to-all(f32[32,1,128]{2,1,0:T(1,128)S(1)} %bitcast.18), channel_id=1, replica_groups=mesh['group'=16,'slab'=32] {'slab'}, dimensions={0} | all-to-all | bytes 32768 | tf_op jit(solution)/shard_map/all_to_all | solution.py:467
  43.1 26.0 %all_to_all.23 = f32[16,1,128]{2,1,0:T(1,128)S(1)} all-to-all(f32[16,1,128]{2,1,0:T(1,128)S(1)} %bitcast.15), channel_id=1, replica_groups=mesh['group'=16,'slab'=32] {'group'}, dimensions={0} | all-to-all | bytes 16384 | tf_op jit(solution)/shard_map/all_to_all | solution.py:476
  69.1 0.0 copy-done
  69.1 1.5 %finish.1 = (f32[8,128]{1,0:T(8,128)}, f32[8,128]{1,0:T(8,128)}, f32[9,9]{1,0:T(8,128)}) custom-call(f32[16,128]{1,0:T(8,128)S(1)} %bitcast.14, f32[72,128]{1,0:T(8,128)S(1)} %get-tuple-element.19.basis_ref, f32[8,128]{1,0:T(8,128)S(1)} %bitcast.17, f32[8]{0:T(128)S(1)} %copy-done.1), custom_call_target="tpu_custom_call" | custom-call | tf_op jit(solution)/shard_map/finish/pallas_call | solution.py:477
  (1 shorter events, 0.0 us)
Async XLA Ops:
  0.6 13.5 %copy-start.1 = (f32[8]{0:T(128)S(1)}, f32[8]{0:T(128)}, u32[]{:S(2)}) copy-start(f32[8]{0:T(128)} %shifts_ref.7) | copy-start | bytes 100
  2.7 18.2 %collective-permute-start.4 = (f32[2256,128]{1,0:T(8,128)S(1)}, f32[2256,128]{1,0:T(8,128)S(1)}, u32[]{:S(2)}, u32[]{:S(2)}) collective-permute-start(f32[2256,128]{1,0:T(8,128)S(1)} %get-tuple-element.17), channel_id=1, source_target_pairs={{1,2},{2,1},{3,4},{4,3},{5,6},{6,5},{7,8},{8,7},{9,10},{10,9},{11,... | collective-permute-start | bytes 3465224 | tf_op jit(solution)/shard_map/ppermute | solution.py:27
  7.2 7.0 %collective-permute-start = (f32[1296,128]{1,0:T(8,128)S(1)}, f32[1296,128]{1,0:T(8,128)S(1)}, u32[]{:S(2)}, u32[]{:S(2)}) collective-permute-start(f32[1296,128]{1,0:T(8,128)S(1)} %get-tuple-element.13.inner), channel_id=1, source_target_pairs={{0,1},{1,0},{2,3},{3,2},{4,5},{5,4},{6,7},{7,6},{8,9},{9,8},{10,11... | collective-permute-start | bytes 1990664 | tf_op jit(solution)/shard_map/ppermute | solution.py:32
  12.2 6.0 %collective-permute-start.2 = (f32[1280,128]{1,0:T(8,128)S(1)}, f32[1280,128]{1,0:T(8,128)S(1)}, u32[]{:S(2)}, u32[]{:S(2)}) collective-permute-start(f32[1280,128]{1,0:T(8,128)S(1)} %get-tuple-element.15.outer), channel_id=1, source_target_pairs={{0,1},{1,0},{2,3},{3,2},{4,5},{5,4},{6,7},{7,6},{8,9},{9,8},{10,11... | collective-permute-start | bytes 1966088 | tf_op jit(solution)/shard_map/ppermute | solution.py:32
  15.0 5.9 %collective-permute-start.1 = (f32[8,128]{1,0:T(8,128)S(1)}, f32[8,128]{1,0:T(8,128)S(1)}, u32[]{:S(2)}, u32[]{:S(2)}) collective-permute-start(f32[8,128]{1,0:T(8,128)S(1)} %get-tuple-element.14), channel_id=1, source_target_pairs={{1,2},{2,1},{3,4},{4,3},{5,6},{6,5},{7,8},{8,7},{9,10},{10,9},{11,... | collective-permute-start | bytes 12296 | tf_op jit(solution)/shard_map/ppermute | solution.py:27
  16.9 4.0 %collective-permute-start.3 = (f32[8,128]{1,0:T(8,128)S(1)}, f32[8,128]{1,0:T(8,128)S(1)}, u32[]{:S(2)}, u32[]{:S(2)}) collective-permute-start(f32[8,128]{1,0:T(8,128)S(1)} %get-tuple-element.16), channel_id=1, source_target_pairs={{1,3},{2,0},{3,5},{4,2},{5,7},{6,4},{7,9},{8,6},{9,11},{10,8},{11,... | collective-permute-start | bytes 12296 | tf_op jit(solution)/shard_map/ppermute | solution.py:38
  20.8 48.3 %copy-start = (f32[1024]{0:T(1024)S(1)}, f32[1024]{0:T(1024)}, u32[]{:S(2)}) copy-start(f32[1024]{0:T(1024)} %param.10) | copy-start | bytes 12292
